TPU v7x, 768 devices: a whole 4x8x12 slice. The times are simulated.
768 devices in a mesh: lon: 24 (over z_lo, x), lat: 16 (over y, core), section: 2 (over z_hi).
Axes of the slice: x: 4, y: 8, z: 12 (z_hi: 2, z_lo: 6; z = z_hi * 6 + z_lo), core: 2. Of those that a mesh axis runs over, the one named last changes fastest.
Arguments:
- inputs: bfloat16 [2, 4, 96, 288, 320], P('section', None, 'lat', 'lon'), may hold values from -6 to 6
- ln_gain: bfloat16 [2, 2, 320], P('section'), may hold values from 0.099609375 to 1.8984375
- ln_shift: bfloat16 [2, 2, 320], P('section'), may hold values from -3 to 3
- qkv_weight: bfloat16 [2, 320, 960], P('section')
- qkv_bias: bfloat16 [2, 960], P('section'), may hold values from -2 to 2
- proj_weight: bfloat16 [2, 320, 320], P('section'), may hold values from -0.3125 to 0.3125
- fc1_weight: bfloat16 [2, 320, 1280], P('section'), may hold values from -0.3125 to 0.3125
- fc1_bias: bfloat16 [2, 1280], P('section'), may hold values from -2 to 2
- fc2_weight: bfloat16 [2, 1280, 320], P('section'), may hold values from -0.15625 to 0.15625
- out_bias: bfloat16 [2, 2, 320], P('section'), may hold values from -2 to 2
- bias_table: bfloat16 [2, 2, 16, 10, 3312], P('section', None, 'lat'), may hold values from -5 to 5
Outputs:
- result: bfloat16 [2, 4, 96, 288, 320], P('section', None, 'lat', 'lon')
All inputs are finite; a program needn't handle non-finite values.
Results may differ from a plain program's by a relative error of at most 0.012.
The roundings to bfloat16 on the way count: a program that leaves them out, or rounds other values in their place, can miss the bound.
Values may be sent and summed in bfloat16 or wider, within the bound.
No kernel may reach another device: no remote copies, remote signals or barrier semaphores. Data moves between devices by JAX's collectives and lax.ppermute only.
A program may use at most 128 MiB of HBM per device.

v0:
```python
import jax
import jax.numpy as jnp
import numpy as np
from jax import lax
from jax.sharding import PartitionSpec as P

HD = 32
WLEV = 2
WLAT = 6
WLON = 12


def shifted(block, axis, distance):
    devices = range(lax.axis_size(axis))
    route = [((i - distance) % len(devices), i) for i in devices]
    return lax.ppermute(block, axis, route)


def partner(x, axis, apart):
    return lax.ppermute(x, axis, [(i, i ^ 1 << apart) for i in range(lax.axis_size(axis))])


def pair_index():
    lev_pos, lat_pos, lon_pos = np.meshgrid(
        np.arange(WLEV), np.arange(WLAT), np.arange(WLON), indexing="ij"
    )
    lev_pos = lev_pos.reshape(-1)
    lat_pos = lat_pos.reshape(-1)
    lon_pos = lon_pos.reshape(-1)
    pair_ids = (lev_pos[:, None] + lev_pos[None, :] * WLEV) * (WLAT * WLAT * (2 * WLON - 1))
    pair_ids = pair_ids + (lat_pos[:, None] + lat_pos[None, :] * WLAT) * (2 * WLON - 1)
    pair_ids = pair_ids + lon_pos[:, None] - lon_pos[None, :] + WLON - 1
    return pair_ids.reshape(-1).astype(np.int32)


def layer_norm(values, norm_gain, norm_shift):
    center = values - jnp.mean(values, axis=-1, keepdims=True)
    spread = jnp.mean(center * center, axis=-1, keepdims=True)
    return center * lax.rsqrt(spread + 1e-05) * norm_gain.astype(jnp.float32) + norm_shift.astype(
        jnp.float32
    )


def to_windows(field_grid):
    levels, lat_cells, lon_cells, channels = field_grid.shape
    field_grid = field_grid.reshape(
        levels // WLEV, WLEV, lat_cells // WLAT, WLAT, lon_cells // WLON, WLON, channels
    )
    field_grid = field_grid.transpose(0, 2, 4, 1, 3, 5, 6)
    return field_grid.reshape(
        levels // WLEV, lat_cells // WLAT, lon_cells // WLON, WLEV * WLAT * WLON, channels
    )


def from_windows(windows, levels, lat_cells, lon_cells):
    channels = windows.shape[-1]
    field_grid = windows.reshape(
        levels // WLEV, lat_cells // WLAT, lon_cells // WLON, WLEV, WLAT, WLON, channels
    )
    field_grid = field_grid.transpose(0, 3, 1, 4, 2, 5, 6)
    return field_grid.reshape(levels, lat_cells, lon_cells, channels)


def attend(windows, qkv_w, qkv_b, addend):
    channels = windows.shape[-1]
    head_count = channels // HD
    leading = windows.shape[:4]
    packed = jnp.einsum("abcnd,de->abcne", windows, qkv_w, preferred_element_type=jnp.float32)
    packed = (packed + qkv_b.astype(jnp.float32)).astype(jnp.bfloat16)
    queries = packed[..., :channels].reshape(leading + (head_count, HD))
    key_rows = packed[..., channels : 2 * channels].reshape(leading + (head_count, HD))
    values = packed[..., 2 * channels :].reshape(leading + (head_count, HD))
    scores = jnp.einsum(
        "abcnhd,abcmhd->abchnm", queries, key_rows, preferred_element_type=jnp.float32
    ) * HD ** (-0.5)
    scores = scores + addend[:, :, None]
    row_peak = jnp.max(scores, axis=-1, keepdims=True)
    raised = jnp.exp(scores - row_peak)
    weights_bf = (raised / jnp.sum(raised, axis=-1, keepdims=True)).astype(jnp.bfloat16)
    mixed = jnp.einsum(
        "abchnm,abcmhd->abcnhd", weights_bf, values, preferred_element_type=jnp.float32
    )
    return mixed.astype(jnp.bfloat16).reshape(leading + (channels,))


def dense_bias(table):
    win_count = WLEV * WLAT * WLON
    pair_ids = jnp.asarray(pair_index())
    dense = jnp.take(table, pair_ids, axis=3).astype(jnp.float32)
    return dense.reshape(table.shape[0], table.shape[1], table.shape[2], win_count, win_count)


def window_groups(levels, lat_cells, offsets):
    lev_off, lat_off, lon_off = offsets
    lat_total = lat_cells * lax.axis_size("lat")
    lat_start = lax.axis_index("lat") * lat_cells + lat_off
    lev_flag = (jnp.arange(levels, dtype=jnp.int32) + lev_off >= levels).astype(jnp.int32)
    lat_flag = (jnp.arange(lat_cells, dtype=jnp.int32) + lat_start >= lat_total).astype(jnp.int32)
    group_grid = jnp.broadcast_to(
        lev_flag[:, None, None] * 2 + lat_flag[None, :, None], (levels, lat_cells, WLON)
    )
    return to_windows(group_grid[..., None])[:, :, 0, :, 0]


def prepare(table, groups):
    dense = dense_bias(table)
    allowed = groups[:, :, None, :, None] == groups[:, :, None, None, :]
    return dense + jnp.where(allowed, 0.0, -1e30).astype(jnp.float32)


def finish_block(field_wide, owned, params):
    ln_g, ln_s, qkv_w, qkv_b, proj_w, fc1_w, fc1_b, fc2_w, out_b, table = params
    levels, lat_cells, lon_cells, channels = owned.shape
    flat_att = owned.reshape(-1, channels)
    mid = (
        field_wide.reshape(-1, channels)
        + jnp.dot(flat_att, proj_w, preferred_element_type=jnp.float32)
        + out_b[0].astype(jnp.float32)
    )
    normed_two = layer_norm(mid, ln_g[1], ln_s[1]).astype(jnp.bfloat16)
    hidden = jax.nn.gelu(
        jnp.dot(normed_two, fc1_w, preferred_element_type=jnp.float32) + fc1_b.astype(jnp.float32),
        approximate=False,
    ).astype(jnp.bfloat16)
    outcome = (
        mid
        + jnp.dot(hidden, fc2_w, preferred_element_type=jnp.float32)
        + out_b[1].astype(jnp.float32)
    )
    return outcome.astype(jnp.bfloat16).reshape(levels, lat_cells, lon_cells, channels)


def apply_block(field, params, offsets, addend):
    ln_g, ln_s, qkv_w, qkv_b, proj_w, fc1_w, fc1_b, fc2_w, out_b, table = params
    levels, lat_cells, lon_cells, channels = field.shape
    field_wide = field.astype(jnp.float32)
    normed = layer_norm(field_wide, ln_g[0], ln_s[0]).astype(jnp.bfloat16)
    lev_off, lat_off, lon_off = offsets
    lat_rim_rows = WLAT // 2
    lon_rim_cols = WLON // 2
    lat_rim = shifted(normed[:, :lat_rim_rows], "lat", -1)
    taller = jnp.concatenate([normed, lat_rim], axis=1)
    lon_rim = shifted(taller[:, :, :lon_rim_cols], "lon", -1)
    extended = jnp.concatenate([taller, lon_rim], axis=2)
    extended = jnp.concatenate([extended, extended[: WLEV // 2]], axis=0)
    anchor = jnp.int32(0)
    slab = lax.dynamic_slice(
        extended, (lev_off, lat_off, lon_off, anchor), (levels, lat_cells, lon_cells, channels)
    )
    mixed = attend(to_windows(slab), qkv_w, qkv_b, addend)
    attended = from_windows(mixed, levels, lat_cells, lon_cells)
    doubled = jnp.concatenate([attended[levels - WLEV // 2 :], attended], axis=0)
    attended = lax.dynamic_slice_in_dim(doubled, WLEV // 2 - lev_off, levels, 0)
    placed = jnp.zeros(
        (levels, lat_cells + lat_rim_rows, lon_cells + lon_rim_cols, channels), jnp.bfloat16
    )
    placed = lax.dynamic_update_slice(placed, attended, (anchor, lat_off, lon_off, anchor))
    lon_back = shifted(placed[:, :, lon_cells:], "lon", 1)
    middle = jnp.concatenate(
        [placed[:, :, :lon_rim_cols] + lon_back, placed[:, :, lon_rim_cols:lon_cells]], axis=2
    )
    lat_back = shifted(middle[:, lat_cells:], "lat", 1)
    owned = jnp.concatenate(
        [middle[:, :lat_rim_rows] + lat_back, middle[:, lat_rim_rows:lat_cells]], axis=1
    )
    return finish_block(field_wide, owned, params)


def body(
    inputs,
    ln_gain,
    ln_shift,
    qkv_weight,
    qkv_bias,
    proj_weight,
    fc1_weight,
    fc1_bias,
    fc2_weight,
    out_bias,
    bias_table,
):
    section_index = lax.axis_index("section")
    micro_count = inputs.shape[0]
    levels = inputs.shape[1]
    lat_cells = inputs.shape[2]
    stacked = (
        ln_gain,
        ln_shift,
        qkv_weight,
        qkv_bias,
        proj_weight,
        fc1_weight,
        fc1_bias,
        fc2_weight,
        out_bias,
        bias_table,
    )
    params = tuple((member[0] for member in stacked))
    offsets = (
        section_index * (WLEV // 2),
        section_index * (WLAT // 2),
        section_index * (WLON // 2),
    )
    addend = prepare(params[9], window_groups(levels, lat_cells, offsets))
    is_first = section_index == 0

    def advance(carry, step_index):
        current, results = carry
        pair_step = step_index // 2
        is_even = step_index % 2 == 0
        produced = apply_block(current, params, offsets, addend)
        keep_last = jnp.logical_and(
            jnp.logical_not(is_first), jnp.logical_and(is_even, pair_step >= 1)
        )
        stored = lax.dynamic_update_index_in_dim(
            results, produced, jnp.maximum(pair_step - 1, 0), 0
        )
        results = jnp.where(keep_last, stored, results)
        own_input = lax.dynamic_index_in_dim(inputs, pair_step, 0, keepdims=False)
        outgoing = jnp.where(
            jnp.logical_or(is_first, jnp.logical_not(is_even)), produced, own_input
        )
        incoming = partner(outgoing, "section", 0)
        keep_first = jnp.logical_and(is_first, jnp.logical_not(is_even))
        results = jnp.where(
            keep_first, lax.dynamic_update_index_in_dim(results, incoming, pair_step, 0), results
        )
        following = lax.dynamic_index_in_dim(
            inputs, jnp.minimum(pair_step + 1, micro_count - 1), 0, keepdims=False
        )
        current = jnp.where(keep_first, following, incoming)
        return ((current, results), None)

    initial = (inputs[0], jnp.zeros_like(inputs))
    (current, results), unused = lax.scan(
        advance, initial, jnp.arange(2 * micro_count, dtype=jnp.int32)
    )
    produced = apply_block(current, params, offsets, addend)
    finished = lax.dynamic_update_index_in_dim(results, produced, micro_count - 1, 0)
    return jnp.where(is_first, results, finished)


def solution(mesh):
    return jax.shard_map(
        body,
        mesh=mesh,
        in_specs=(
            P("section", None, "lat", "lon", None),
            P("section", None, None),
            P("section", None, None),
            P("section", None, None),
            P("section", None),
            P("section", None, None),
            P("section", None, None),
            P("section", None),
            P("section", None, None),
            P("section", None, None),
            P("section", None, "lat", None, None),
        ),
        out_specs=P("section", None, "lat", "lon", None),
        check_vma=False,
    )
```

profile of v0, /device:TPU:32, one launch (start us, length us, event | category | flops | bytes accessed | tf_op | source)
XLA Modules:
  0.0 374.9 jit_solution(18397783101509293065)
XLA Ops:
  1.3 3.7 copy.32
  5.0 51.2 %gather_fusion = bf16[20736,2,10]{2,1,0:T(2,128)(2,1)} fusion(bf16[2,10,3312]{1,0,2:T(2,128)(2,1)S(1)} %bitcast.128, s32[21504]{0:T(1024)S(1)} %pad_clamp_fusion), kind=kCustom, calls=%fused_computation | custom fusion | bytes 1741824 | tf_op jit(solution)/shard_map/jit(_take)/gather | solution.py:89
  56.2 11.4 %convert_element_type.291 = f32[20736,2,10]{2,1,0:T(2,128)} convert(bf16[20736,2,10]{2,1,0:T(2,128)(2,1)} %gather_fusion) | non-fusion elementwise | flops 414720 | bytes 2488320 | tf_op jit(solution)/shard_map/convert_element_type | solution.py:89
  67.6 28.5 %copy.48 = f32[2,1,10,144,144]{4,3,0,2,1:T(8,128)S(1)} copy(f32[2,1,10,144,144]{2,0,4,3,1:T(2,128)} %bitcast.120) | data formatting | bytes 3317760 | tf_op jit(solution)/shard_map/convert_element_type | solution.py:89
  96.2 2.0 broadcast_add_fusion
  98.2 4.0 %copy.37 = f32[2,1,10,144,144]{3,4,2,0,1:T(8,128)} copy(f32[2,1,10,144,144]{4,3,0,2,1:T(8,128)} %broadcast_add_fusion) | data formatting | bytes 3317760
  103.3 1.3 copy.35
  105.8 180.3 %while.15 = (s32[]{:T(128)}, bf16[4,6,12,320]{3,2,1,0:T(8,128)(2,1)S(1)}, bf16[1,4,6,12,320]{4,3,2,1,0:T(8,128)(2,1)}, s32[2]{0:T(128)}, pred[]{:T(512)}, /*inde...) while((s32[]{:T(128)}, ...), condition=%wide.region_7.8_spmd.clone, body=%wide.region_0.7_spmd.clone.sunk | while | flops 794450176 | bytes 33053972 | solution.py:235
  107.1 2.7 collective-permute-done
  109.8 14.9 %collective-permute-start.1 = (bf16[4,9,6,320]{3,2,1,0:T(8,128)(2,1)S(1)}, bf16[4,9,6,320]{3,2,1,0:T(8,128)(2,1)S(1)}, u32[]{:S(2)}, u32[]{:S(2)}) collective-permute-start(bf16[4,9,6,320]{3,2,1,0:T(8,128)(2,1)S(1)} %pad_maximum_fusion.3), channel_id=1, source_target_pairs={{32,0},{64,32},{96,64},{128,96},{160,128},{192,160},{224,192},{256... | collective-permute-start | bytes 414728 | tf_op jit(solution)/shard_map/while/body/eval_jaxpr/ppermute | solution.py:16
  125.4 4.4 %collective-permute-done.1 = bf16[4,9,6,320]{3,2,1,0:T(8,128)(2,1)S(1)} collective-permute-done((bf16[4,9,6,320]{3,2,1,0:T(8,128)(2,1)S(1)}, bf16[4,9,6,320]{3,2,1,0:T(8,128)(2,1)S(1)}, u32[]{:S(2)}, u32[]{:S(2)}) %collective-permute-start.1) | collective-permute-done | bytes 138272 | tf_op jit(solution)/shard_map/while/body/eval_jaxpr/ppermute | solution.py:16
  129.8 1.4 fusion.267
  131.3 1.6 fusion.268
  133.6 0.9 copy.59
  134.5 0.9 copy.60
  135.5 2.6 bitcast_add_fusion.2
  138.1 1.2 fusion.270
  139.3 1.9 copy.58
  141.2 2.5 fusion.271
  143.7 1.9 copy.61
  146.5 1.3 dynamic_update_slice.17
  147.9 1.9 collective-permute-start.2
  152.5 12.8 %collective-permute-done.2 = bf16[4,9,6,320]{3,2,1,0:T(8,128)(2,1)S(1)} collective-permute-done((bf16[4,9,6,320]{3,2,1,0:T(8,128)(2,1)S(1)}, bf16[4,9,6,320]{3,2,1,0:T(8,128)(2,1)S(1)}, u32[]{:S(2)}, u32[]{:S(2)}) %collective-permute-start.2) | collective-permute-done | bytes 138272 | tf_op jit(solution)/shard_map/while/body/eval_jaxpr/ppermute | solution.py:16
  165.5 5.7 %collective-permute-done.3 = bf16[4,3,12,320]{3,2,1,0:T(8,128)(2,1)S(1)} collective-permute-done((bf16[4,3,12,320]{3,2,1,0:T(8,128)(2,1)S(1)}, bf16[4,3,12,320]{3,2,1,0:T(8,128)(2,1)S(1)}, u32[]{:S(2)}, u32[]{:S(2)}) %collective-permute-start.3) | collective-permute-done | bytes 92192 | tf_op jit(solution)/shard_map/while/body/eval_jaxpr/ppermute | solution.py:16
  172.5 5.1 %fusion.277 = bf16[288,320]{1,0:T(8,128)(2,1)S(1)} fusion(f32[288,320]{1,0:T(8,128)S(1)} %get-tuple-element.601, bf16[1280,320]{1,0:T(8,128)(2,1)S(1)} %copy-done.8, bf16[320,1280]{1,0:T(8,128)(2,1)} %get-tuple-element.675, f32[1280]{0:T(1024)S(1)} %convert_element_type.385, f32[320]{0:T(512)S(1)} %get-tuple-element.602, f32[320]{0:T(512)S(1)} %copy-done.18, ...), kind=kOutput, calls=%fused_computation.34.clone.1 | convolution fusion | flops 496926720 | bytes 2202624 | tf_op jit(solution)/shard_map/while/body/eval_jaxpr/dot_general | solution.py:127
  177.8 10.0 %collective-permute-start.4 = (bf16[4,6,12,320]{3,2,1,0:T(8,128)(2,1)S(1)}, bf16[4,6,12,320]{3,2,1,0:T(8,128)(2,1)S(1)}, u32[]{:S(2)}, u32[]{:S(2)}) collective-permute-start(bf16[4,6,12,320]{3,2,1,0:T(8,128)(2,1)S(1)} %bitcast_select_fusion.6), channel_id=1, source_target_pairs={{0,1},{1,0},{2,3},{3,2},{4,5},{5,4},{6,7},{7,6},{8,9},{9,8},{10,11... | collective-permute-start | bytes 552968 | tf_op jit(solution)/shard_map/while/body/eval_jaxpr/ppermute | solution.py:20
  188.6 14.1 %collective-permute-done.4 = bf16[4,6,12,320]{3,2,1,0:T(8,128)(2,1)S(1)} collective-permute-done((bf16[4,6,12,320]{3,2,1,0:T(8,128)(2,1)S(1)}, bf16[4,6,12,320]{3,2,1,0:T(8,128)(2,1)S(1)}, u32[]{:S(2)}, u32[]{:S(2)}) %collective-permute-start.4) | collective-permute-done | bytes 184352 | tf_op jit(solution)/shard_map/while/body/eval_jaxpr/ppermute | solution.py:20
  204.9 2.7 collective-permute-done
  207.6 6.2 %collective-permute-start.1 = (bf16[4,9,6,320]{3,2,1,0:T(8,128)(2,1)S(1)}, bf16[4,9,6,320]{3,2,1,0:T(8,128)(2,1)S(1)}, u32[]{:S(2)}, u32[]{:S(2)}) collective-permute-start(bf16[4,9,6,320]{3,2,1,0:T(8,128)(2,1)S(1)} %pad_maximum_fusion.3), channel_id=1, source_target_pairs={{32,0},{64,32},{96,64},{128,96},{160,128},{192,160},{224,192},{256... | collective-permute-start | bytes 414728 | tf_op jit(solution)/shard_map/while/body/eval_jaxpr/ppermute | solution.py:16
  214.5 4.2 %collective-permute-done.1 = bf16[4,9,6,320]{3,2,1,0:T(8,128)(2,1)S(1)} collective-permute-done((bf16[4,9,6,320]{3,2,1,0:T(8,128)(2,1)S(1)}, bf16[4,9,6,320]{3,2,1,0:T(8,128)(2,1)S(1)}, u32[]{:S(2)}, u32[]{:S(2)}) %collective-permute-start.1) | collective-permute-done | bytes 138272 | tf_op jit(solution)/shard_map/while/body/eval_jaxpr/ppermute | solution.py:16
  218.7 1.4 fusion.267
  220.2 1.6 fusion.268
  222.5 0.9 copy.59
  223.5 0.9 copy.60
  224.4 2.6 bitcast_add_fusion.2
  227.1 1.2 fusion.270
  228.3 1.9 copy.58
  230.1 2.5 fusion.271
  232.6 1.9 copy.61
  235.4 1.3 dynamic_update_slice.17
  236.8 1.9 collective-permute-start.2
  241.4 12.9 %collective-permute-done.2 = bf16[4,9,6,320]{3,2,1,0:T(8,128)(2,1)S(1)} collective-permute-done((bf16[4,9,6,320]{3,2,1,0:T(8,128)(2,1)S(1)}, bf16[4,9,6,320]{3,2,1,0:T(8,128)(2,1)S(1)}, u32[]{:S(2)}, u32[]{:S(2)}) %collective-permute-start.2) | collective-permute-done | bytes 138272 | tf_op jit(solution)/shard_map/while/body/eval_jaxpr/ppermute | solution.py:16
  254.6 5.6 %collective-permute-done.3 = bf16[4,3,12,320]{3,2,1,0:T(8,128)(2,1)S(1)} collective-permute-done((bf16[4,3,12,320]{3,2,1,0:T(8,128)(2,1)S(1)}, bf16[4,3,12,320]{3,2,1,0:T(8,128)(2,1)S(1)}, u32[]{:S(2)}, u32[]{:S(2)}) %collective-permute-start.3) | collective-permute-done | bytes 92192 | tf_op jit(solution)/shard_map/while/body/eval_jaxpr/ppermute | solution.py:16
  261.6 5.1 %fusion.277 = bf16[288,320]{1,0:T(8,128)(2,1)S(1)} fusion(f32[288,320]{1,0:T(8,128)S(1)} %get-tuple-element.601, bf16[1280,320]{1,0:T(8,128)(2,1)S(1)} %copy-done.8, bf16[320,1280]{1,0:T(8,128)(2,1)} %get-tuple-element.675, f32[1280]{0:T(1024)S(1)} %convert_element_type.385, f32[320]{0:T(512)S(1)} %get-tuple-element.602, f32[320]{0:T(512)S(1)} %copy-done.18, ...), kind=kOutput, calls=%fused_computation.34.clone.1 | convolution fusion | flops 496926720 | bytes 2202624 | tf_op jit(solution)/shard_map/while/body/eval_jaxpr/dot_general | solution.py:127
  266.8 3.2 collective-permute-start.4
  270.8 14.3 %collective-permute-done.4 = bf16[4,6,12,320]{3,2,1,0:T(8,128)(2,1)S(1)} collective-permute-done((bf16[4,6,12,320]{3,2,1,0:T(8,128)(2,1)S(1)}, bf16[4,6,12,320]{3,2,1,0:T(8,128)(2,1)S(1)}, u32[]{:S(2)}, u32[]{:S(2)}) %collective-permute-start.4) | collective-permute-done | bytes 184352 | tf_op jit(solution)/shard_map/while/body/eval_jaxpr/ppermute | solution.py:20
  287.4 2.7 collective-permute-done.5
  290.8 4.0 %collective-permute-start.6 = (bf16[4,9,6,320]{3,2,1,0:T(8,128)(2,1)}, bf16[4,9,6,320]{3,2,1,0:T(8,128)(2,1)}, u32[]{:S(2)}, u32[]{:S(2)}) collective-permute-start(bf16[4,9,6,320]{3,2,1,0:T(8,128)(2,1)} %pad_maximum_fusion.1), channel_id=1, source_target_pairs={{32,0},{64,32},{96,64},{128,96},{160,128},{192,160},{224,192},{256... | collective-permute-start | bytes 414728 | tf_op jit(solution)/shard_map/ppermute | solution.py:16
  295.5 30.1 %copy.42 = f32[2,10,144,144]{2,3,1,0:T(8,128)S(1)} copy(f32[2,10,144,144]{1,0,3,2:T(2,128)} %bitcast.121) | data formatting | bytes 3317760 | tf_op jit(solution)/shard_map/convert_element_type | solution.py:89
  325.6 2.8 fusion.162
  328.4 1.1 reshape.373
  329.4 1.6 fusion.116
  331.0 0.9 fusion.213
  331.9 1.8 copy.39
  333.7 1.8 copy.40
  335.5 1.7 add_add_fusion
  337.8 1.0 copy-done
  339.0 3.5 fusion.121
  342.6 0.9 copy.44
  344.4 1.3 dynamic_update_slice.14
  345.7 2.2 collective-permute-start.7
  348.0 14.4 %collective-permute-done.7 = bf16[4,9,6,320]{3,2,1,0:T(8,128)(2,1)S(1)} collective-permute-done((bf16[4,9,6,320]{3,2,1,0:T(8,128)(2,1)S(1)}, bf16[4,9,6,320]{3,2,1,0:T(8,128)(2,1)S(1)}, u32[]{:S(2)}, u32[]{:S(2)}) %collective-permute-start.7) | collective-permute-done | bytes 138272 | tf_op jit(solution)/shard_map/ppermute | solution.py:16
  362.7 5.7 %collective-permute-done.8 = bf16[4,3,12,320]{3,2,1,0:T(8,128)(2,1)S(1)} collective-permute-done((bf16[4,3,12,320]{3,2,1,0:T(8,128)(2,1)S(1)}, bf16[4,3,12,320]{3,2,1,0:T(8,128)(2,1)S(1)}, u32[]{:S(2)}, u32[]{:S(2)}) %collective-permute-start.8) | collective-permute-done | bytes 92192 | tf_op jit(solution)/shard_map/ppermute | solution.py:16
  369.9 4.0 %fusion.120 = bf16[288,320]{1,0:T(8,128)(2,1)S(1)} fusion(f32[288,320]{1,0:T(8,128)S(1)} %get-tuple-element.450, bf16[1,1280,320]{1,2,0:T(8,128)(2,1)S(1)} %copy-done.11, f32[1280]{0:T(1024)S(1)} %add.402, f32[320]{0:T(512)S(1)} %get-tuple-element.389, f32[320]{0:T(512)S(1)} %copy-done.22, f32[320]{0:T(512)S(1)} %copy-done.23, ...), kind=kOutput, calls=%fused_computation.184 | convolution fusion | flops 496926720 | bytes 2202624 | tf_op jit(solution)/shard_map/dot_general | solution.py:127
  (185 shorter events, 24.5 us)
Async XLA Ops:
  0.0 5.0 %copy-start.17 = (s32[20736]{0:T(1024)S(1)}, s32[20736]{0:T(1024)}, u32[]{:S(2)}) copy-start(s32[20736]{0:T(1024)} %constant.406) | copy-start | bytes 248836
  0.4 0.7 copy-start.6
  98.2 4.0 %copy-start.16 = (bf16[1,4,6,12,320]{4,1,3,2,0:T(4,128)(2,1)S(1)}, bf16[1,4,6,12,320]{4,1,3,2,0:T(4,128)(2,1)}, u32[]{:S(2)}) copy-start(bf16[1,4,6,12,320]{4,1,3,2,0:T(4,128)(2,1)} %param.14) | copy-start | bytes 552964
  98.2 4.1 %copy-start.20 = (bf16[1,1280]{1,0:T(2,128)(2,1)S(1)}, bf16[1,1280]{1,0:T(2,128)(2,1)}, u32[]{:S(2)}) copy-start(bf16[1,1280]{1,0:T(2,128)(2,1)} %param.21) | copy-start | bytes 7684
  98.2 4.2 %copy-start.21 = (bf16[1,960]{1,0:T(2,128)(2,1)S(1)}, bf16[1,960]{1,0:T(2,128)(2,1)}, u32[]{:S(2)}) copy-start(bf16[1,960]{1,0:T(2,128)(2,1)} %param.18) | copy-start | bytes 5764
  102.2 1.1 copy-start.10
  102.2 2.5 copy-start.13
  102.2 2.5 copy-start.14
  102.2 3.6 copy-start.15
  107.0 2.7 collective-permute-start
  109.8 20.0 %collective-permute-start.1 = (bf16[4,9,6,320]{3,2,1,0:T(8,128)(2,1)S(1)}, bf16[4,9,6,320]{3,2,1,0:T(8,128)(2,1)S(1)}, u32[]{:S(2)}, u32[]{:S(2)}) collective-permute-start(bf16[4,9,6,320]{3,2,1,0:T(8,128)(2,1)S(1)} %pad_maximum_fusion.3), channel_id=1, source_target_pairs={{32,0},{64,32},{96,64},{128,96},{160,128},{192,160},{224,192},{256... | collective-permute-start | bytes 414728 | tf_op jit(solution)/shard_map/while/body/eval_jaxpr/ppermute | solution.py:16
  146.3 3.6 copy-start.25
  147.9 17.4 %collective-permute-start.2 = (bf16[4,9,6,320]{3,2,1,0:T(8,128)(2,1)S(1)}, bf16[4,9,6,320]{3,2,1,0:T(8,128)(2,1)S(1)}, u32[]{:S(2)}, u32[]{:S(2)}) collective-permute-start(bf16[4,9,6,320]{3,2,1,0:T(8,128)(2,1)S(1)} %slice.318), channel_id=1, source_target_pairs={{736,0},{0,32},{32,64},{64,96},{96,128},{128,160},{160,192},{192,2... | collective-permute-start | bytes 414728 | tf_op jit(solution)/shard_map/while/body/eval_jaxpr/ppermute | solution.py:16
  165.4 6.2 %copy-start.4 = (bf16[320,320]{1,0:T(8,128)(2,1)S(1)}, bf16[320,320]{1,0:T(8,128)(2,1)}, u32[]{:S(2)}) copy-start(bf16[320,320]{1,0:T(8,128)(2,1)} %get-tuple-element.673) | copy-start | bytes 614404 | tf_op jit(solution)/shard_map/while
  165.5 5.8 %collective-permute-start.3 = (bf16[4,3,12,320]{3,2,1,0:T(8,128)(2,1)S(1)}, bf16[4,3,12,320]{3,2,1,0:T(8,128)(2,1)S(1)}, u32[]{:S(2)}, u32[]{:S(2)}) collective-permute-start(bf16[4,3,12,320]{3,2,1,0:T(8,128)(2,1)S(1)} %fusion.273), channel_id=1, source_target_pairs={{30,0},{0,2},{2,4},{4,6},{6,8},{8,10},{10,12},{12,14},{14,16},{16,... | collective-permute-start | bytes 276488 | tf_op jit(solution)/shard_map/while/body/eval_jaxpr/ppermute | solution.py:16
  171.3 1.2 copy-start.8
  171.3 1.2 copy-start.18
  171.4 1.2 copy-start.19
  177.7 25.1 %copy-start.1 = (bf16[1,4,6,12,320]{4,3,2,1,0:T(8,128)(2,1)S(1)}, bf16[1,4,6,12,320]{4,3,2,1,0:T(8,128)(2,1)}, u32[]{:S(2)}) copy-start(bf16[1,4,6,12,320]{4,3,2,1,0:T(8,128)(2,1)} %get-tuple-element.634) | copy-start | bytes 552964 | tf_op jit(solution)/shard_map/while
  177.8 24.9 %collective-permute-start.4 = (bf16[4,6,12,320]{3,2,1,0:T(8,128)(2,1)S(1)}, bf16[4,6,12,320]{3,2,1,0:T(8,128)(2,1)S(1)}, u32[]{:S(2)}, u32[]{:S(2)}) collective-permute-start(bf16[4,6,12,320]{3,2,1,0:T(8,128)(2,1)S(1)} %bitcast_select_fusion.6), channel_id=1, source_target_pairs={{0,1},{1,0},{2,3},{3,2},{4,5},{5,4},{6,7},{7,6},{8,9},{9,8},{10,11... | collective-permute-start | bytes 552968 | tf_op jit(solution)/shard_map/while/body/eval_jaxpr/ppermute | solution.py:20
  202.9 0.7 copy-start.2
  204.9 2.7 collective-permute-start
  207.6 11.1 %collective-permute-start.1 = (bf16[4,9,6,320]{3,2,1,0:T(8,128)(2,1)S(1)}, bf16[4,9,6,320]{3,2,1,0:T(8,128)(2,1)S(1)}, u32[]{:S(2)}, u32[]{:S(2)}) collective-permute-start(bf16[4,9,6,320]{3,2,1,0:T(8,128)(2,1)S(1)} %pad_maximum_fusion.3), channel_id=1, source_target_pairs={{32,0},{64,32},{96,64},{128,96},{160,128},{192,160},{224,192},{256... | collective-permute-start | bytes 414728 | tf_op jit(solution)/shard_map/while/body/eval_jaxpr/ppermute | solution.py:16
  235.3 3.6 copy-start.25
  236.8 17.5 %collective-permute-start.2 = (bf16[4,9,6,320]{3,2,1,0:T(8,128)(2,1)S(1)}, bf16[4,9,6,320]{3,2,1,0:T(8,128)(2,1)S(1)}, u32[]{:S(2)}, u32[]{:S(2)}) collective-permute-start(bf16[4,9,6,320]{3,2,1,0:T(8,128)(2,1)S(1)} %slice.318), channel_id=1, source_target_pairs={{736,0},{0,32},{32,64},{64,96},{96,128},{128,160},{160,192},{192,2... | collective-permute-start | bytes 414728 | tf_op jit(solution)/shard_map/while/body/eval_jaxpr/ppermute | solution.py:16
  254.4 6.2 %copy-start.4 = (bf16[320,320]{1,0:T(8,128)(2,1)S(1)}, bf16[320,320]{1,0:T(8,128)(2,1)}, u32[]{:S(2)}) copy-start(bf16[320,320]{1,0:T(8,128)(2,1)} %get-tuple-element.673) | copy-start | bytes 614404 | tf_op jit(solution)/shard_map/while
  254.5 5.8 %collective-permute-start.3 = (bf16[4,3,12,320]{3,2,1,0:T(8,128)(2,1)S(1)}, bf16[4,3,12,320]{3,2,1,0:T(8,128)(2,1)S(1)}, u32[]{:S(2)}, u32[]{:S(2)}) collective-permute-start(bf16[4,3,12,320]{3,2,1,0:T(8,128)(2,1)S(1)} %fusion.273), channel_id=1, source_target_pairs={{30,0},{0,2},{2,4},{4,6},{6,8},{8,10},{10,12},{12,14},{14,16},{16,... | collective-permute-start | bytes 276488 | tf_op jit(solution)/shard_map/while/body/eval_jaxpr/ppermute | solution.py:16
  260.4 1.2 copy-start.8
  260.4 1.2 copy-start.18
  260.4 1.2 copy-start.19
  266.7 18.5 %copy-start.1 = (bf16[1,4,6,12,320]{4,3,2,1,0:T(8,128)(2,1)S(1)}, bf16[1,4,6,12,320]{4,3,2,1,0:T(8,128)(2,1)}, u32[]{:S(2)}) copy-start(bf16[1,4,6,12,320]{4,3,2,1,0:T(8,128)(2,1)} %get-tuple-element.634) | copy-start | bytes 552964 | tf_op jit(solution)/shard_map/while
  266.8 18.3 %collective-permute-start.4 = (bf16[4,6,12,320]{3,2,1,0:T(8,128)(2,1)S(1)}, bf16[4,6,12,320]{3,2,1,0:T(8,128)(2,1)S(1)}, u32[]{:S(2)}, u32[]{:S(2)}) collective-permute-start(bf16[4,6,12,320]{3,2,1,0:T(8,128)(2,1)S(1)} %bitcast_select_fusion.6), channel_id=1, source_target_pairs={{0,1},{1,0},{2,3},{3,2},{4,5},{5,4},{6,7},{7,6},{8,9},{9,8},{10,11... | collective-permute-start | bytes 552968 | tf_op jit(solution)/shard_map/while/body/eval_jaxpr/ppermute | solution.py:20
  285.3 0.7 copy-start.2
  287.4 2.7 collective-permute-start.5
  290.1 5.4 %copy-start.12 = (bf16[4,3,12,320]{3,2,1,0:T(8,128)(2,1)}, bf16[4,3,12,320]{3,2,1,0:T(8,128)(2,1)S(1)}, u32[]{:S(2)}) copy-start(bf16[4,3,12,320]{3,2,1,0:T(8,128)(2,1)S(1)} %collective-permute-done.5) | copy-start | bytes 276484
  290.8 34.8 %collective-permute-start.6 = (bf16[4,9,6,320]{3,2,1,0:T(8,128)(2,1)}, bf16[4,9,6,320]{3,2,1,0:T(8,128)(2,1)}, u32[]{:S(2)}, u32[]{:S(2)}) collective-permute-start(bf16[4,9,6,320]{3,2,1,0:T(8,128)(2,1)} %pad_maximum_fusion.1), channel_id=1, source_target_pairs={{32,0},{64,32},{96,64},{128,96},{160,128},{192,160},{224,192},{256... | collective-permute-start | bytes 414728 | tf_op jit(solution)/shard_map/ppermute | solution.py:16
  331.0 4.6 %copy-start.7 = (f32[2,144,144]{1,2,0:T(8,128)S(1)}, f32[2,144,144]{1,2,0:T(8,128)}, u32[]{:S(2)}) copy-start(f32[2,144,144]{1,2,0:T(8,128)} %copy-done.6) | copy-start | bytes 497668
  337.2 1.6 copy-start
  337.2 1.6 copy-start.9
  345.7 16.7 %collective-permute-start.7 = (bf16[4,9,6,320]{3,2,1,0:T(8,128)(2,1)S(1)}, bf16[4,9,6,320]{3,2,1,0:T(8,128)(2,1)S(1)}, u32[]{:S(2)}, u32[]{:S(2)}) collective-permute-start(bf16[4,9,6,320]{3,2,1,0:T(8,128)(2,1)S(1)} %slice.235), channel_id=1, source_target_pairs={{736,0},{0,32},{32,64},{64,96},{96,128},{128,160},{160,192},{192,2... | collective-permute-start | bytes 414728 | tf_op jit(solution)/shard_map/ppermute | solution.py:16
  362.6 6.2 %copy-start.5 = (bf16[320,320]{1,0:T(8,128)(2,1)S(1)}, bf16[320,320]{1,0:T(8,128)(2,1)}, u32[]{:S(2)}) copy-start(bf16[320,320]{1,0:T(8,128)(2,1)} %get-tuple-element.686) | copy-start | bytes 614404
  362.7 5.8 %collective-permute-start.8 = (bf16[4,3,12,320]{3,2,1,0:T(8,128)(2,1)S(1)}, bf16[4,3,12,320]{3,2,1,0:T(8,128)(2,1)S(1)}, u32[]{:S(2)}, u32[]{:S(2)}) collective-permute-start(bf16[4,3,12,320]{3,2,1,0:T(8,128)(2,1)S(1)} %fusion.173), channel_id=1, source_target_pairs={{30,0},{0,2},{2,4},{4,6},{6,8},{8,10},{10,12},{12,14},{14,16},{16,... | collective-permute-start | bytes 276488 | tf_op jit(solution)/shard_map/ppermute | solution.py:16
  368.5 1.1 copy-start.11
  368.5 1.1 copy-start.22
  368.6 1.1 copy-start.23
  368.6 1.4 copy-start.24
  369.9 4.1 %copy-start.3 = (bf16[1,4,6,12,320]{4,3,2,1,0:T(8,128)(2,1)S(1)}, bf16[1,4,6,12,320]{4,3,2,1,0:T(8,128)(2,1)}, u32[]{:S(2)}) copy-start(bf16[1,4,6,12,320]{4,3,2,1,0:T(8,128)(2,1)} %get-tuple-element.269) | copy-start | bytes 552964
where the time goes:
time: 377 us; the launch traced here: 375 us
  local copies, waits for them, and re-layouts  153 us (41%)
  waiting for transfers between devices  102 us (27%)
  starting transfers between devices  44.6 us (12%)
  matrix products  35.8 us (9%)
  other arithmetic  32.3 us (9%)
  loops' own time  5.97 us (2%)
    ppermute x12, waiting for transfers between devices, shifted(): return lax.ppermute(block, axis, route)  73.9 us
    convert_element_type x2, local copies, waits for them, and re-layouts, dense_bias(): dense = jnp.take(table, pair_ids, axis=3).astype(jnp.float32)  58.6 us
    gather x1, local copies, waits for them, and re-layouts, dense_bias(): dense = jnp.take(table, pair_ids, axis=3).astype(jnp.float32)  51.2 us
    ppermute x12, starting transfers between devices, shifted(): return lax.ppermute(block, axis, route)  31.4 us
    ppermute x2, waiting for transfers between devices, partner(): lax.ppermute(x, axis, [(i, i ^ 1 << apart) for i in range(lax.axis_size(a...  28.5 us
    dot_general x3, matrix products, finish_block(): jnp.dot(hidden, fc2_w, preferred_element_type=jnp.float32)  14.3 us
    ppermute x2, starting transfers between devices, partner(): lax.ppermute(x, axis, [(i, i ^ 1 << apart) for i in range(lax.axis_size(a...  13.3 us
    unnamed x43, local copies, waits for them, and re-layouts  11.7 us
  transfers between devices with their start and end apart: 14, of which 13 were waited for; matrix products, arithmetic and copies ran while one was open for 9% of the time, Pallas kernels for 0%

commit v1 on v0

v1 whole, which is shorter than its diff:
```python
import functools

import jax
import jax.numpy as jnp
import numpy as np
from jax import lax
from jax.experimental import pallas as pl
from jax.experimental.pallas import tpu as pltpu
from jax.sharding import PartitionSpec as P

HD = 32
HEADS = 10
C = 320
WLEV = 2
WLAT = 6
WLON = 12
WIN = WLEV * WLAT * WLON
QUARTER = WIN // 4
PIECE = QUARTER // WLEV
SPAN = 2 * WLON - 1
AXES = ("lon", "lat", "section")
VMEM_LIMIT = 20 * 1024 * 1024


def token_row(lev, lat, lon):
    quarter = (lat // 3) * 2 + lon // 6
    return quarter * QUARTER + lev * PIECE + (lat % 3) * 6 + lon % 6


def spread_matrix():
    spread = np.zeros((WLEV * WLAT * SPAN, WLON, 256), np.float32)
    for lev in range(WLEV):
        for lat in range(WLAT):
            for lon in range(WLON):
                for query_lon in range(WLON):
                    source = (lev * WLAT + lat) * SPAN + query_lon - lon + WLON - 1
                    spread[source, query_lon, token_row(lev, lat, lon)] = 1.0
    return spread.reshape(WLEV * WLAT * SPAN, WLON * 256).astype(jnp.bfloat16)


def arrange_matrix():
    arrange = np.zeros((2 * WIN, 2 * WIN), np.float32)
    for lev in range(4):
        for lat in range(WLAT):
            for lon in range(WLON):
                row = (lev // 2) * WIN + token_row(lev % 2, lat, lon)
                arrange[row, (lat * WLON + lon) * 4 + lev] = 1.0
    return arrange.astype(jnp.bfloat16)


def place_matrix():
    arrange = np.zeros((2 * WIN, 2 * WIN), np.float32)
    for lev in range(4):
        for lat in range(WLAT):
            for lon in range(WLON):
                quarter = (lat // 3) * 2 + lon // 6
                source = ((quarter * 4 + (lev + 3) % 4) * 3 + lat % 3) * 6 + lon % 6
                arrange[(lat * WLON + lon) * 4 + lev, source] = 1.0
    return arrange.astype(jnp.bfloat16)


def prepare_kernel(table_ref, spread_ref, addend_ref, wide_ref):
    section = lax.axis_index("section")
    last_lat = lax.axis_index("lat") == lax.axis_size("lat") - 1
    wide_ref[0:HEADS, :] = table_ref[0, 0, 0].astype(jnp.float32)
    wide_ref[16 : 16 + HEADS, :] = table_ref[0, 1, 0].astype(jnp.float32)
    for lev in range(WLEV):
        for lat in range(WLAT):
            parts = []
            for key_lev in range(WLEV):
                for key_lat in range(WLAT):
                    at = ((key_lev * WLEV + lev) * WLAT * WLAT + key_lat * WLAT + lat) * SPAN
                    parts.append(wide_ref[:, at : at + SPAN])
            rows = jnp.concatenate(parts, axis=1).astype(jnp.bfloat16)
            dense = jnp.dot(rows, spread_ref[...], preferred_element_type=jnp.float32)
            for lon in range(WLON):
                row = token_row(lev, lat, lon)
                for window in range(2):
                    for tile in range(2):
                        lanes = lon * 256 + tile * 128
                        addend_ref[
                            tile, pl.ds(window * HEADS * WIN + row, HEADS, stride=WIN), :
                        ] = dense[window * 16 : window * 16 + HEADS, lanes : lanes + 128]

    @pl.when(section == 1)
    def mask():
        for tile in range(2):
            query = lax.broadcasted_iota(jnp.int32, (WIN, 128), 0)
            key = lax.broadcasted_iota(jnp.int32, (WIN, 128), 1) + tile * 128
            lat_differs = jnp.logical_and((query >= 2 * QUARTER) != (key >= 2 * QUARTER), last_lat)
            lev_differs = (query % QUARTER >= PIECE) != (key % QUARTER >= PIECE)
            for window in range(2):
                barred = jnp.logical_or(lat_differs, lev_differs) if window else lat_differs
                for head in range(HEADS):
                    at = (window * HEADS + head) * WIN
                    addend_ref[tile, at : at + WIN, :] = jnp.where(
                        barred, jnp.float32(-1e30), addend_ref[tile, at : at + WIN, :]
                    )


def layer_norm(values, norm_gain, norm_shift):
    center = values - jnp.mean(values, axis=-1, keepdims=True)
    spread = jnp.mean(center * center, axis=-1, keepdims=True)
    return center * lax.rsqrt(spread + 1e-05) * norm_gain.astype(jnp.float32) + norm_shift.astype(
        jnp.float32
    )


def run_block(field_ref, params, addend_ref, packed_ref, attended_ref):
    ln_g, ln_s, qkv_w, qkv_b, proj_w, fc1_w, fc1_b, fc2_w, out_b = params
    normed = layer_norm(field_ref[...], ln_g[0, 0:1], ln_s[0, 0:1]).astype(jnp.bfloat16)
    packed = jnp.dot(normed, qkv_w[0], preferred_element_type=jnp.float32)
    packed = (packed + qkv_b[...].astype(jnp.float32)).astype(jnp.bfloat16)
    packed_ref[:, 0:C] = packed[:, 0:C]
    packed_ref[:, 384 : 384 + C] = packed[:, C : 2 * C]
    packed_ref[:, 768 : 768 + C] = packed[:, 2 * C :]
    for window in range(2):
        first = window * WIN
        for group in range(3):
            width = 128 if group < 2 else 64
            heads = width // HD
            lanes = group * 128
            queries = packed_ref[first : first + WIN, lanes : lanes + width]
            keys = packed_ref[first : first + WIN, 384 + lanes : 384 + lanes + width]
            values = packed_ref[first : first + WIN, 768 + lanes : 768 + lanes + width]
            lane_head = lax.broadcasted_iota(jnp.int32, (WIN, width), 1) // HD
            ones = jnp.ones((WIN, width), jnp.bfloat16)
            values = jnp.concatenate([values, ones], axis=1)
            gathered = jnp.zeros((WIN, width), jnp.float32)
            for head in range(heads):
                own = jnp.where(lane_head == head, queries, jnp.zeros_like(queries))
                scores = lax.dot_general(
                    own, keys, (((1,), (1,)), ((), ())), preferred_element_type=jnp.float32
                ) * HD ** (-0.5)
                at = (window * HEADS + group * 4 + head) * WIN
                scores = scores + jnp.concatenate(
                    [addend_ref[0, at : at + WIN, :], addend_ref[1, at : at + WIN, 0 : WIN - 128]],
                    axis=1,
                )
                raised = jnp.exp(scores - jnp.max(scores, axis=-1, keepdims=True))
                mixed = jnp.dot(
                    raised.astype(jnp.bfloat16), values, preferred_element_type=jnp.float32
                )
                mixed = mixed[:, :width] / mixed[:, width:]
                gathered = jnp.where(lane_head == head, mixed, gathered)
            attended_ref[first : first + WIN, lanes : lanes + width] = gathered.astype(jnp.bfloat16)
    mid = (
        field_ref[...]
        + jnp.dot(attended_ref[...], proj_w[0], preferred_element_type=jnp.float32)
        + out_b[0, 0:1].astype(jnp.float32)
    )
    normed_two = layer_norm(mid, ln_g[0, 1:2], ln_s[0, 1:2]).astype(jnp.bfloat16)
    hidden = jnp.dot(normed_two, fc1_w[0], preferred_element_type=jnp.float32)
    hidden = hidden + fc1_b[...].astype(jnp.float32)
    hidden = (hidden * 0.5 * (1.0 + lax.erf(hidden * np.float32(np.sqrt(0.5))))).astype(
        jnp.bfloat16
    )
    field_ref[...] = (
        mid
        + jnp.dot(hidden, fc2_w[0], preferred_element_type=jnp.float32)
        + out_b[0, 1:2].astype(jnp.float32)
    )


def first_kernel(patch_ref, arrange_ref, *refs):
    params, (addend_ref,), outs = refs[:9], refs[9:10], refs[10:14]
    field_ref, packed_ref, attended_ref, quarter_ref = refs[14:]

    @pl.when(lax.axis_index("section") == 0)
    def work():
        for lat in range(WLAT):
            for lon in range(WLON):
                at = (lat * WLON + lon) * 4
                field_ref[at : at + 4, :] = patch_ref[0, lat, lon].astype(jnp.float32)
        field_ref[...] = jnp.dot(
            arrange_ref[...],
            field_ref[...].astype(jnp.bfloat16),
            preferred_element_type=jnp.float32,
        )
        run_block(field_ref, params, addend_ref, packed_ref, attended_ref)
        for quarter in range(4):
            for place in range(4):
                lev = (place + 1) % 4
                at = (lev // 2) * WIN + quarter * QUARTER + (lev % 2) * PIECE
                quarter_ref[place * PIECE : (place + 1) * PIECE, :] = field_ref[at : at + PIECE, :]
            outs[quarter][...] = quarter_ref[...].astype(jnp.bfloat16)


def second_kernel(*refs):
    quarters, params, (addend_ref,), outs = refs[:4], refs[4:13], refs[13:14], refs[14:18]
    field_ref, packed_ref, attended_ref, quarter_ref = refs[18:]

    @pl.when(lax.axis_index("section") == 1)
    def work():
        for quarter in range(4):
            held = quarters[quarter][...].astype(jnp.float32)
            for window in range(2):
                at = window * WIN + quarter * QUARTER
                field_ref[at : at + QUARTER, :] = held[window * QUARTER : (window + 1) * QUARTER]
        run_block(field_ref, params, addend_ref, packed_ref, attended_ref)
        for quarter in range(4):
            for window in range(2):
                at = window * WIN + quarter * QUARTER
                quarter_ref[window * QUARTER : (window + 1) * QUARTER, :] = field_ref[
                    at : at + QUARTER, :
                ]
            outs[quarter][...] = quarter_ref[...].astype(jnp.bfloat16)


def place_kernel(*refs):
    arrange_ref, out_ref, grid_ref = refs[8:]

    def place(quarters):
        held = jnp.concatenate([quarter[...] for quarter in quarters], axis=0)
        grid_ref[...] = jnp.dot(arrange_ref[...], held, preferred_element_type=jnp.float32)
        for lat in range(WLAT):
            for lon in range(WLON):
                at = (lat * WLON + lon) * 4
                out_ref[0, lat, lon] = grid_ref[at : at + 4, :].astype(jnp.bfloat16)

    section = lax.axis_index("section")
    pl.when(section == 0)(lambda: place(refs[0:4]))
    pl.when(section == 1)(lambda: place(refs[4:8]))


def call(kernel, operands, outs, scratch, flops):
    whole = pl.BlockSpec(memory_space=pltpu.VMEM)
    moved = sum(op.size * op.dtype.itemsize for op in operands)
    return pl.pallas_call(
        kernel,
        out_shape=outs,
        in_specs=[whole] * len(operands),
        out_specs=jax.tree.map(lambda unused: whole, outs),
        scratch_shapes=scratch,
        compiler_params=pltpu.CompilerParams(vmem_limit_bytes=VMEM_LIMIT),
        cost_estimate=pl.CostEstimate(flops=flops, bytes_accessed=moved, transcendentals=0),
    )(*operands)


QUARTERS = [jax.ShapeDtypeStruct((2 * QUARTER, C), jnp.bfloat16)] * 4
BLOCK_SCRATCH = [
    pltpu.VMEM((2 * WIN, C), jnp.float32),
    pltpu.VMEM((2 * WIN, 3 * 384), jnp.bfloat16),
    pltpu.VMEM((2 * WIN, C), jnp.bfloat16),
    pltpu.VMEM((2 * QUARTER, C), jnp.float32),
]
BLOCK_FLOPS = 800_000_000


def send(block, source, target, lat_step, lon_step):
    lons, lats = lax.axis_size("lon"), lax.axis_size("lat")
    route = []
    for lon in range(lons):
        for lat in range(lats):
            there = ((lon + lon_step) % lons) * lats + (lat + lat_step) % lats
            route.append(((lon * lats + lat) * 2 + source, there * 2 + target))
    return lax.ppermute(block, AXES, route)


def to_shifted(quarters):
    moved = [send(quarters[q], 0, 1, q // 2 - 1, q % 2 - 1) for q in range(4)]
    return [moved[3 - q] for q in range(4)]


def body(
    inputs,
    ln_gain,
    ln_shift,
    qkv_weight,
    qkv_bias,
    proj_weight,
    fc1_weight,
    fc1_bias,
    fc2_weight,
    out_bias,
    bias_table,
):
    params = (
        ln_gain,
        ln_shift,
        qkv_weight,
        qkv_bias,
        proj_weight,
        fc1_weight,
        fc1_bias,
        fc2_weight,
        out_bias,
    )
    patch = inputs.transpose(0, 2, 3, 1, 4)
    other = send(patch, 1, 0, 0, 0)
    addend = call(
        prepare_kernel,
        (bias_table, jnp.asarray(spread_matrix())),
        jax.ShapeDtypeStruct((2, 2 * HEADS * WIN, 128), jnp.float32),
        [pltpu.VMEM((32, bias_table.shape[-1]), jnp.float32)],
        200_000_000,
    )
    arrange = jnp.asarray(arrange_matrix())
    block_one = functools.partial(
        call, first_kernel, outs=QUARTERS, scratch=BLOCK_SCRATCH, flops=BLOCK_FLOPS
    )
    block_two = functools.partial(
        call, second_kernel, outs=QUARTERS, scratch=BLOCK_SCRATCH, flops=BLOCK_FLOPS
    )
    own_shifted = to_shifted(block_one((patch, arrange, *params, addend)))
    other_shifted = to_shifted(block_one((other, arrange, *params, addend)))
    own_done = block_two((*own_shifted, *params, addend))
    own_back = [send(own_done[3 - q], 1, 0, 1 - q // 2, 1 - q % 2) for q in range(4)]
    other_done = block_two((*other_shifted, *params, addend))
    other_back = [send(other_done[3 - q], 1, 1, 1 - q // 2, 1 - q % 2) for q in range(3)]
    placed = call(
        place_kernel,
        (*own_back, *other_back, other_done[0], jnp.asarray(place_matrix())),
        jax.ShapeDtypeStruct(patch.shape, patch.dtype),
        [pltpu.VMEM((2 * WIN, C), jnp.float32)],
        1_000_000,
    )
    return placed.transpose(0, 3, 1, 2, 4)


def solution(mesh):
    return jax.shard_map(
        body,
        mesh=mesh,
        in_specs=(
            P("section", None, "lat", "lon", None),
            P("section", None, None),
            P("section", None, None),
            P("section", None, None),
            P("section", None),
            P("section", None, None),
            P("section", None, None),
            P("section", None),
            P("section", None, None),
            P("section", None, None),
            P("section", None, "lat", None, None),
        ),
        out_specs=P("section", None, "lat", "lon", None),
        check_vma=False,
    )
```

time: 377 us -> 91.9 us (0.24)
  the two profiles are of different devices: /device:TPU:32 before, /device:TPU:728 now
where the time goes in v1:
time: 91.9 us; the launch traced here: 91.5 us
  starting transfers between devices  59.8 us (65%)
  waiting for transfers between devices  15 us (16%)
  Pallas kernels  12.2 us (13%)
  local copies, waits for them, and re-layouts  4.11 us (4%)
    ppermute x16, starting transfers between devices, send(): return lax.ppermute(block, AXES, route)  59.8 us
    ppermute x16, waiting for transfers between devices, send(): return lax.ppermute(block, AXES, route)  15 us
    pallas_call x6, Pallas kernels, call(): pl.pallas_call(kernel, out_shape=outs, in_specs=[whole] * len(operands),...  12.2 us
    unnamed x26, local copies, waits for them, and re-layouts  4.11 us
  transfers between devices with their start and end apart: 16, of which 4 were waited for; matrix products, arithmetic and copies ran while one was open for 3% of the time, Pallas kernels for 12%

profile of v1, /device:TPU:728, one launch (start us, length us, event | category | flops | bytes accessed | tf_op | source)
XLA Modules:
  0.0 91.5 jit_solution(16325858800142899326)
XLA Ops:
  0.0 2.7 %collective-permute-start.8 = (bf16[1,6,12,4,320]{4,3,2,1,0:T(4,128)(2,1)}, bf16[1,6,12,4,320]{4,3,2,1,0:T(4,128)(2,1)S(1)}, u32[]{:S(2)}, u32[]{:S(2)}) collective-permute-start(bf16[1,6,12,4,320]{4,3,2,1,0:T(4,128)(2,1)} %bitcast.2), channel_id=1, source_target_pairs={{1,0},{3,2},{5,4},{7,6},{9,8},{11,10},{13,12},{15,14},{17,16},{19,... | collective-permute-start | bytes 552968 | tf_op jit(solution)/shard_map/ppermute | solution.py:257
  2.7 0.9 %copy.15.table_ref = bf16[1,2,1,10,3312]{4,3,2,1,0:T(8,128)(2,1)S(1)} copy(bf16[1,2,1,10,3312]{4,1,3,2,0:T(2,128)(2,1)} %param.24) | data formatting | bytes 264960 | tf_op args[10]
  3.7 0.0 copy-start
  3.7 0.0 copy-start.1
  3.7 0.0 copy-start.2
  3.7 0.0 copy-start.7
  3.7 0.0 copy-start.8
  3.7 0.0 copy-start.9
  3.7 0.0 copy-start.10
  3.7 0.0 copy-start.11
  3.8 1.7 %copy.16.refs_7_.refs_11_ = bf16[1,1280,320]{2,1,0:T(8,128)(2,1)S(1)} copy(bf16[1,1280,320]{1,2,0:T(8,128)(2,1)} %param.22) | data formatting | bytes 1638400 | tf_op args[8]
  5.4 0.0 copy-start.3
  5.4 1.5 %copy-done.3 = bf16[276,3072]{1,0:T(8,128)(2,1)S(1)} copy-done((bf16[276,3072]{1,0:T(8,128)(2,1)S(1)}, bf16[276,3072]{1,0:T(8,128)(2,1)}, u32[]{:S(2)}) %copy-start.3) | copy-done | bytes 1695768
  6.9 0.0 copy-start.4
  6.9 0.0 copy-start.6
  6.9 4.4 %shard_map.136.refs_9_.refs_13_ = f32[2,2880,128]{2,1,0:T(8,128)S(1)} custom-call(bf16[1,2,1,10,3312]{4,3,2,1,0:T(8,128)(2,1)S(1)} %copy.15.table_ref, bf16[276,3072]{1,0:T(8,128)(2,1)S(1)} %copy-done.3), custom_call_target="tpu_custom_call" | custom-call | flops 200000000 | bytes 1828224 | tf_op jit(solution)/shard_map/pallas_call | solution.py:229
  11.3 0.0 copy-done
  11.3 0.0 copy-done.1
  11.3 0.0 copy-done.2
  11.3 0.0 copy-done.7
  11.4 0.0 copy-done.8
  11.4 0.0 copy-done.9
  11.4 0.0 copy-done.10
  11.4 0.0 copy-done.11
  11.4 0.0 copy-done.4
  11.4 0.0 copy-done.6
  11.4 1.3 %collective-permute-start = (bf16[72,320]{1,0:T(8,128)(2,1)S(1)}, bf16[72,320]{1,0:T(8,128)(2,1)S(1)}, u32[]{:S(2)}, u32[]{:S(2)}) collective-permute-start(bf16[72,320]{1,0:T(8,128)(2,1)S(1)} %get-tuple-element.21), channel_id=1, source_target_pairs={{0,1},{2,3},{4,5},{6,7},{8,9},{10,11},{12,13},{14,15},{16,17},{18,... | collective-permute-start | bytes 138248 | tf_op jit(solution)/shard_map/ppermute | solution.py:257
  12.7 1.3 %collective-permute-start.1 = (bf16[72,320]{1,0:T(8,128)(2,1)S(1)}, bf16[72,320]{1,0:T(8,128)(2,1)S(1)}, u32[]{:S(2)}, u32[]{:S(2)}) collective-permute-start(bf16[72,320]{1,0:T(8,128)(2,1)S(1)} %get-tuple-element.22), channel_id=1, source_target_pairs={{0,737},{2,739},{4,741},{6,743},{8,745},{10,747},{12,749},{14,751}... | collective-permute-start | bytes 138248 | tf_op jit(solution)/shard_map/ppermute | solution.py:257
  14.0 1.3 %collective-permute-start.2 = (bf16[72,320]{1,0:T(8,128)(2,1)S(1)}, bf16[72,320]{1,0:T(8,128)(2,1)S(1)}, u32[]{:S(2)}, u32[]{:S(2)}) collective-permute-start(bf16[72,320]{1,0:T(8,128)(2,1)S(1)} %get-tuple-element.23), channel_id=1, source_target_pairs={{0,31},{2,1},{4,3},{6,5},{8,7},{10,9},{12,11},{14,13},{16,15},{18,... | collective-permute-start | bytes 138248 | tf_op jit(solution)/shard_map/ppermute | solution.py:257
  15.3 1.3 %collective-permute-start.3 = (bf16[72,320]{1,0:T(8,128)(2,1)S(1)}, bf16[72,320]{1,0:T(8,128)(2,1)S(1)}, u32[]{:S(2)}, u32[]{:S(2)}) collective-permute-start(bf16[72,320]{1,0:T(8,128)(2,1)S(1)} %get-tuple-element.24), channel_id=1, source_target_pairs={{0,767},{2,737},{4,739},{6,741},{8,743},{10,745},{12,747},{14,749}... | collective-permute-start | bytes 138248 | tf_op jit(solution)/shard_map/ppermute | solution.py:257
  16.6 0.0 collective-permute-done.8.patch_ref
  16.7 1.3 %collective-permute-start.9 = (bf16[72,320]{1,0:T(8,128)(2,1)S(1)}, bf16[72,320]{1,0:T(8,128)(2,1)S(1)}, u32[]{:S(2)}, u32[]{:S(2)}) collective-permute-start(bf16[72,320]{1,0:T(8,128)(2,1)S(1)} %get-tuple-element.29), channel_id=1, source_target_pairs={{0,1},{2,3},{4,5},{6,7},{8,9},{10,11},{12,13},{14,15},{16,17},{18,... | collective-permute-start | bytes 138248 | tf_op jit(solution)/shard_map/ppermute | solution.py:257
  18.0 6.0 %collective-permute-done.refs_0_ = bf16[72,320]{1,0:T(8,128)(2,1)S(1)} collective-permute-done((bf16[72,320]{1,0:T(8,128)(2,1)S(1)}, bf16[72,320]{1,0:T(8,128)(2,1)S(1)}, u32[]{:S(2)}, u32[]{:S(2)}) %collective-permute-start) | collective-permute-done | bytes 46112 | tf_op jit(solution)/shard_map/ppermute | solution.py:257
  24.0 1.3 %collective-permute-start.10 = (bf16[72,320]{1,0:T(8,128)(2,1)S(1)}, bf16[72,320]{1,0:T(8,128)(2,1)S(1)}, u32[]{:S(2)}, u32[]{:S(2)}) collective-permute-start(bf16[72,320]{1,0:T(8,128)(2,1)S(1)} %get-tuple-element.30), channel_id=1, source_target_pairs={{0,737},{2,739},{4,741},{6,743},{8,745},{10,747},{12,749},{14,751}... | collective-permute-start | bytes 138248 | tf_op jit(solution)/shard_map/ppermute | solution.py:257
  25.2 0.9 collective-permute-done.1.refs_1_
  26.1 1.3 %collective-permute-start.11 = (bf16[72,320]{1,0:T(8,128)(2,1)S(1)}, bf16[72,320]{1,0:T(8,128)(2,1)S(1)}, u32[]{:S(2)}, u32[]{:S(2)}) collective-permute-start(bf16[72,320]{1,0:T(8,128)(2,1)S(1)} %get-tuple-element.31), channel_id=1, source_target_pairs={{0,31},{2,1},{4,3},{6,5},{8,7},{10,9},{12,11},{14,13},{16,15},{18,... | collective-permute-start | bytes 138248 | tf_op jit(solution)/shard_map/ppermute | solution.py:257
  27.4 0.0 collective-permute-done.2.refs_2_
  27.4 1.3 %collective-permute-start.12 = (bf16[72,320]{1,0:T(8,128)(2,1)S(1)}, bf16[72,320]{1,0:T(8,128)(2,1)S(1)}, u32[]{:S(2)}, u32[]{:S(2)}) collective-permute-start(bf16[72,320]{1,0:T(8,128)(2,1)S(1)} %get-tuple-element.32), channel_id=1, source_target_pairs={{0,767},{2,737},{4,739},{6,741},{8,743},{10,745},{12,747},{14,749}... | collective-permute-start | bytes 138248 | tf_op jit(solution)/shard_map/ppermute | solution.py:257
  28.7 0.0 collective-permute-done.3.refs_3_
  28.7 3.4 %shard_map.138 = (bf16[72,320]{1,0:T(8,128)(2,1)S(1)}, bf16[72,320]{1,0:T(8,128)(2,1)S(1)}, bf16[72,320]{1,0:T(8,128)(2,1)S(1)}, bf16[72,320]{1,0:T(8,128)(2,1)S(1)}) custom-call(bf16[72,320]{1,0:T(8,128)(2,1)S(1)} %collective-permute-done.refs_0_, bf16[72,320]{1,0:T(8,128)(2,1)S(1)} %collective-permute-done.1.refs_1_, ...), custom_call_target="tpu_custom_call" | custom-call | flops 800000000 | bytes 5599360 | tf_op jit(solution)/shard_map/pallas_call | solution.py:229
  32.2 8.3 %collective-permute-start.4 = (bf16[72,320]{1,0:T(8,128)(2,1)S(1)}, bf16[72,320]{1,0:T(8,128)(2,1)S(1)}, u32[]{:S(2)}, u32[]{:S(2)}) collective-permute-start(bf16[72,320]{1,0:T(8,128)(2,1)S(1)} %get-tuple-element.25), channel_id=1, source_target_pairs={{1,34},{3,36},{5,38},{7,40},{9,42},{11,44},{13,46},{15,48},{17,50}... | collective-permute-start | bytes 138248 | tf_op jit(solution)/shard_map/ppermute | solution.py:257
  40.5 0.0 collective-permute-done.9.refs_0_
  40.5 0.0 copy-start.5
  40.5 30.0 %collective-permute-start.5 = (bf16[72,320]{1,0:T(8,128)(2,1)S(1)}, bf16[72,320]{1,0:T(8,128)(2,1)S(1)}, u32[]{:S(2)}, u32[]{:S(2)}) collective-permute-start(bf16[72,320]{1,0:T(8,128)(2,1)S(1)} %get-tuple-element.26), channel_id=1, source_target_pairs={{1,2},{3,4},{5,6},{7,8},{9,10},{11,12},{13,14},{15,16},{17,18},{19... | collective-permute-start | bytes 138248 | tf_op jit(solution)/shard_map/ppermute | solution.py:257
  70.5 0.0 collective-permute-done.10.refs_1_
  70.5 1.3 %collective-permute-start.6 = (bf16[72,320]{1,0:T(8,128)(2,1)S(1)}, bf16[72,320]{1,0:T(8,128)(2,1)S(1)}, u32[]{:S(2)}, u32[]{:S(2)}) collective-permute-start(bf16[72,320]{1,0:T(8,128)(2,1)S(1)} %get-tuple-element.27), channel_id=1, source_target_pairs={{1,32},{3,34},{5,36},{7,38},{9,40},{11,42},{13,44},{15,46},{17,48}... | collective-permute-start | bytes 138248 | tf_op jit(solution)/shard_map/ppermute | solution.py:257
  71.8 0.0 collective-permute-done.11.refs_2_
  71.8 1.3 %collective-permute-start.7 = (bf16[72,320]{1,0:T(8,128)(2,1)S(1)}, bf16[72,320]{1,0:T(8,128)(2,1)S(1)}, u32[]{:S(2)}, u32[]{:S(2)}) collective-permute-start(bf16[72,320]{1,0:T(8,128)(2,1)S(1)} %get-tuple-element.28), channel_id=1, source_target_pairs={{1,0},{3,2},{5,4},{7,6},{9,8},{11,10},{13,12},{15,14},{17,16},{19,... | collective-permute-start | bytes 138248 | tf_op jit(solution)/shard_map/ppermute | solution.py:257
  73.1 0.0 collective-permute-done.12.refs_3_
  73.1 3.3 %shard_map.140 = (bf16[72,320]{1,0:T(8,128)(2,1)S(1)}, bf16[72,320]{1,0:T(8,128)(2,1)S(1)}, bf16[72,320]{1,0:T(8,128)(2,1)S(1)}, bf16[72,320]{1,0:T(8,128)(2,1)S(1)}) custom-call(bf16[72,320]{1,0:T(8,128)(2,1)S(1)} %collective-permute-done.9.refs_0_, bf16[72,320]{1,0:T(8,128)(2,1)S(1)} %collective-permute-done.10.refs_1_, ...), custom_call_target="tpu_custom_call" | custom-call | flops 800000000 | bytes 5599360 | tf_op jit(solution)/shard_map/pallas_call | solution.py:229
  76.4 1.9 %collective-permute-start.13 = (bf16[72,320]{1,0:T(8,128)(2,1)S(1)}, bf16[72,320]{1,0:T(8,128)(2,1)S(1)}, u32[]{:S(2)}, u32[]{:S(2)}) collective-permute-start(bf16[72,320]{1,0:T(8,128)(2,1)S(1)} %get-tuple-element.33), channel_id=1, source_target_pairs={{1,35},{3,37},{5,39},{7,41},{9,43},{11,45},{13,47},{15,49},{17,51}... | collective-permute-start | bytes 138248 | tf_op jit(solution)/shard_map/ppermute | solution.py:257
  78.3 0.0 collective-permute-done.4.refs_0_
  78.4 2.0 %collective-permute-start.14 = (bf16[72,320]{1,0:T(8,128)(2,1)S(1)}, bf16[72,320]{1,0:T(8,128)(2,1)S(1)}, u32[]{:S(2)}, u32[]{:S(2)}) collective-permute-start(bf16[72,320]{1,0:T(8,128)(2,1)S(1)} %get-tuple-element.34), channel_id=1, source_target_pairs={{1,3},{3,5},{5,7},{7,9},{9,11},{11,13},{13,15},{15,17},{17,19},{19... | collective-permute-start | bytes 138248 | tf_op jit(solution)/shard_map/ppermute | solution.py:257
  80.4 0.0 collective-permute-done.5.refs_1_
  80.4 1.9 %collective-permute-start.15 = (bf16[72,320]{1,0:T(8,128)(2,1)S(1)}, bf16[72,320]{1,0:T(8,128)(2,1)S(1)}, u32[]{:S(2)}, u32[]{:S(2)}) collective-permute-start(bf16[72,320]{1,0:T(8,128)(2,1)S(1)} %get-tuple-element.35), channel_id=1, source_target_pairs={{1,33},{3,35},{5,37},{7,39},{9,41},{11,43},{13,45},{15,47},{17,49}... | collective-permute-start | bytes 138248 | tf_op jit(solution)/shard_map/ppermute | solution.py:257
  82.3 0.0 collective-permute-done.6.refs_2_
  82.3 0.0 collective-permute-done.7.refs_3_
  82.3 2.6 %collective-permute-done.13.refs_4_ = bf16[72,320]{1,0:T(8,128)(2,1)S(1)} collective-permute-done((bf16[72,320]{1,0:T(8,128)(2,1)S(1)}, bf16[72,320]{1,0:T(8,128)(2,1)S(1)}, u32[]{:S(2)}, u32[]{:S(2)}) %collective-permute-start.13) | collective-permute-done | bytes 46112 | tf_op jit(solution)/shard_map/ppermute | solution.py:257
  84.9 0.0 collective-permute-done.14.refs_5_
  84.9 5.6 %collective-permute-done.15.refs_6_ = bf16[72,320]{1,0:T(8,128)(2,1)S(1)} collective-permute-done((bf16[72,320]{1,0:T(8,128)(2,1)S(1)}, bf16[72,320]{1,0:T(8,128)(2,1)S(1)}, u32[]{:S(2)}, u32[]{:S(2)}) %collective-permute-start.15) | collective-permute-done | bytes 46112 | tf_op jit(solution)/shard_map/ppermute | solution.py:257
  90.5 0.0 copy-done.5
  90.5 1.0 %shard_map.141 = bf16[1,6,12,4,320]{4,3,2,1,0:T(4,128)(2,1)} custom-call(bf16[72,320]{1,0:T(8,128)(2,1)S(1)} %collective-permute-done.4.refs_0_, bf16[72,320]{1,0:T(8,128)(2,1)S(1)} %collective-permute-done.5.refs_1_, bf16[72,320]{1,0:T(8,128)(2,1)S(1)} %collective-permute-done.6.refs_2_, bf16[72,320]{1,0:T(8,128)(2,1)S(1)} %collective-permute-done.7.refs_3_, ...), custom_call_target="tpu_custom_call" | custom-call | flops 1000000 | bytes 534528 | tf_op jit(solution)/shard_map/pallas_call | solution.py:229
  (2 shorter events, 0.0 us)
Async XLA Ops:
  0.0 16.6 %collective-permute-start.8 = (bf16[1,6,12,4,320]{4,3,2,1,0:T(4,128)(2,1)}, bf16[1,6,12,4,320]{4,3,2,1,0:T(4,128)(2,1)S(1)}, u32[]{:S(2)}, u32[]{:S(2)}) collective-permute-start(bf16[1,6,12,4,320]{4,3,2,1,0:T(4,128)(2,1)} %bitcast.2), channel_id=1, source_target_pairs={{1,0},{3,2},{5,4},{7,6},{9,8},{11,10},{13,12},{15,14},{17,16},{19,... | collective-permute-start | bytes 552968 | tf_op jit(solution)/shard_map/ppermute | solution.py:257
  3.7 7.7 %copy-start = (bf16[1,320,1280]{2,1,0:T(8,128)(2,1)S(1)}, bf16[1,320,1280]{2,1,0:T(8,128)(2,1)}, u32[]{:S(2)}) copy-start(bf16[1,320,1280]{2,1,0:T(8,128)(2,1)} %refs_9_.3) | copy-start | bytes 2457604
  3.7 7.7 %copy-start.1 = (bf16[1,320,960]{2,1,0:T(8,128)(2,1)S(1)}, bf16[1,320,960]{2,1,0:T(8,128)(2,1)}, u32[]{:S(2)}) copy-start(bf16[1,320,960]{2,1,0:T(8,128)(2,1)} %refs_6_.7) | copy-start | bytes 1843204
  3.7 7.7 %copy-start.2 = (bf16[1,320,320]{2,1,0:T(8,128)(2,1)S(1)}, bf16[1,320,320]{2,1,0:T(8,128)(2,1)}, u32[]{:S(2)}) copy-start(bf16[1,320,320]{2,1,0:T(8,128)(2,1)} %refs_8_.8) | copy-start | bytes 614404
  3.7 7.6 %copy-start.7 = (bf16[1,1280]{1,0:T(2,128)(2,1)S(1)}, bf16[1,1280]{1,0:T(2,128)(2,1)}, u32[]{:S(2)}) copy-start(bf16[1,1280]{1,0:T(2,128)(2,1)} %refs_10_.3) | copy-start | bytes 7684
  3.7 7.6 %copy-start.8 = (bf16[1,960]{1,0:T(2,128)(2,1)S(1)}, bf16[1,960]{1,0:T(2,128)(2,1)}, u32[]{:S(2)}) copy-start(bf16[1,960]{1,0:T(2,128)(2,1)} %refs_7_.5) | copy-start | bytes 5764
  3.7 7.6 %copy-start.9 = (bf16[1,2,320]{2,1,0:T(2,128)(2,1)S(1)}, bf16[1,2,320]{2,1,0:T(2,128)(2,1)}, u32[]{:S(2)}) copy-start(bf16[1,2,320]{2,1,0:T(2,128)(2,1)} %refs_4_.7) | copy-start | bytes 3844
  3.7 7.6 %copy-start.10 = (bf16[1,2,320]{2,1,0:T(2,128)(2,1)S(1)}, bf16[1,2,320]{2,1,0:T(2,128)(2,1)}, u32[]{:S(2)}) copy-start(bf16[1,2,320]{2,1,0:T(2,128)(2,1)} %refs_5_.7) | copy-start | bytes 3844
  3.7 7.6 %copy-start.11 = (bf16[1,2,320]{2,1,0:T(2,128)(2,1)S(1)}, bf16[1,2,320]{2,1,0:T(2,128)(2,1)}, u32[]{:S(2)}) copy-start(bf16[1,2,320]{2,1,0:T(2,128)(2,1)} %refs_12_.3) | copy-start | bytes 3844
  5.4 1.5 %copy-start.3 = (bf16[276,3072]{1,0:T(8,128)(2,1)S(1)}, bf16[276,3072]{1,0:T(8,128)(2,1)}, u32[]{:S(2)}) copy-start(bf16[276,3072]{1,0:T(8,128)(2,1)} %constant.6.clone.spread_ref) | copy-start | bytes 5087236
  6.9 4.5 %copy-start.4 = (bf16[288,288]{1,0:T(8,128)(2,1)S(1)}, bf16[288,288]{1,0:T(8,128)(2,1)}, u32[]{:S(2)}) copy-start(bf16[288,288]{1,0:T(8,128)(2,1)} %constant.7.clone.arrange_ref) | copy-start | bytes 497668
  6.9 4.5 %copy-start.6 = (bf16[1,4,6,12,320]{4,1,3,2,0:T(4,128)(2,1)S(1)}, bf16[1,4,6,12,320]{4,1,3,2,0:T(4,128)(2,1)}, u32[]{:S(2)}) copy-start(bf16[1,4,6,12,320]{4,1,3,2,0:T(4,128)(2,1)} %param.14) | copy-start | bytes 552964
  11.4 12.5 %collective-permute-start = (bf16[72,320]{1,0:T(8,128)(2,1)S(1)}, bf16[72,320]{1,0:T(8,128)(2,1)S(1)}, u32[]{:S(2)}, u32[]{:S(2)}) collective-permute-start(bf16[72,320]{1,0:T(8,128)(2,1)S(1)} %get-tuple-element.21), channel_id=1, source_target_pairs={{0,1},{2,3},{4,5},{6,7},{8,9},{10,11},{12,13},{14,15},{16,17},{18,... | collective-permute-start | bytes 138248 | tf_op jit(solution)/shard_map/ppermute | solution.py:257
  12.7 13.4 %collective-permute-start.1 = (bf16[72,320]{1,0:T(8,128)(2,1)S(1)}, bf16[72,320]{1,0:T(8,128)(2,1)S(1)}, u32[]{:S(2)}, u32[]{:S(2)}) collective-permute-start(bf16[72,320]{1,0:T(8,128)(2,1)S(1)} %get-tuple-element.22), channel_id=1, source_target_pairs={{0,737},{2,739},{4,741},{6,743},{8,745},{10,747},{12,749},{14,751}... | collective-permute-start | bytes 138248 | tf_op jit(solution)/shard_map/ppermute | solution.py:257
  14.0 13.4 %collective-permute-start.2 = (bf16[72,320]{1,0:T(8,128)(2,1)S(1)}, bf16[72,320]{1,0:T(8,128)(2,1)S(1)}, u32[]{:S(2)}, u32[]{:S(2)}) collective-permute-start(bf16[72,320]{1,0:T(8,128)(2,1)S(1)} %get-tuple-element.23), channel_id=1, source_target_pairs={{0,31},{2,1},{4,3},{6,5},{8,7},{10,9},{12,11},{14,13},{16,15},{18,... | collective-permute-start | bytes 138248 | tf_op jit(solution)/shard_map/ppermute | solution.py:257
  15.3 13.4 %collective-permute-start.3 = (bf16[72,320]{1,0:T(8,128)(2,1)S(1)}, bf16[72,320]{1,0:T(8,128)(2,1)S(1)}, u32[]{:S(2)}, u32[]{:S(2)}) collective-permute-start(bf16[72,320]{1,0:T(8,128)(2,1)S(1)} %get-tuple-element.24), channel_id=1, source_target_pairs={{0,767},{2,737},{4,739},{6,741},{8,743},{10,745},{12,747},{14,749}... | collective-permute-start | bytes 138248 | tf_op jit(solution)/shard_map/ppermute | solution.py:257
  16.7 23.8 %collective-permute-start.9 = (bf16[72,320]{1,0:T(8,128)(2,1)S(1)}, bf16[72,320]{1,0:T(8,128)(2,1)S(1)}, u32[]{:S(2)}, u32[]{:S(2)}) collective-permute-start(bf16[72,320]{1,0:T(8,128)(2,1)S(1)} %get-tuple-element.29), channel_id=1, source_target_pairs={{0,1},{2,3},{4,5},{6,7},{8,9},{10,11},{12,13},{14,15},{16,17},{18,... | collective-permute-start | bytes 138248 | tf_op jit(solution)/shard_map/ppermute | solution.py:257
  24.0 46.6 %collective-permute-start.10 = (bf16[72,320]{1,0:T(8,128)(2,1)S(1)}, bf16[72,320]{1,0:T(8,128)(2,1)S(1)}, u32[]{:S(2)}, u32[]{:S(2)}) collective-permute-start(bf16[72,320]{1,0:T(8,128)(2,1)S(1)} %get-tuple-element.30), channel_id=1, source_target_pairs={{0,737},{2,739},{4,741},{6,743},{8,745},{10,747},{12,749},{14,751}... | collective-permute-start | bytes 138248 | tf_op jit(solution)/shard_map/ppermute | solution.py:257
  26.1 45.7 %collective-permute-start.11 = (bf16[72,320]{1,0:T(8,128)(2,1)S(1)}, bf16[72,320]{1,0:T(8,128)(2,1)S(1)}, u32[]{:S(2)}, u32[]{:S(2)}) collective-permute-start(bf16[72,320]{1,0:T(8,128)(2,1)S(1)} %get-tuple-element.31), channel_id=1, source_target_pairs={{0,31},{2,1},{4,3},{6,5},{8,7},{10,9},{12,11},{14,13},{16,15},{18,... | collective-permute-start | bytes 138248 | tf_op jit(solution)/shard_map/ppermute | solution.py:257
  27.4 45.7 %collective-permute-start.12 = (bf16[72,320]{1,0:T(8,128)(2,1)S(1)}, bf16[72,320]{1,0:T(8,128)(2,1)S(1)}, u32[]{:S(2)}, u32[]{:S(2)}) collective-permute-start(bf16[72,320]{1,0:T(8,128)(2,1)S(1)} %get-tuple-element.32), channel_id=1, source_target_pairs={{0,767},{2,737},{4,739},{6,741},{8,743},{10,745},{12,747},{14,749}... | collective-permute-start | bytes 138248 | tf_op jit(solution)/shard_map/ppermute | solution.py:257
  32.2 46.2 %collective-permute-start.4 = (bf16[72,320]{1,0:T(8,128)(2,1)S(1)}, bf16[72,320]{1,0:T(8,128)(2,1)S(1)}, u32[]{:S(2)}, u32[]{:S(2)}) collective-permute-start(bf16[72,320]{1,0:T(8,128)(2,1)S(1)} %get-tuple-element.25), channel_id=1, source_target_pairs={{1,34},{3,36},{5,38},{7,40},{9,42},{11,44},{13,46},{15,48},{17,50}... | collective-permute-start | bytes 138248 | tf_op jit(solution)/shard_map/ppermute | solution.py:257
  40.5 50.0 %copy-start.5 = (bf16[288,288]{1,0:T(8,128)(2,1)S(1)}, bf16[288,288]{1,0:T(8,128)(2,1)}, u32[]{:S(2)}) copy-start(bf16[288,288]{1,0:T(8,128)(2,1)} %constant.8.clone.refs_8_) | copy-start | bytes 497668
  40.5 39.9 %collective-permute-start.5 = (bf16[72,320]{1,0:T(8,128)(2,1)S(1)}, bf16[72,320]{1,0:T(8,128)(2,1)S(1)}, u32[]{:S(2)}, u32[]{:S(2)}) collective-permute-start(bf16[72,320]{1,0:T(8,128)(2,1)S(1)} %get-tuple-element.26), channel_id=1, source_target_pairs={{1,2},{3,4},{5,6},{7,8},{9,10},{11,12},{13,14},{15,16},{17,18},{19... | collective-permute-start | bytes 138248 | tf_op jit(solution)/shard_map/ppermute | solution.py:257
  70.5 11.8 %collective-permute-start.6 = (bf16[72,320]{1,0:T(8,128)(2,1)S(1)}, bf16[72,320]{1,0:T(8,128)(2,1)S(1)}, u32[]{:S(2)}, u32[]{:S(2)}) collective-permute-start(bf16[72,320]{1,0:T(8,128)(2,1)S(1)} %get-tuple-element.27), channel_id=1, source_target_pairs={{1,32},{3,34},{5,36},{7,38},{9,40},{11,42},{13,44},{15,46},{17,48}... | collective-permute-start | bytes 138248 | tf_op jit(solution)/shard_map/ppermute | solution.py:257
  71.8 10.5 %collective-permute-start.7 = (bf16[72,320]{1,0:T(8,128)(2,1)S(1)}, bf16[72,320]{1,0:T(8,128)(2,1)S(1)}, u32[]{:S(2)}, u32[]{:S(2)}) collective-permute-start(bf16[72,320]{1,0:T(8,128)(2,1)S(1)} %get-tuple-element.28), channel_id=1, source_target_pairs={{1,0},{3,2},{5,4},{7,6},{9,8},{11,10},{13,12},{15,14},{17,16},{19,... | collective-permute-start | bytes 138248 | tf_op jit(solution)/shard_map/ppermute | solution.py:257
  76.4 8.5 %collective-permute-start.13 = (bf16[72,320]{1,0:T(8,128)(2,1)S(1)}, bf16[72,320]{1,0:T(8,128)(2,1)S(1)}, u32[]{:S(2)}, u32[]{:S(2)}) collective-permute-start(bf16[72,320]{1,0:T(8,128)(2,1)S(1)} %get-tuple-element.33), channel_id=1, source_target_pairs={{1,35},{3,37},{5,39},{7,41},{9,43},{11,45},{13,47},{15,49},{17,51}... | collective-permute-start | bytes 138248 | tf_op jit(solution)/shard_map/ppermute | solution.py:257
  78.4 6.5 %collective-permute-start.14 = (bf16[72,320]{1,0:T(8,128)(2,1)S(1)}, bf16[72,320]{1,0:T(8,128)(2,1)S(1)}, u32[]{:S(2)}, u32[]{:S(2)}) collective-permute-start(bf16[72,320]{1,0:T(8,128)(2,1)S(1)} %get-tuple-element.34), channel_id=1, source_target_pairs={{1,3},{3,5},{5,7},{7,9},{9,11},{11,13},{13,15},{15,17},{17,19},{19... | collective-permute-start | bytes 138248 | tf_op jit(solution)/shard_map/ppermute | solution.py:257
  80.4 10.1 %collective-permute-start.15 = (bf16[72,320]{1,0:T(8,128)(2,1)S(1)}, bf16[72,320]{1,0:T(8,128)(2,1)S(1)}, u32[]{:S(2)}, u32[]{:S(2)}) collective-permute-start(bf16[72,320]{1,0:T(8,128)(2,1)S(1)} %get-tuple-element.35), channel_id=1, source_target_pairs={{1,33},{3,35},{5,37},{7,39},{9,41},{11,43},{13,45},{15,47},{17,49}... | collective-permute-start | bytes 138248 | tf_op jit(solution)/shard_map/ppermute | solution.py:257

commit v2 on v1

--- a/solution.py
+++ b/solution.py
@@ -59,11 +59,9 @@
     return arrange.astype(jnp.bfloat16)
 
 
-def prepare_kernel(table_ref, spread_ref, addend_ref, wide_ref):
-    section = lax.axis_index("section")
-    last_lat = lax.axis_index("lat") == lax.axis_size("lat") - 1
-    wide_ref[0:HEADS, :] = table_ref[0, 0, 0].astype(jnp.float32)
-    wide_ref[16 : 16 + HEADS, :] = table_ref[0, 1, 0].astype(jnp.float32)
+def lay_out_bias(table_ref, spread_ref, addend_ref, wide_ref):
+    for head in range(HEADS):
+        wide_ref[2 * head : 2 * head + 2, :] = table_ref[0, 0, head].astype(jnp.float32)
     for lev in range(WLEV):
         for lat in range(WLAT):
             parts = []
@@ -75,15 +73,31 @@
             dense = jnp.dot(rows, spread_ref[...], preferred_element_type=jnp.float32)
             for lon in range(WLON):
                 row = token_row(lev, lat, lon)
-                for window in range(2):
-                    for tile in range(2):
-                        lanes = lon * 256 + tile * 128
-                        addend_ref[
-                            tile, pl.ds(window * HEADS * WIN + row, HEADS, stride=WIN), :
-                        ] = dense[window * 16 : window * 16 + HEADS, lanes : lanes + 128]
-
-    @pl.when(section == 1)
-    def mask():
+                for tile in range(2):
+                    lanes = lon * 256 + tile * 128
+                    addend_ref[tile, pl.ds(row, 2 * HEADS, stride=WIN), :] = dense[
+                        : 2 * HEADS, lanes : lanes + 128
+                    ]
+
+
+def fetch(sources, targets, sems):
+    copies = [
+        pltpu.make_async_copy(source, target, sems.at[at])
+        for at, (source, target) in enumerate(zip(sources, targets, strict=True))
+    ]
+    for copy in copies:
+        copy.start()
+    return copies
+
+
+def prepare_kernel(table_hbm, spread_hbm, after_ref, addend_ref, table_ref, spread_ref, wide_ref, sems):
+    last_lat = lax.axis_index("lat") == lax.axis_size("lat") - 1
+
+    @pl.when(lax.axis_index("section") == 1)
+    def work():
+        for copy in fetch((table_hbm, spread_hbm), (table_ref, spread_ref), sems):
+            copy.wait()
+        lay_out_bias(table_ref, spread_ref, addend_ref, wide_ref)
         for tile in range(2):
             query = lax.broadcasted_iota(jnp.int32, (WIN, 128), 0)
             key = lax.broadcasted_iota(jnp.int32, (WIN, 128), 1) + tile * 128
@@ -92,7 +106,7 @@
             for window in range(2):
                 barred = jnp.logical_or(lat_differs, lev_differs) if window else lat_differs
                 for head in range(HEADS):
-                    at = (window * HEADS + head) * WIN
+                    at = (2 * head + window) * WIN
                     addend_ref[tile, at : at + WIN, :] = jnp.where(
                         barred, jnp.float32(-1e30), addend_ref[tile, at : at + WIN, :]
                     )
@@ -106,8 +120,10 @@
     )
 
 
-def run_block(field_ref, params, addend_ref, packed_ref, attended_ref):
+def run_block(field_ref, params, copies, addend_ref, packed_ref, attended_ref):
     ln_g, ln_s, qkv_w, qkv_b, proj_w, fc1_w, fc1_b, fc2_w, out_b = params
+    for copy in copies[:4]:
+        copy.wait()
     normed = layer_norm(field_ref[...], ln_g[0, 0:1], ln_s[0, 0:1]).astype(jnp.bfloat16)
     packed = jnp.dot(normed, qkv_w[0], preferred_element_type=jnp.float32)
     packed = (packed + qkv_b[...].astype(jnp.float32)).astype(jnp.bfloat16)
@@ -132,7 +148,7 @@
                 scores = lax.dot_general(
                     own, keys, (((1,), (1,)), ((), ())), preferred_element_type=jnp.float32
                 ) * HD ** (-0.5)
-                at = (window * HEADS + group * 4 + head) * WIN
+                at = (2 * (group * 4 + head) + window) * WIN
                 scores = scores + jnp.concatenate(
                     [addend_ref[0, at : at + WIN, :], addend_ref[1, at : at + WIN, 0 : WIN - 128]],
                     axis=1,
@@ -144,6 +160,8 @@
                 mixed = mixed[:, :width] / mixed[:, width:]
                 gathered = jnp.where(lane_head == head, mixed, gathered)
             attended_ref[first : first + WIN, lanes : lanes + width] = gathered.astype(jnp.bfloat16)
+    for copy in copies[4:]:
+        copy.wait()
     mid = (
         field_ref[...]
         + jnp.dot(attended_ref[...], proj_w[0], preferred_element_type=jnp.float32)
@@ -157,27 +175,49 @@
     )
     field_ref[...] = (
         mid
-        + jnp.dot(hidden, fc2_w[0], preferred_element_type=jnp.float32)
+        + lax.dot_general(
+            hidden, fc2_w[0], (((1,), (1,)), ((), ())), preferred_element_type=jnp.float32
+        )
         + out_b[0, 1:2].astype(jnp.float32)
     )
 
 
-def first_kernel(patch_ref, arrange_ref, *refs):
-    params, (addend_ref,), outs = refs[:9], refs[9:10], refs[10:14]
-    field_ref, packed_ref, attended_ref, quarter_ref = refs[14:]
+def first_kernel(prepares, patch_ref, arrange_hbm, *refs):
+    hbm, refs = refs[:9], refs[9:]
+    if prepares:
+        table_hbm, spread_hbm = refs[:2]
+        outs, addend_ref, refs = refs[2:6], refs[6], refs[7:]
+    else:
+        addend_ref, outs, refs = refs[0], refs[1:5], refs[5:]
+    field_ref, packed_ref, attended_ref, quarter_ref, arrange_ref = refs[:5]
+    params, sems = refs[5:14], refs[14]
 
     @pl.when(lax.axis_index("section") == 0)
     def work():
+        if prepares:
+            own_ref, table_ref, spread_ref, wide_ref, more_sems = refs[15:]
+            early = fetch(
+                (table_hbm, spread_hbm, patch_ref), (table_ref, spread_ref, own_ref), more_sems
+            )
+        else:
+            own_ref = patch_ref
+        (arranging,) = fetch((arrange_hbm,), (arrange_ref,), sems.at[pl.ds(9, 1)])
+        copies = fetch(hbm, params, sems)
+        if prepares:
+            for copy in early:
+                copy.wait()
+            lay_out_bias(table_ref, spread_ref, addend_ref, wide_ref)
         for lat in range(WLAT):
             for lon in range(WLON):
                 at = (lat * WLON + lon) * 4
-                field_ref[at : at + 4, :] = patch_ref[0, lat, lon].astype(jnp.float32)
+                field_ref[at : at + 4, :] = own_ref[0, lat, lon].astype(jnp.float32)
+        arranging.wait()
         field_ref[...] = jnp.dot(
             arrange_ref[...],
             field_ref[...].astype(jnp.bfloat16),
             preferred_element_type=jnp.float32,
         )
-        run_block(field_ref, params, addend_ref, packed_ref, attended_ref)
+        run_block(field_ref, params, copies, addend_ref, packed_ref, attended_ref)
         for quarter in range(4):
             for place in range(4):
                 lev = (place + 1) % 4
@@ -187,17 +227,19 @@
 
 
 def second_kernel(*refs):
-    quarters, params, (addend_ref,), outs = refs[:4], refs[4:13], refs[13:14], refs[14:18]
-    field_ref, packed_ref, attended_ref, quarter_ref = refs[18:]
+    quarters, hbm, (addend_ref,), outs = refs[:4], refs[4:13], refs[13:14], refs[14:18]
+    field_ref, packed_ref, attended_ref, quarter_ref = refs[18:22]
+    params, sems = refs[22:31], refs[31]
 
     @pl.when(lax.axis_index("section") == 1)
     def work():
+        copies = fetch(hbm, params, sems)
         for quarter in range(4):
             held = quarters[quarter][...].astype(jnp.float32)
             for window in range(2):
                 at = window * WIN + quarter * QUARTER
                 field_ref[at : at + QUARTER, :] = held[window * QUARTER : (window + 1) * QUARTER]
-        run_block(field_ref, params, addend_ref, packed_ref, attended_ref)
+        run_block(field_ref, params, copies, addend_ref, packed_ref, attended_ref)
         for quarter in range(4):
             for window in range(2):
                 at = window * WIN + quarter * QUARTER
@@ -223,17 +265,20 @@
     pl.when(section == 1)(lambda: place(refs[4:8]))
 
 
-def call(kernel, operands, outs, scratch, flops):
-    whole = pl.BlockSpec(memory_space=pltpu.VMEM)
-    moved = sum(op.size * op.dtype.itemsize for op in operands)
+def call(kernel, operands, places, outs, scratch, flops):
+    spaces = {"h": pltpu.HBM, "v": pltpu.VMEM}
+    operands = [
+        pltpu.with_memory_space_constraint(operand, pltpu.HBM) if place == "h" else operand
+        for operand, place in zip(operands, places, strict=True)
+    ]
     return pl.pallas_call(
         kernel,
         out_shape=outs,
-        in_specs=[whole] * len(operands),
-        out_specs=jax.tree.map(lambda unused: whole, outs),
+        in_specs=[pl.BlockSpec(memory_space=spaces[place]) for place in places],
+        out_specs=jax.tree.map(lambda unused: pl.BlockSpec(memory_space=pltpu.VMEM), outs),
         scratch_shapes=scratch,
         compiler_params=pltpu.CompilerParams(vmem_limit_bytes=VMEM_LIMIT),
-        cost_estimate=pl.CostEstimate(flops=flops, bytes_accessed=moved, transcendentals=0),
+        cost_estimate=pl.CostEstimate(flops=flops, bytes_accessed=4_000_000, transcendentals=0),
     )(*operands)
 
 
@@ -247,18 +292,35 @@
 BLOCK_FLOPS = 800_000_000
 
 
-def send(block, source, target, lat_step, lon_step):
+def held(array):
+    return pltpu.VMEM(array.shape, array.dtype)
+
+
+def mirrored(lon):
+    lons = lax.axis_size("lon")
+    across = 4 if lons % 4 == 0 else 1
+    return (lons // across - 1 - lon // across) * across + lon % across
+
+
+def straight(lon):
+    return lon
+
+
+def send(block, sections, steps, source_at, target_at):
     lons, lats = lax.axis_size("lon"), lax.axis_size("lat")
     route = []
     for lon in range(lons):
         for lat in range(lats):
-            there = ((lon + lon_step) % lons) * lats + (lat + lat_step) % lats
-            route.append(((lon * lats + lat) * 2 + source, there * 2 + target))
+            here = source_at(lon) * lats + lat
+            there = target_at((lon + steps[1]) % lons) * lats + (lat + steps[0]) % lats
+            route.append((here * 2 + sections[0], there * 2 + sections[1]))
     return lax.ppermute(block, AXES, route)
 
 
-def to_shifted(quarters):
-    moved = [send(quarters[q], 0, 1, q // 2 - 1, q % 2 - 1) for q in range(4)]
+def to_shifted(quarters, source_at, target_at):
+    moved = [
+        send(quarters[q], (0, 1), (q // 2 - 1, q % 2 - 1), source_at, target_at) for q in range(4)
+    ]
     return [moved[3 - q] for q in range(4)]
 
 
@@ -286,31 +348,76 @@
         fc2_weight,
         out_bias,
     )
+    params = (*params[:7], fc2_weight.transpose(0, 2, 1), out_bias)
     patch = inputs.transpose(0, 2, 3, 1, 4)
-    other = send(patch, 1, 0, 0, 0)
-    addend = call(
+    table = bias_table.transpose(0, 2, 3, 1, 4)
+    other = send(patch, (1, 0), (0, 0), straight, mirrored)
+    arrange = jnp.asarray(arrange_matrix())
+    spread = jnp.asarray(spread_matrix())
+    addend_shape = jax.ShapeDtypeStruct((2, 2 * HEADS * WIN, 128), jnp.float32)
+    wide = pltpu.VMEM((24, table.shape[-1]), jnp.float32)
+    first_scratch = [
+        *BLOCK_SCRATCH,
+        held(arrange),
+        *map(held, params),
+        pltpu.SemaphoreType.DMA((10,)),
+    ]
+    second_scratch = [*BLOCK_SCRATCH, *map(held, params), pltpu.SemaphoreType.DMA((9,))]
+    *own_first, addend_one = call(
+        functools.partial(first_kernel, True),
+        (patch, arrange, *params, table, spread),
+        "h" * 13,
+        [*QUARTERS, addend_shape],
+        [
+            *first_scratch,
+            held(patch),
+            held(table),
+            held(spread),
+            wide,
+            pltpu.SemaphoreType.DMA((3,)),
+        ],
+        BLOCK_FLOPS,
+    )
+    own_shifted = to_shifted(own_first, straight, mirrored)
+    addend_two = call(
         prepare_kernel,
-        (bias_table, jnp.asarray(spread_matrix())),
-        jax.ShapeDtypeStruct((2, 2 * HEADS * WIN, 128), jnp.float32),
-        [pltpu.VMEM((32, bias_table.shape[-1]), jnp.float32)],
+        (table, spread, own_first[0]),
+        "hhv",
+        addend_shape,
+        [held(table), held(spread), wide, pltpu.SemaphoreType.DMA((2,))],
         200_000_000,
     )
-    arrange = jnp.asarray(arrange_matrix())
-    block_one = functools.partial(
-        call, first_kernel, outs=QUARTERS, scratch=BLOCK_SCRATCH, flops=BLOCK_FLOPS
-    )
+    other_first = call(
+        functools.partial(first_kernel, False),
+        (other, arrange, *params, addend_one),
+        "vh" + "h" * 9 + "v",
+        QUARTERS,
+        first_scratch,
+        BLOCK_FLOPS,
+    )
+    other_shifted = to_shifted(other_first, mirrored, straight)
     block_two = functools.partial(
-        call, second_kernel, outs=QUARTERS, scratch=BLOCK_SCRATCH, flops=BLOCK_FLOPS
-    )
-    own_shifted = to_shifted(block_one((patch, arrange, *params, addend)))
-    other_shifted = to_shifted(block_one((other, arrange, *params, addend)))
-    own_done = block_two((*own_shifted, *params, addend))
-    own_back = [send(own_done[3 - q], 1, 0, 1 - q // 2, 1 - q % 2) for q in range(4)]
-    other_done = block_two((*other_shifted, *params, addend))
-    other_back = [send(other_done[3 - q], 1, 1, 1 - q // 2, 1 - q % 2) for q in range(3)]
+        call,
+        second_kernel,
+        places="vvvv" + "h" * 9 + "v",
+        outs=QUARTERS,
+        scratch=second_scratch,
+        flops=BLOCK_FLOPS,
+    )
+    own_done = block_two((*own_shifted, *params, addend_two))
+    own_back = [
+        send(own_done[3 - q], (1, 0), (1 - q // 2, 1 - q % 2), mirrored, straight)
+        for q in range(4)
+    ]
+    other_done = block_two((*other_shifted, *params, addend_two))
+    other_back = [
+        send(other_done[3 - q], (1, 1), (1 - q // 2, 1 - q % 2), straight, straight)
+        for q in range(3)
+    ]
     placed = call(
         place_kernel,
         (*own_back, *other_back, other_done[0], jnp.asarray(place_matrix())),
+        "v" * 9,
         jax.ShapeDtypeStruct(patch.shape, patch.dtype),
         [pltpu.VMEM((2 * WIN, C), jnp.float32)],
         1_000_000,

time: 91.9 us -> 74.1 us (0.81)
  the two profiles are of different devices: /device:TPU:728 before, /device:TPU:401 now
where the time goes in v2:
time: 74.1 us; the launch traced here: 73.7 us
  starting transfers between devices  28.5 us (38%)
  waiting for transfers between devices  28.5 us (38%)
  Pallas kernels  16.4 us (22%)
    ppermute x16, waiting for transfers between devices, send(): return lax.ppermute(block, AXES, route)  28.5 us
    ppermute x16, starting transfers between devices, send(): return lax.ppermute(block, AXES, route)  28.5 us
    pallas_call x6, Pallas kernels, call(): pl.pallas_call(kernel, out_shape=outs, in_specs=[pl.BlockSpec(memory_spac...  16.4 us
  transfers between devices with their start and end apart: 16, of which 6 were waited for; matrix products, arithmetic and copies ran while one was open for 0% of the time, Pallas kernels for 21%

profile of v2, /device:TPU:401, one launch (start us, length us, event | category | flops | bytes accessed | tf_op | source)
XLA Modules:
  0.0 73.7 jit_solution(9795741537391981970)
XLA Ops:
  0.0 1.3 %collective-permute-start.8 = (bf16[1,6,12,4,320]{4,3,2,1,0:T(4,128)(2,1)}, bf16[1,6,12,4,320]{4,3,2,1,0:T(4,128)(2,1)S(1)}, u32[]{:S(2)}, u32[]{:S(2)}) collective-permute-start(bf16[1,6,12,4,320]{4,3,2,1,0:T(4,128)(2,1)} %bitcast.10), channel_id=1, source_target_pairs={{1,640},{3,642},{5,644},{7,646},{9,648},{11,650},{13,652},{15,654}... | collective-permute-start | bytes 552968 | tf_op jit(solution)/shard_map/ppermute | solution.py:317
  1.3 0.1 shard_map.136
  1.4 1.3 %collective-permute-start = (bf16[72,320]{1,0:T(8,128)(2,1)S(1)}, bf16[72,320]{1,0:T(8,128)(2,1)S(1)}, u32[]{:S(2)}, u32[]{:S(2)}) collective-permute-start(bf16[72,320]{1,0:T(8,128)(2,1)S(1)} %get-tuple-element.22), channel_id=1, source_target_pairs={{0,641},{2,643},{4,645},{6,647},{8,649},{10,651},{12,653},{14,655}... | collective-permute-start | bytes 138248 | tf_op jit(solution)/shard_map/ppermute | solution.py:317
  2.7 1.3 %collective-permute-start.1 = (bf16[72,320]{1,0:T(8,128)(2,1)S(1)}, bf16[72,320]{1,0:T(8,128)(2,1)S(1)}, u32[]{:S(2)}, u32[]{:S(2)}) collective-permute-start(bf16[72,320]{1,0:T(8,128)(2,1)S(1)} %get-tuple-element.23), channel_id=1, source_target_pairs={{0,97},{2,99},{4,101},{6,103},{8,105},{10,107},{12,109},{14,111},{... | collective-permute-start | bytes 138248 | tf_op jit(solution)/shard_map/ppermute | solution.py:317
  4.0 1.3 %collective-permute-start.2 = (bf16[72,320]{1,0:T(8,128)(2,1)S(1)}, bf16[72,320]{1,0:T(8,128)(2,1)S(1)}, u32[]{:S(2)}, u32[]{:S(2)}) collective-permute-start(bf16[72,320]{1,0:T(8,128)(2,1)S(1)} %get-tuple-element.24), channel_id=1, source_target_pairs={{0,671},{2,641},{4,643},{6,645},{8,647},{10,649},{12,651},{14,653}... | collective-permute-start | bytes 138248 | tf_op jit(solution)/shard_map/ppermute | solution.py:317
  5.3 1.3 %collective-permute-start.3 = (bf16[72,320]{1,0:T(8,128)(2,1)S(1)}, bf16[72,320]{1,0:T(8,128)(2,1)S(1)}, u32[]{:S(2)}, u32[]{:S(2)}) collective-permute-start(bf16[72,320]{1,0:T(8,128)(2,1)S(1)} %get-tuple-element.25.after_ref), channel_id=1, source_target_pairs={{0,127},{2,97},{4,99},{6,101},{8,103},{10,105},{12,107},{14,109},{... | collective-permute-start | bytes 138248 | tf_op jit(solution)/shard_map/ppermute | solution.py:317
  6.6 5.9 %shard_map.137.refs_13_ = f32[2,2880,128]{2,1,0:T(8,128)S(1)} custom-call(bf16[1,1,10,2,3312]{4,3,2,1,0:T(2,128)(2,1)} %bitcast.9, bf16[276,3072]{1,0:T(8,128)(2,1)} %constant.7.clone.refs_10_.spread_hbm, bf16[72,320]{1,0:T(8,128)(2,1)S(1)} %get-tuple-element.25.after_ref), custom_call_target="tpu_custom_call" | custom-call | flops 200000000 | bytes 4000000 | tf_op jit(solution)/shard_map/pallas_call | solution.py:274
  12.5 2.6 %collective-permute-done.8.patch_ref = bf16[1,6,12,4,320]{4,3,2,1,0:T(4,128)(2,1)S(1)} collective-permute-done((bf16[1,6,12,4,320]{4,3,2,1,0:T(4,128)(2,1)}, bf16[1,6,12,4,320]{4,3,2,1,0:T(4,128)(2,1)S(1)}, u32[]{:S(2)}, u32[]{:S(2)}) %collective-permute-start.8) | collective-permute-done | bytes 184352 | tf_op jit(solution)/shard_map/ppermute | solution.py:317
  15.2 0.1 shard_map.139
  15.3 1.3 %collective-permute-start.9 = (bf16[72,320]{1,0:T(8,128)(2,1)S(1)}, bf16[72,320]{1,0:T(8,128)(2,1)S(1)}, u32[]{:S(2)}, u32[]{:S(2)}) collective-permute-start(bf16[72,320]{1,0:T(8,128)(2,1)S(1)} %get-tuple-element.31), channel_id=1, source_target_pairs={{640,1},{642,3},{644,5},{646,7},{648,9},{650,11},{652,13},{654,15}... | collective-permute-start | bytes 138248 | tf_op jit(solution)/shard_map/ppermute | solution.py:317
  16.6 6.2 %collective-permute-done.refs_0_ = bf16[72,320]{1,0:T(8,128)(2,1)S(1)} collective-permute-done((bf16[72,320]{1,0:T(8,128)(2,1)S(1)}, bf16[72,320]{1,0:T(8,128)(2,1)S(1)}, u32[]{:S(2)}, u32[]{:S(2)}) %collective-permute-start) | collective-permute-done | bytes 46112 | tf_op jit(solution)/shard_map/ppermute | solution.py:317
  22.8 1.3 %collective-permute-start.10 = (bf16[72,320]{1,0:T(8,128)(2,1)S(1)}, bf16[72,320]{1,0:T(8,128)(2,1)S(1)}, u32[]{:S(2)}, u32[]{:S(2)}) collective-permute-start(bf16[72,320]{1,0:T(8,128)(2,1)S(1)} %get-tuple-element.32), channel_id=1, source_target_pairs={{640,737},{642,739},{644,741},{646,743},{648,745},{650,747},{652,7... | collective-permute-start | bytes 138248 | tf_op jit(solution)/shard_map/ppermute | solution.py:317
  24.1 10.3 %collective-permute-done.1.refs_1_ = bf16[72,320]{1,0:T(8,128)(2,1)S(1)} collective-permute-done((bf16[72,320]{1,0:T(8,128)(2,1)S(1)}, bf16[72,320]{1,0:T(8,128)(2,1)S(1)}, u32[]{:S(2)}, u32[]{:S(2)}) %collective-permute-start.1) | collective-permute-done | bytes 46112 | tf_op jit(solution)/shard_map/ppermute | solution.py:317
  34.4 1.3 %collective-permute-start.11 = (bf16[72,320]{1,0:T(8,128)(2,1)S(1)}, bf16[72,320]{1,0:T(8,128)(2,1)S(1)}, u32[]{:S(2)}, u32[]{:S(2)}) collective-permute-start(bf16[72,320]{1,0:T(8,128)(2,1)S(1)} %get-tuple-element.33), channel_id=1, source_target_pairs={{640,31},{642,1},{644,3},{646,5},{648,7},{650,9},{652,11},{654,13}... | collective-permute-start | bytes 138248 | tf_op jit(solution)/shard_map/ppermute | solution.py:317
  35.7 0.0 collective-permute-done.2.refs_2_
  35.7 1.3 %collective-permute-start.12 = (bf16[72,320]{1,0:T(8,128)(2,1)S(1)}, bf16[72,320]{1,0:T(8,128)(2,1)S(1)}, u32[]{:S(2)}, u32[]{:S(2)}) collective-permute-start(bf16[72,320]{1,0:T(8,128)(2,1)S(1)} %get-tuple-element.34), channel_id=1, source_target_pairs={{640,767},{642,737},{644,739},{646,741},{648,743},{650,745},{652,7... | collective-permute-start | bytes 138248 | tf_op jit(solution)/shard_map/ppermute | solution.py:317
  37.0 0.6 collective-permute-done.3.refs_3_
  37.7 4.7 %shard_map.138 = (bf16[72,320]{1,0:T(8,128)(2,1)S(1)}, bf16[72,320]{1,0:T(8,128)(2,1)S(1)}, bf16[72,320]{1,0:T(8,128)(2,1)S(1)}, bf16[72,320]{1,0:T(8,128)(2,1)S(1)}) custom-call(bf16[72,320]{1,0:T(8,128)(2,1)S(1)} %collective-permute-done.refs_0_, bf16[72,320]{1,0:T(8,128)(2,1)S(1)} %collective-permute-done.1.refs_1_, ...), custom_call_target="tpu_custom_call" | custom-call | flops 800000000 | bytes 4000000 | tf_op jit(solution)/shard_map/pallas_call | solution.py:274
  42.3 0.0 copy-start
  42.3 1.4 %collective-permute-start.4 = (bf16[72,320]{1,0:T(8,128)(2,1)S(1)}, bf16[72,320]{1,0:T(8,128)(2,1)S(1)}, u32[]{:S(2)}, u32[]{:S(2)}) collective-permute-start(bf16[72,320]{1,0:T(8,128)(2,1)S(1)} %get-tuple-element.26), channel_id=1, source_target_pairs={{641,34},{643,36},{645,38},{647,40},{649,42},{651,44},{653,46},{65... | collective-permute-start | bytes 138248 | tf_op jit(solution)/shard_map/ppermute | solution.py:317
  43.8 0.0 collective-permute-done.9.refs_0_
  43.8 1.3 %collective-permute-start.5 = (bf16[72,320]{1,0:T(8,128)(2,1)S(1)}, bf16[72,320]{1,0:T(8,128)(2,1)S(1)}, u32[]{:S(2)}, u32[]{:S(2)}) collective-permute-start(bf16[72,320]{1,0:T(8,128)(2,1)S(1)} %get-tuple-element.27), channel_id=1, source_target_pairs={{641,2},{643,4},{645,6},{647,8},{649,10},{651,12},{653,14},{655,16... | collective-permute-start | bytes 138248 | tf_op jit(solution)/shard_map/ppermute | solution.py:317
  45.1 0.0 collective-permute-done.10.refs_1_
  45.1 1.3 %collective-permute-start.6 = (bf16[72,320]{1,0:T(8,128)(2,1)S(1)}, bf16[72,320]{1,0:T(8,128)(2,1)S(1)}, u32[]{:S(2)}, u32[]{:S(2)}) collective-permute-start(bf16[72,320]{1,0:T(8,128)(2,1)S(1)} %get-tuple-element.28), channel_id=1, source_target_pairs={{641,32},{643,34},{645,36},{647,38},{649,40},{651,42},{653,44},{65... | collective-permute-start | bytes 138248 | tf_op jit(solution)/shard_map/ppermute | solution.py:317
  46.4 0.0 collective-permute-done.11.refs_2_
  46.4 1.3 %collective-permute-start.7 = (bf16[72,320]{1,0:T(8,128)(2,1)S(1)}, bf16[72,320]{1,0:T(8,128)(2,1)S(1)}, u32[]{:S(2)}, u32[]{:S(2)}) collective-permute-start(bf16[72,320]{1,0:T(8,128)(2,1)S(1)} %get-tuple-element.29), channel_id=1, source_target_pairs={{641,0},{643,2},{645,4},{647,6},{649,8},{651,10},{653,12},{655,14}... | collective-permute-start | bytes 138248 | tf_op jit(solution)/shard_map/ppermute | solution.py:317
  47.7 0.0 collective-permute-done.12.refs_3_
  47.7 4.7 %shard_map.140 = (bf16[72,320]{1,0:T(8,128)(2,1)S(1)}, bf16[72,320]{1,0:T(8,128)(2,1)S(1)}, bf16[72,320]{1,0:T(8,128)(2,1)S(1)}, bf16[72,320]{1,0:T(8,128)(2,1)S(1)}) custom-call(bf16[72,320]{1,0:T(8,128)(2,1)S(1)} %collective-permute-done.9.refs_0_, bf16[72,320]{1,0:T(8,128)(2,1)S(1)} %collective-permute-done.10.refs_1_, ...), custom_call_target="tpu_custom_call" | custom-call | flops 800000000 | bytes 4000000 | tf_op jit(solution)/shard_map/pallas_call | solution.py:274
  52.4 3.9 %collective-permute-start.13 = (bf16[72,320]{1,0:T(8,128)(2,1)S(1)}, bf16[72,320]{1,0:T(8,128)(2,1)S(1)}, u32[]{:S(2)}, u32[]{:S(2)}) collective-permute-start(bf16[72,320]{1,0:T(8,128)(2,1)S(1)} %get-tuple-element.35), channel_id=1, source_target_pairs={{1,35},{3,37},{5,39},{7,41},{9,43},{11,45},{13,47},{15,49},{17,51}... | collective-permute-start | bytes 138248 | tf_op jit(solution)/shard_map/ppermute | solution.py:317
  56.3 0.0 collective-permute-done.4.refs_0_
  56.3 4.5 %collective-permute-start.14 = (bf16[72,320]{1,0:T(8,128)(2,1)S(1)}, bf16[72,320]{1,0:T(8,128)(2,1)S(1)}, u32[]{:S(2)}, u32[]{:S(2)}) collective-permute-start(bf16[72,320]{1,0:T(8,128)(2,1)S(1)} %get-tuple-element.36), channel_id=1, source_target_pairs={{1,3},{3,5},{5,7},{7,9},{9,11},{11,13},{13,15},{15,17},{17,19},{19... | collective-permute-start | bytes 138248 | tf_op jit(solution)/shard_map/ppermute | solution.py:317
  60.8 0.0 collective-permute-done.5.refs_1_
  60.8 3.1 %collective-permute-start.15 = (bf16[72,320]{1,0:T(8,128)(2,1)S(1)}, bf16[72,320]{1,0:T(8,128)(2,1)S(1)}, u32[]{:S(2)}, u32[]{:S(2)}) collective-permute-start(bf16[72,320]{1,0:T(8,128)(2,1)S(1)} %get-tuple-element.37), channel_id=1, source_target_pairs={{1,33},{3,35},{5,37},{7,39},{9,41},{11,43},{13,45},{15,47},{17,49}... | collective-permute-start | bytes 138248 | tf_op jit(solution)/shard_map/ppermute | solution.py:317
  64.0 0.0 collective-permute-done.6.refs_2_
  64.0 0.0 collective-permute-done.7.refs_3_
  64.0 1.4 %collective-permute-done.13.refs_4_ = bf16[72,320]{1,0:T(8,128)(2,1)S(1)} collective-permute-done((bf16[72,320]{1,0:T(8,128)(2,1)S(1)}, bf16[72,320]{1,0:T(8,128)(2,1)S(1)}, u32[]{:S(2)}, u32[]{:S(2)}) %collective-permute-start.13) | collective-permute-done | bytes 46112 | tf_op jit(solution)/shard_map/ppermute | solution.py:317
  65.4 0.0 collective-permute-done.14.refs_5_
  65.4 7.3 %collective-permute-done.15.refs_6_ = bf16[72,320]{1,0:T(8,128)(2,1)S(1)} collective-permute-done((bf16[72,320]{1,0:T(8,128)(2,1)S(1)}, bf16[72,320]{1,0:T(8,128)(2,1)S(1)}, u32[]{:S(2)}, u32[]{:S(2)}) %collective-permute-start.15) | collective-permute-done | bytes 46112 | tf_op jit(solution)/shard_map/ppermute | solution.py:317
  72.7 0.0 copy-done
  72.7 1.0 %shard_map.141 = bf16[1,6,12,4,320]{4,3,2,1,0:T(4,128)(2,1)} custom-call(bf16[72,320]{1,0:T(8,128)(2,1)S(1)} %collective-permute-done.4.refs_0_, bf16[72,320]{1,0:T(8,128)(2,1)S(1)} %collective-permute-done.5.refs_1_, bf16[72,320]{1,0:T(8,128)(2,1)S(1)} %collective-permute-done.6.refs_2_, bf16[72,320]{1,0:T(8,128)(2,1)S(1)} %collective-permute-done.7.refs_3_, ...), custom_call_target="tpu_custom_call" | custom-call | flops 1000000 | bytes 4000000 | tf_op jit(solution)/shard_map/pallas_call | solution.py:274
Async XLA Ops:
  0.0 15.2 %collective-permute-start.8 = (bf16[1,6,12,4,320]{4,3,2,1,0:T(4,128)(2,1)}, bf16[1,6,12,4,320]{4,3,2,1,0:T(4,128)(2,1)S(1)}, u32[]{:S(2)}, u32[]{:S(2)}) collective-permute-start(bf16[1,6,12,4,320]{4,3,2,1,0:T(4,128)(2,1)} %bitcast.10), channel_id=1, source_target_pairs={{1,640},{3,642},{5,644},{7,646},{9,648},{11,650},{13,652},{15,654}... | collective-permute-start | bytes 552968 | tf_op jit(solution)/shard_map/ppermute | solution.py:317
  1.4 21.4 %collective-permute-start = (bf16[72,320]{1,0:T(8,128)(2,1)S(1)}, bf16[72,320]{1,0:T(8,128)(2,1)S(1)}, u32[]{:S(2)}, u32[]{:S(2)}) collective-permute-start(bf16[72,320]{1,0:T(8,128)(2,1)S(1)} %get-tuple-element.22), channel_id=1, source_target_pairs={{0,641},{2,643},{4,645},{6,647},{8,649},{10,651},{12,653},{14,655}... | collective-permute-start | bytes 138248 | tf_op jit(solution)/shard_map/ppermute | solution.py:317
  2.7 31.7 %collective-permute-start.1 = (bf16[72,320]{1,0:T(8,128)(2,1)S(1)}, bf16[72,320]{1,0:T(8,128)(2,1)S(1)}, u32[]{:S(2)}, u32[]{:S(2)}) collective-permute-start(bf16[72,320]{1,0:T(8,128)(2,1)S(1)} %get-tuple-element.23), channel_id=1, source_target_pairs={{0,97},{2,99},{4,101},{6,103},{8,105},{10,107},{12,109},{14,111},{... | collective-permute-start | bytes 138248 | tf_op jit(solution)/shard_map/ppermute | solution.py:317
  4.0 31.7 %collective-permute-start.2 = (bf16[72,320]{1,0:T(8,128)(2,1)S(1)}, bf16[72,320]{1,0:T(8,128)(2,1)S(1)}, u32[]{:S(2)}, u32[]{:S(2)}) collective-permute-start(bf16[72,320]{1,0:T(8,128)(2,1)S(1)} %get-tuple-element.24), channel_id=1, source_target_pairs={{0,671},{2,641},{4,643},{6,645},{8,647},{10,649},{12,651},{14,653}... | collective-permute-start | bytes 138248 | tf_op jit(solution)/shard_map/ppermute | solution.py:317
  5.3 32.3 %collective-permute-start.3 = (bf16[72,320]{1,0:T(8,128)(2,1)S(1)}, bf16[72,320]{1,0:T(8,128)(2,1)S(1)}, u32[]{:S(2)}, u32[]{:S(2)}) collective-permute-start(bf16[72,320]{1,0:T(8,128)(2,1)S(1)} %get-tuple-element.25.after_ref), channel_id=1, source_target_pairs={{0,127},{2,97},{4,99},{6,101},{8,103},{10,105},{12,107},{14,109},{... | collective-permute-start | bytes 138248 | tf_op jit(solution)/shard_map/ppermute | solution.py:317
  15.3 28.5 %collective-permute-start.9 = (bf16[72,320]{1,0:T(8,128)(2,1)S(1)}, bf16[72,320]{1,0:T(8,128)(2,1)S(1)}, u32[]{:S(2)}, u32[]{:S(2)}) collective-permute-start(bf16[72,320]{1,0:T(8,128)(2,1)S(1)} %get-tuple-element.31), channel_id=1, source_target_pairs={{640,1},{642,3},{644,5},{646,7},{648,9},{650,11},{652,13},{654,15}... | collective-permute-start | bytes 138248 | tf_op jit(solution)/shard_map/ppermute | solution.py:317
  22.8 22.3 %collective-permute-start.10 = (bf16[72,320]{1,0:T(8,128)(2,1)S(1)}, bf16[72,320]{1,0:T(8,128)(2,1)S(1)}, u32[]{:S(2)}, u32[]{:S(2)}) collective-permute-start(bf16[72,320]{1,0:T(8,128)(2,1)S(1)} %get-tuple-element.32), channel_id=1, source_target_pairs={{640,737},{642,739},{644,741},{646,743},{648,745},{650,747},{652,7... | collective-permute-start | bytes 138248 | tf_op jit(solution)/shard_map/ppermute | solution.py:317
  34.4 12.0 %collective-permute-start.11 = (bf16[72,320]{1,0:T(8,128)(2,1)S(1)}, bf16[72,320]{1,0:T(8,128)(2,1)S(1)}, u32[]{:S(2)}, u32[]{:S(2)}) collective-permute-start(bf16[72,320]{1,0:T(8,128)(2,1)S(1)} %get-tuple-element.33), channel_id=1, source_target_pairs={{640,31},{642,1},{644,3},{646,5},{648,7},{650,9},{652,11},{654,13}... | collective-permute-start | bytes 138248 | tf_op jit(solution)/shard_map/ppermute | solution.py:317
  35.7 12.0 %collective-permute-start.12 = (bf16[72,320]{1,0:T(8,128)(2,1)S(1)}, bf16[72,320]{1,0:T(8,128)(2,1)S(1)}, u32[]{:S(2)}, u32[]{:S(2)}) collective-permute-start(bf16[72,320]{1,0:T(8,128)(2,1)S(1)} %get-tuple-element.34), channel_id=1, source_target_pairs={{640,767},{642,737},{644,739},{646,741},{648,743},{650,745},{652,7... | collective-permute-start | bytes 138248 | tf_op jit(solution)/shard_map/ppermute | solution.py:317
  42.3 30.3 %copy-start = (bf16[288,288]{1,0:T(8,128)(2,1)S(1)}, bf16[288,288]{1,0:T(8,128)(2,1)}, u32[]{:S(2)}) copy-start(bf16[288,288]{1,0:T(8,128)(2,1)} %constant.8.clone.refs_8_) | copy-start | bytes 497668
  42.3 14.0 %collective-permute-start.4 = (bf16[72,320]{1,0:T(8,128)(2,1)S(1)}, bf16[72,320]{1,0:T(8,128)(2,1)S(1)}, u32[]{:S(2)}, u32[]{:S(2)}) collective-permute-start(bf16[72,320]{1,0:T(8,128)(2,1)S(1)} %get-tuple-element.26), channel_id=1, source_target_pairs={{641,34},{643,36},{645,38},{647,40},{649,42},{651,44},{653,46},{65... | collective-permute-start | bytes 138248 | tf_op jit(solution)/shard_map/ppermute | solution.py:317
  43.8 17.1 %collective-permute-start.5 = (bf16[72,320]{1,0:T(8,128)(2,1)S(1)}, bf16[72,320]{1,0:T(8,128)(2,1)S(1)}, u32[]{:S(2)}, u32[]{:S(2)}) collective-permute-start(bf16[72,320]{1,0:T(8,128)(2,1)S(1)} %get-tuple-element.27), channel_id=1, source_target_pairs={{641,2},{643,4},{645,6},{647,8},{649,10},{651,12},{653,14},{655,16... | collective-permute-start | bytes 138248 | tf_op jit(solution)/shard_map/ppermute | solution.py:317
  45.1 18.9 %collective-permute-start.6 = (bf16[72,320]{1,0:T(8,128)(2,1)S(1)}, bf16[72,320]{1,0:T(8,128)(2,1)S(1)}, u32[]{:S(2)}, u32[]{:S(2)}) collective-permute-start(bf16[72,320]{1,0:T(8,128)(2,1)S(1)} %get-tuple-element.28), channel_id=1, source_target_pairs={{641,32},{643,34},{645,36},{647,38},{649,40},{651,42},{653,44},{65... | collective-permute-start | bytes 138248 | tf_op jit(solution)/shard_map/ppermute | solution.py:317
  46.4 17.6 %collective-permute-start.7 = (bf16[72,320]{1,0:T(8,128)(2,1)S(1)}, bf16[72,320]{1,0:T(8,128)(2,1)S(1)}, u32[]{:S(2)}, u32[]{:S(2)}) collective-permute-start(bf16[72,320]{1,0:T(8,128)(2,1)S(1)} %get-tuple-element.29), channel_id=1, source_target_pairs={{641,0},{643,2},{645,4},{647,6},{649,8},{651,10},{653,12},{655,14}... | collective-permute-start | bytes 138248 | tf_op jit(solution)/shard_map/ppermute | solution.py:317
  52.4 13.0 %collective-permute-start.13 = (bf16[72,320]{1,0:T(8,128)(2,1)S(1)}, bf16[72,320]{1,0:T(8,128)(2,1)S(1)}, u32[]{:S(2)}, u32[]{:S(2)}) collective-permute-start(bf16[72,320]{1,0:T(8,128)(2,1)S(1)} %get-tuple-element.35), channel_id=1, source_target_pairs={{1,35},{3,37},{5,39},{7,41},{9,43},{11,45},{13,47},{15,49},{17,51}... | collective-permute-start | bytes 138248 | tf_op jit(solution)/shard_map/ppermute | solution.py:317
  56.3 9.1 %collective-permute-start.14 = (bf16[72,320]{1,0:T(8,128)(2,1)S(1)}, bf16[72,320]{1,0:T(8,128)(2,1)S(1)}, u32[]{:S(2)}, u32[]{:S(2)}) collective-permute-start(bf16[72,320]{1,0:T(8,128)(2,1)S(1)} %get-tuple-element.36), channel_id=1, source_target_pairs={{1,3},{3,5},{5,7},{7,9},{9,11},{11,13},{13,15},{15,17},{17,19},{19... | collective-permute-start | bytes 138248 | tf_op jit(solution)/shard_map/ppermute | solution.py:317
  60.8 11.8 %collective-permute-start.15 = (bf16[72,320]{1,0:T(8,128)(2,1)S(1)}, bf16[72,320]{1,0:T(8,128)(2,1)S(1)}, u32[]{:S(2)}, u32[]{:S(2)}) collective-permute-start(bf16[72,320]{1,0:T(8,128)(2,1)S(1)} %get-tuple-element.37), channel_id=1, source_target_pairs={{1,33},{3,35},{5,37},{7,39},{9,41},{11,43},{13,45},{15,47},{17,49}... | collective-permute-start | bytes 138248 | tf_op jit(solution)/shard_map/ppermute | solution.py:317

commit v3 on v2

--- a/solution.py
+++ b/solution.py
@@ -59,7 +59,7 @@
     return arrange.astype(jnp.bfloat16)
 
 
-def lay_out_bias(table_ref, spread_ref, addend_ref, wide_ref):
+def lay_out_bias(table_ref, spread_ref, addend_ref, wide_ref, rows_ref):
     for head in range(HEADS):
         wide_ref[2 * head : 2 * head + 2, :] = table_ref[0, 0, head].astype(jnp.float32)
     for lev in range(WLEV):
@@ -69,14 +69,20 @@
                 for key_lat in range(WLAT):
                     at = ((key_lev * WLEV + lev) * WLAT * WLAT + key_lat * WLAT + lat) * SPAN
                     parts.append(wide_ref[:, at : at + SPAN])
-            rows = jnp.concatenate(parts, axis=1).astype(jnp.bfloat16)
-            dense = jnp.dot(rows, spread_ref[...], preferred_element_type=jnp.float32)
-            for lon in range(WLON):
+            first = (lev * WLAT + lat) * 24
+            rows_ref[first : first + 24, :] = jnp.concatenate(parts, axis=1)
+    rows = rows_ref[...].astype(jnp.bfloat16)
+    for lon in range(WLON):
+        dense = jnp.dot(
+            rows, spread_ref[:, lon * 256 : lon * 256 + 256], preferred_element_type=jnp.float32
+        )
+        for lev in range(WLEV):
+            for lat in range(WLAT):
+                first = (lev * WLAT + lat) * 24
                 row = token_row(lev, lat, lon)
                 for tile in range(2):
-                    lanes = lon * 256 + tile * 128
                     addend_ref[tile, pl.ds(row, 2 * HEADS, stride=WIN), :] = dense[
-                        : 2 * HEADS, lanes : lanes + 128
+                        first : first + 2 * HEADS, tile * 128 : tile * 128 + 128
                     ]
 
 
@@ -90,14 +96,38 @@
     return copies
 
 
-def prepare_kernel(table_hbm, spread_hbm, after_ref, addend_ref, table_ref, spread_ref, wide_ref, sems):
+def pack(quarter_ref):
+    rest = jnp.concatenate(
+        [quarter_ref[0:QUARTER, 256:C], quarter_ref[QUARTER : 2 * QUARTER, 256:C]], axis=1
+    )
+    return jnp.concatenate(
+        [quarter_ref[:, 0:128], quarter_ref[:, 128:256], rest], axis=0
+    ).astype(jnp.bfloat16)
+
+
+def unpack(packed_ref, target_ref, starts):
+    packed = packed_ref[...].astype(jnp.float32)
+    for half, at in enumerate(starts):
+        rows = slice(at, at + QUARTER)
+        target_ref[rows, 0:128] = packed[half * QUARTER : (half + 1) * QUARTER]
+        target_ref[rows, 128:256] = packed[(2 + half) * QUARTER : (3 + half) * QUARTER]
+        target_ref[rows, 256:C] = packed[4 * QUARTER :, half * 64 : half * 64 + 64]
+
+
+def prepare_kernel(*refs):
+    table_hbm, spread_hbm, hbm = refs[0], refs[1], refs[2:11]
+    addend_ref, params = refs[12], refs[13:22]
+    table_ref, spread_ref, wide_ref, rows_ref, sems = refs[22:]
     last_lat = lax.axis_index("lat") == lax.axis_size("lat") - 1
 
     @pl.when(lax.axis_index("section") == 1)
     def work():
-        for copy in fetch((table_hbm, spread_hbm), (table_ref, spread_ref), sems):
+        copies = fetch(
+            (table_hbm, spread_hbm, *hbm), (table_ref, spread_ref, *params), sems
+        )
+        for copy in copies:
             copy.wait()
-        lay_out_bias(table_ref, spread_ref, addend_ref, wide_ref)
+        lay_out_bias(table_ref, spread_ref, addend_ref, wide_ref, rows_ref)
         for tile in range(2):
             query = lax.broadcasted_iota(jnp.int32, (WIN, 128), 0)
             key = lax.broadcasted_iota(jnp.int32, (WIN, 128), 1) + tile * 128
@@ -182,36 +212,33 @@
     )
 
 
-def first_kernel(prepares, patch_ref, arrange_hbm, *refs):
-    hbm, refs = refs[:9], refs[9:]
+def first_kernel(prepares, *refs):
     if prepares:
-        table_hbm, spread_hbm = refs[:2]
-        outs, addend_ref, refs = refs[2:6], refs[6], refs[7:]
+        patch_hbm, arrange_hbm, hbm, table_hbm, spread_hbm = *refs[:2], refs[2:11], *refs[11:13]
+        outs, addend_ref, arrange_ref, params = refs[13:17], refs[17], refs[18], refs[19:28]
+        field_ref, packed_ref, attended_ref, quarter_ref = refs[28:32]
+        patch_ref, table_ref, spread_ref, wide_ref, rows_ref, sems = refs[32:]
     else:
-        addend_ref, outs, refs = refs[0], refs[1:5], refs[5:]
-    field_ref, packed_ref, attended_ref, quarter_ref, arrange_ref = refs[:5]
-    params, sems = refs[5:14], refs[14]
+        patch_ref, arrange_ref, params, addend_ref = *refs[:2], refs[2:11], refs[11]
+        outs, (field_ref, packed_ref, attended_ref, quarter_ref) = refs[12:16], refs[16:]
 
     @pl.when(lax.axis_index("section") == 0)
     def work():
+        copies = []
         if prepares:
-            own_ref, table_ref, spread_ref, wide_ref, more_sems = refs[15:]
-            early = fetch(
-                (table_hbm, spread_hbm, patch_ref), (table_ref, spread_ref, own_ref), more_sems
+            copies = fetch(
+                (table_hbm, spread_hbm, patch_hbm, arrange_hbm, *hbm),
+                (table_ref, spread_ref, patch_ref, arrange_ref, *params),
+                sems,
             )
-        else:
-            own_ref = patch_ref
-        (arranging,) = fetch((arrange_hbm,), (arrange_ref,), sems.at[pl.ds(9, 1)])
-        copies = fetch(hbm, params, sems)
-        if prepares:
-            for copy in early:
+            for copy in copies[:4]:
                 copy.wait()
-            lay_out_bias(table_ref, spread_ref, addend_ref, wide_ref)
+            copies = copies[4:]
+            lay_out_bias(table_ref, spread_ref, addend_ref, wide_ref, rows_ref)
         for lat in range(WLAT):
             for lon in range(WLON):
                 at = (lat * WLON + lon) * 4
-                field_ref[at : at + 4, :] = own_ref[0, lat, lon].astype(jnp.float32)
-        arranging.wait()
+                field_ref[at : at + 4, :] = patch_ref[0, lat, lon].astype(jnp.float32)
         field_ref[...] = jnp.dot(
             arrange_ref[...],
             field_ref[...].astype(jnp.bfloat16),
@@ -223,38 +250,39 @@
                 lev = (place + 1) % 4
                 at = (lev // 2) * WIN + quarter * QUARTER + (lev % 2) * PIECE
                 quarter_ref[place * PIECE : (place + 1) * PIECE, :] = field_ref[at : at + PIECE, :]
-            outs[quarter][...] = quarter_ref[...].astype(jnp.bfloat16)
+            outs[quarter][...] = pack(quarter_ref)
 
 
 def second_kernel(*refs):
-    quarters, hbm, (addend_ref,), outs = refs[:4], refs[4:13], refs[13:14], refs[14:18]
-    field_ref, packed_ref, attended_ref, quarter_ref = refs[18:22]
-    params, sems = refs[22:31], refs[31]
+    quarters, params, addend_ref, outs = refs[:4], refs[4:13], refs[13], refs[14:18]
+    field_ref, packed_ref, attended_ref, quarter_ref = refs[18:]
 
     @pl.when(lax.axis_index("section") == 1)
     def work():
-        copies = fetch(hbm, params, sems)
         for quarter in range(4):
-            held = quarters[quarter][...].astype(jnp.float32)
-            for window in range(2):
-                at = window * WIN + quarter * QUARTER
-                field_ref[at : at + QUARTER, :] = held[window * QUARTER : (window + 1) * QUARTER]
-        run_block(field_ref, params, copies, addend_ref, packed_ref, attended_ref)
+            at = quarter * QUARTER
+            unpack(quarters[quarter], field_ref, (at, WIN + at))
+        run_block(field_ref, params, [], addend_ref, packed_ref, attended_ref)
         for quarter in range(4):
             for window in range(2):
                 at = window * WIN + quarter * QUARTER
                 quarter_ref[window * QUARTER : (window + 1) * QUARTER, :] = field_ref[
                     at : at + QUARTER, :
                 ]
-            outs[quarter][...] = quarter_ref[...].astype(jnp.bfloat16)
+            outs[quarter][...] = pack(quarter_ref)
 
 
 def place_kernel(*refs):
     arrange_ref, out_ref, grid_ref = refs[8:]
 
     def place(quarters):
-        held = jnp.concatenate([quarter[...] for quarter in quarters], axis=0)
-        grid_ref[...] = jnp.dot(arrange_ref[...], held, preferred_element_type=jnp.float32)
+        for at, quarter in enumerate(quarters):
+            unpack(quarter, grid_ref, (2 * at * QUARTER, (2 * at + 1) * QUARTER))
+        grid_ref[...] = jnp.dot(
+            arrange_ref[...],
+            grid_ref[...].astype(jnp.bfloat16),
+            preferred_element_type=jnp.float32,
+        )
         for lat in range(WLAT):
             for lon in range(WLON):
                 at = (lat * WLON + lon) * 4
@@ -282,7 +310,7 @@
     )(*operands)
 
 
-QUARTERS = [jax.ShapeDtypeStruct((2 * QUARTER, C), jnp.bfloat16)] * 4
+QUARTERS = [jax.ShapeDtypeStruct((5 * QUARTER, 128), jnp.bfloat16)] * 4
 BLOCK_SCRATCH = [
     pltpu.VMEM((2 * WIN, C), jnp.float32),
     pltpu.VMEM((2 * WIN, 3 * 384), jnp.bfloat16),
@@ -355,65 +383,59 @@
     arrange = jnp.asarray(arrange_matrix())
     spread = jnp.asarray(spread_matrix())
     addend_shape = jax.ShapeDtypeStruct((2, 2 * HEADS * WIN, 128), jnp.float32)
-    wide = pltpu.VMEM((24, table.shape[-1]), jnp.float32)
-    first_scratch = [
-        *BLOCK_SCRATCH,
-        held(arrange),
-        *map(held, params),
-        pltpu.SemaphoreType.DMA((10,)),
-    ]
-    second_scratch = [*BLOCK_SCRATCH, *map(held, params), pltpu.SemaphoreType.DMA((9,))]
-    *own_first, addend_one = call(
+    bias_scratch = [
+        held(table),
+        held(spread),
+        pltpu.VMEM((24, table.shape[-1]), jnp.float32),
+        pltpu.VMEM((12 * 24, spread.shape[0]), jnp.float32),
+    ]
+    brought = [jax.ShapeDtypeStruct(member.shape, member.dtype) for member in params]
+    made = call(
         functools.partial(first_kernel, True),
         (patch, arrange, *params, table, spread),
         "h" * 13,
-        [*QUARTERS, addend_shape],
-        [
-            *first_scratch,
-            held(patch),
-            held(table),
-            held(spread),
-            wide,
-            pltpu.SemaphoreType.DMA((3,)),
-        ],
+        [*QUARTERS, addend_shape, jax.ShapeDtypeStruct(arrange.shape, arrange.dtype), *brought],
+        [*BLOCK_SCRATCH, held(patch), *bias_scratch, pltpu.SemaphoreType.DMA((13,))],
         BLOCK_FLOPS,
     )
+    own_first, (addend_one, arranging), params_one = made[:4], made[4:6], made[6:]
     own_shifted = to_shifted(own_first, straight, mirrored)
-    addend_two = call(
+    addend_two, *params_two = call(
         prepare_kernel,
-        (table, spread, own_first[0]),
-        "hhv",
-        addend_shape,
-        [held(table), held(spread), wide, pltpu.SemaphoreType.DMA((2,))],
+        (table, spread, *params, own_first[0]),
+        "h" * 11 + "v",
+        [addend_shape, *brought],
+        [*bias_scratch, pltpu.SemaphoreType.DMA((11,))],
         200_000_000,
     )
     other_first = call(
         functools.partial(first_kernel, False),
-        (other, arrange, *params, addend_one),
-        "vh" + "h" * 9 + "v",
+        (other, arranging, *params_one, addend_one),
+        "v" * 12,
         QUARTERS,
-        first_scratch,
+        BLOCK_SCRATCH,
         BLOCK_FLOPS,
     )
     other_shifted = to_shifted(other_first, mirrored, straight)
     block_two = functools.partial(
         call,
         second_kernel,
-        places="vvvv" + "h" * 9 + "v",
+        places="v" * 14,
         outs=QUARTERS,
-        scratch=second_scratch,
+        scratch=BLOCK_SCRATCH,
         flops=BLOCK_FLOPS,
     )
-    own_done = block_two((*own_shifted, *params, addend_two))
+    own_done = block_two((*own_shifted, *params_two, addend_two))
     own_back = [
         send(own_done[3 - q], (1, 0), (1 - q // 2, 1 - q % 2), mirrored, straight)
         for q in range(4)
     ]
-    other_done = block_two((*other_shifted, *params, addend_two))
-    other_back = [
+    other_done = block_two((*other_shifted, *params_two, addend_two))
+    across, along, upward = [
         send(other_done[3 - q], (1, 1), (1 - q // 2, 1 - q % 2), straight, straight)
-        for q in range(3)
-    ]
+        for q in (0, 2, 1)
+    ]
+    other_back = (across, upward, along)
     placed = call(
         place_kernel,
         (*own_back, *other_back, other_done[0], jnp.asarray(place_matrix())),

time: 74.1 us -> 65.5 us (0.88)
  waiting for transfers between devices: 28.5 us -> 23.9 us
  Pallas kernels: 16.4 us -> 12.9 us
    ppermute x16, waiting for transfers between devices: 28.5 us -> 23.9 us  [send(): return lax.ppermute(block, AXES, route)]
    pallas_call x6, Pallas kernels: 16.4 us -> 12.9 us  [call(): pl.pallas_call(kernel, out_shape=outs, in_specs=[pl.BlockSpec(memory_spac...]
  transfers between devices with their start and end apart: 16 -> 16, of which waited for: 6 -> 6; matrix products, arithmetic and copies ran while one was open for 0% -> 0% of each run, Pallas kernels for 21% -> 18%
where the time goes in v3:
time: 65.5 us; the launch traced here: 65.1 us
  starting transfers between devices  28.2 us (43%)
  waiting for transfers between devices  23.9 us (36%)
  Pallas kernels  12.9 us (20%)
    ppermute x16, starting transfers between devices, send(): return lax.ppermute(block, AXES, route)  28.2 us
    ppermute x16, waiting for transfers between devices, send(): return lax.ppermute(block, AXES, route)  23.9 us
    pallas_call x6, Pallas kernels, call(): pl.pallas_call(kernel, out_shape=outs, in_specs=[pl.BlockSpec(memory_spac...  12.9 us
  transfers between devices with their start and end apart: 16, of which 6 were waited for; matrix products, arithmetic and copies ran while one was open for 0% of the time, Pallas kernels for 18%

profile of v3, /device:TPU:401, one launch (start us, length us, event | category | flops | bytes accessed | tf_op | source)
XLA Modules:
  0.0 65.1 jit_solution(16029376378103224229)
XLA Ops:
  0.0 1.3 %collective-permute-start.8 = (bf16[1,6,12,4,320]{4,3,2,1,0:T(4,128)(2,1)}, bf16[1,6,12,4,320]{4,3,2,1,0:T(4,128)(2,1)S(1)}, u32[]{:S(2)}, u32[]{:S(2)}) collective-permute-start(bf16[1,6,12,4,320]{4,3,2,1,0:T(4,128)(2,1)} %bitcast.8), channel_id=1, source_target_pairs={{1,640},{3,642},{5,644},{7,646},{9,648},{11,650},{13,652},{15,654}... | collective-permute-start | bytes 552968 | tf_op jit(solution)/shard_map/ppermute | solution.py:345
  1.3 0.1 shard_map.136
  1.4 1.3 %collective-permute-start = (bf16[180,128]{1,0:T(8,128)(2,1)S(1)}, bf16[180,128]{1,0:T(8,128)(2,1)S(1)}, u32[]{:S(2)}, u32[]{:S(2)}) collective-permute-start(bf16[180,128]{1,0:T(8,128)(2,1)S(1)} %get-tuple-element.42), channel_id=1, source_target_pairs={{0,641},{2,643},{4,645},{6,647},{8,649},{10,651},{12,653},{14,655}... | collective-permute-start | bytes 138248 | tf_op jit(solution)/shard_map/ppermute | solution.py:345
  2.8 1.3 %collective-permute-start.1 = (bf16[180,128]{1,0:T(8,128)(2,1)S(1)}, bf16[180,128]{1,0:T(8,128)(2,1)S(1)}, u32[]{:S(2)}, u32[]{:S(2)}) collective-permute-start(bf16[180,128]{1,0:T(8,128)(2,1)S(1)} %get-tuple-element.43), channel_id=1, source_target_pairs={{0,97},{2,99},{4,101},{6,103},{8,105},{10,107},{12,109},{14,111},{... | collective-permute-start | bytes 138248 | tf_op jit(solution)/shard_map/ppermute | solution.py:345
  4.0 1.3 %collective-permute-start.2 = (bf16[180,128]{1,0:T(8,128)(2,1)S(1)}, bf16[180,128]{1,0:T(8,128)(2,1)S(1)}, u32[]{:S(2)}, u32[]{:S(2)}) collective-permute-start(bf16[180,128]{1,0:T(8,128)(2,1)S(1)} %get-tuple-element.44), channel_id=1, source_target_pairs={{0,671},{2,641},{4,643},{6,645},{8,647},{10,649},{12,651},{14,653}... | collective-permute-start | bytes 138248 | tf_op jit(solution)/shard_map/ppermute | solution.py:345
  5.3 1.3 %collective-permute-start.3 = (bf16[180,128]{1,0:T(8,128)(2,1)S(1)}, bf16[180,128]{1,0:T(8,128)(2,1)S(1)}, u32[]{:S(2)}, u32[]{:S(2)}) collective-permute-start(bf16[180,128]{1,0:T(8,128)(2,1)S(1)} %get-tuple-element.45.refs_11_), channel_id=1, source_target_pairs={{0,127},{2,97},{4,99},{6,101},{8,103},{10,105},{12,107},{14,109},{... | collective-permute-start | bytes 138248 | tf_op jit(solution)/shard_map/ppermute | solution.py:345
  6.7 4.7 %shard_map.137 = (f32[2,2880,128]{2,1,0:T(8,128)S(1)}, bf16[1,2,320]{2,1,0:T(2,128)(2,1)S(1)}, bf16[1,2,320]{2,1,0:T(2,128)(2,1)S(1)}, bf16[1,320,960]{2,1,0:T(8...) custom-call(bf16[1,1,10,2,3312]{4,3,2,1,0:T(2,128)(2,1)} %bitcast.7,, ...), custom_call_target="tpu_custom_call" | custom-call | flops 200000000 | bytes 4000000 | tf_op jit(solution)/shard_map/pallas_call | solution.py:302
  11.4 3.8 %collective-permute-done.8.refs_0_ = bf16[1,6,12,4,320]{4,3,2,1,0:T(4,128)(2,1)S(1)} collective-permute-done((bf16[1,6,12,4,320]{4,3,2,1,0:T(4,128)(2,1)}, bf16[1,6,12,4,320]{4,3,2,1,0:T(4,128)(2,1)S(1)}, u32[]{:S(2)}, u32[]{:S(2)}) %collective-permute-start.8) | collective-permute-done | bytes 184352 | tf_op jit(solution)/shard_map/ppermute | solution.py:345
  15.2 1.3 %collective-permute-start.9 = (bf16[180,128]{1,0:T(8,128)(2,1)S(1)}, bf16[180,128]{1,0:T(8,128)(2,1)S(1)}, u32[]{:S(2)}, u32[]{:S(2)}) collective-permute-start(bf16[180,128]{1,0:T(8,128)(2,1)S(1)} %get-tuple-element.71), channel_id=1, source_target_pairs={{640,1},{642,3},{644,5},{646,7},{648,9},{650,11},{652,13},{654,15}... | collective-permute-start | bytes 138248 | tf_op jit(solution)/shard_map/ppermute | solution.py:345
  16.5 0.0 collective-permute-done.refs_0_
  16.5 1.3 %collective-permute-start.10 = (bf16[180,128]{1,0:T(8,128)(2,1)S(1)}, bf16[180,128]{1,0:T(8,128)(2,1)S(1)}, u32[]{:S(2)}, u32[]{:S(2)}) collective-permute-start(bf16[180,128]{1,0:T(8,128)(2,1)S(1)} %get-tuple-element.72), channel_id=1, source_target_pairs={{640,737},{642,739},{644,741},{646,743},{648,745},{650,747},{652,7... | collective-permute-start | bytes 138248 | tf_op jit(solution)/shard_map/ppermute | solution.py:345
  17.8 3.3 %collective-permute-done.1.refs_1_ = bf16[180,128]{1,0:T(8,128)(2,1)S(1)} collective-permute-done((bf16[180,128]{1,0:T(8,128)(2,1)S(1)}, bf16[180,128]{1,0:T(8,128)(2,1)S(1)}, u32[]{:S(2)}, u32[]{:S(2)}) %collective-permute-start.1) | collective-permute-done | bytes 46112 | tf_op jit(solution)/shard_map/ppermute | solution.py:345
  21.1 1.3 %collective-permute-start.11 = (bf16[180,128]{1,0:T(8,128)(2,1)S(1)}, bf16[180,128]{1,0:T(8,128)(2,1)S(1)}, u32[]{:S(2)}, u32[]{:S(2)}) collective-permute-start(bf16[180,128]{1,0:T(8,128)(2,1)S(1)} %get-tuple-element.73), channel_id=1, source_target_pairs={{640,31},{642,1},{644,3},{646,5},{648,7},{650,9},{652,11},{654,13}... | collective-permute-start | bytes 138248 | tf_op jit(solution)/shard_map/ppermute | solution.py:345
  22.4 0.7 %collective-permute-done.2.refs_2_ = bf16[180,128]{1,0:T(8,128)(2,1)S(1)} collective-permute-done((bf16[180,128]{1,0:T(8,128)(2,1)S(1)}, bf16[180,128]{1,0:T(8,128)(2,1)S(1)}, u32[]{:S(2)}, u32[]{:S(2)}) %collective-permute-start.2) | collective-permute-done | bytes 46112 | tf_op jit(solution)/shard_map/ppermute | solution.py:345
  23.1 1.3 %collective-permute-start.12 = (bf16[180,128]{1,0:T(8,128)(2,1)S(1)}, bf16[180,128]{1,0:T(8,128)(2,1)S(1)}, u32[]{:S(2)}, u32[]{:S(2)}) collective-permute-start(bf16[180,128]{1,0:T(8,128)(2,1)S(1)} %get-tuple-element.74), channel_id=1, source_target_pairs={{640,767},{642,737},{644,739},{646,741},{648,743},{650,745},{652,7... | collective-permute-start | bytes 138248 | tf_op jit(solution)/shard_map/ppermute | solution.py:345
  24.4 7.2 %collective-permute-done.3.refs_3_ = bf16[180,128]{1,0:T(8,128)(2,1)S(1)} collective-permute-done((bf16[180,128]{1,0:T(8,128)(2,1)S(1)}, bf16[180,128]{1,0:T(8,128)(2,1)S(1)}, u32[]{:S(2)}, u32[]{:S(2)}) %collective-permute-start.3) | collective-permute-done | bytes 46112 | tf_op jit(solution)/shard_map/ppermute | solution.py:345
  31.5 3.5 %shard_map.138 = (bf16[180,128]{1,0:T(8,128)(2,1)S(1)}, bf16[180,128]{1,0:T(8,128)(2,1)S(1)}, bf16[180,128]{1,0:T(8,128)(2,1)S(1)}, bf16[180,128]{1,0:T(8,128)(2,1)S(1)}) custom-call(bf16[180,128]{1,0:T(8,128)(2,1)S(1)} %collective-permute-done.refs_0_, bf16[180,128]{1,0:T(8,128)(2,1)S(1)} %collective-permute-done.1.refs_1_, ...), custom_call_target="tpu_custom_call" | custom-call | flops 800000000 | bytes 4000000 | tf_op jit(solution)/shard_map/pallas_call | solution.py:302
  35.0 0.0 copy-start
  35.0 1.4 %collective-permute-start.4 = (bf16[180,128]{1,0:T(8,128)(2,1)S(1)}, bf16[180,128]{1,0:T(8,128)(2,1)S(1)}, u32[]{:S(2)}, u32[]{:S(2)}) collective-permute-start(bf16[180,128]{1,0:T(8,128)(2,1)S(1)} %get-tuple-element.56), channel_id=1, source_target_pairs={{641,34},{643,36},{645,38},{647,40},{649,42},{651,44},{653,46},{65... | collective-permute-start | bytes 138248 | tf_op jit(solution)/shard_map/ppermute | solution.py:345
  36.5 0.0 collective-permute-done.9.refs_0_
  36.5 1.3 %collective-permute-start.5 = (bf16[180,128]{1,0:T(8,128)(2,1)S(1)}, bf16[180,128]{1,0:T(8,128)(2,1)S(1)}, u32[]{:S(2)}, u32[]{:S(2)}) collective-permute-start(bf16[180,128]{1,0:T(8,128)(2,1)S(1)} %get-tuple-element.57), channel_id=1, source_target_pairs={{641,2},{643,4},{645,6},{647,8},{649,10},{651,12},{653,14},{655,16... | collective-permute-start | bytes 138248 | tf_op jit(solution)/shard_map/ppermute | solution.py:345
  37.8 0.0 collective-permute-done.10.refs_1_
  37.8 1.3 %collective-permute-start.6 = (bf16[180,128]{1,0:T(8,128)(2,1)S(1)}, bf16[180,128]{1,0:T(8,128)(2,1)S(1)}, u32[]{:S(2)}, u32[]{:S(2)}) collective-permute-start(bf16[180,128]{1,0:T(8,128)(2,1)S(1)} %get-tuple-element.58), channel_id=1, source_target_pairs={{641,32},{643,34},{645,36},{647,38},{649,40},{651,42},{653,44},{65... | collective-permute-start | bytes 138248 | tf_op jit(solution)/shard_map/ppermute | solution.py:345
  39.1 0.0 collective-permute-done.11.refs_2_
  39.1 1.3 %collective-permute-start.7 = (bf16[180,128]{1,0:T(8,128)(2,1)S(1)}, bf16[180,128]{1,0:T(8,128)(2,1)S(1)}, u32[]{:S(2)}, u32[]{:S(2)}) collective-permute-start(bf16[180,128]{1,0:T(8,128)(2,1)S(1)} %get-tuple-element.59), channel_id=1, source_target_pairs={{641,0},{643,2},{645,4},{647,6},{649,8},{651,10},{653,12},{655,14}... | collective-permute-start | bytes 138248 | tf_op jit(solution)/shard_map/ppermute | solution.py:345
  40.4 0.0 collective-permute-done.12.refs_3_
  40.4 3.5 %shard_map.140 = (bf16[180,128]{1,0:T(8,128)(2,1)S(1)}, bf16[180,128]{1,0:T(8,128)(2,1)S(1)}, bf16[180,128]{1,0:T(8,128)(2,1)S(1)}, bf16[180,128]{1,0:T(8,128)(2,1)S(1)}) custom-call(bf16[180,128]{1,0:T(8,128)(2,1)S(1)} %collective-permute-done.9.refs_0_, bf16[180,128]{1,0:T(8,128)(2,1)S(1)} %collective-permute-done.10.refs_1_, ...), custom_call_target="tpu_custom_call" | custom-call | flops 800000000 | bytes 4000000 | tf_op jit(solution)/shard_map/pallas_call | solution.py:302
  43.9 4.0 %collective-permute-start.13 = (bf16[180,128]{1,0:T(8,128)(2,1)S(1)}, bf16[180,128]{1,0:T(8,128)(2,1)S(1)}, u32[]{:S(2)}, u32[]{:S(2)}) collective-permute-start(bf16[180,128]{1,0:T(8,128)(2,1)S(1)} %get-tuple-element.75), channel_id=1, source_target_pairs={{1,35},{3,37},{5,39},{7,41},{9,43},{11,45},{13,47},{15,49},{17,51}... | collective-permute-start | bytes 138248 | tf_op jit(solution)/shard_map/ppermute | solution.py:345
  47.9 0.0 collective-permute-done.4.refs_0_
  47.9 4.4 %collective-permute-start.14 = (bf16[180,128]{1,0:T(8,128)(2,1)S(1)}, bf16[180,128]{1,0:T(8,128)(2,1)S(1)}, u32[]{:S(2)}, u32[]{:S(2)}) collective-permute-start(bf16[180,128]{1,0:T(8,128)(2,1)S(1)} %get-tuple-element.76), channel_id=1, source_target_pairs={{1,3},{3,5},{5,7},{7,9},{9,11},{11,13},{13,15},{15,17},{17,19},{19... | collective-permute-start | bytes 138248 | tf_op jit(solution)/shard_map/ppermute | solution.py:345
  52.3 0.0 collective-permute-done.5.refs_1_
  52.3 2.8 %collective-permute-start.15 = (bf16[180,128]{1,0:T(8,128)(2,1)S(1)}, bf16[180,128]{1,0:T(8,128)(2,1)S(1)}, u32[]{:S(2)}, u32[]{:S(2)}) collective-permute-start(bf16[180,128]{1,0:T(8,128)(2,1)S(1)} %get-tuple-element.77), channel_id=1, source_target_pairs={{1,33},{3,35},{5,37},{7,39},{9,41},{11,43},{13,45},{15,47},{17,49}... | collective-permute-start | bytes 138248 | tf_op jit(solution)/shard_map/ppermute | solution.py:345
  55.2 0.0 collective-permute-done.6.refs_2_
  55.2 0.0 collective-permute-done.7.refs_3_
  55.2 1.3 %collective-permute-done.13.refs_4_ = bf16[180,128]{1,0:T(8,128)(2,1)S(1)} collective-permute-done((bf16[180,128]{1,0:T(8,128)(2,1)S(1)}, bf16[180,128]{1,0:T(8,128)(2,1)S(1)}, u32[]{:S(2)}, u32[]{:S(2)}) %collective-permute-start.13) | collective-permute-done | bytes 46112 | tf_op jit(solution)/shard_map/ppermute | solution.py:345
  56.5 0.0 collective-permute-done.14.refs_5_
  56.5 7.5 %collective-permute-done.15.refs_6_ = bf16[180,128]{1,0:T(8,128)(2,1)S(1)} collective-permute-done((bf16[180,128]{1,0:T(8,128)(2,1)S(1)}, bf16[180,128]{1,0:T(8,128)(2,1)S(1)}, u32[]{:S(2)}, u32[]{:S(2)}) %collective-permute-start.15) | collective-permute-done | bytes 46112 | tf_op jit(solution)/shard_map/ppermute | solution.py:345
  64.1 0.0 copy-done
  64.1 1.1 %shard_map.141 = bf16[1,6,12,4,320]{4,3,2,1,0:T(4,128)(2,1)} custom-call(bf16[180,128]{1,0:T(8,128)(2,1)S(1)} %collective-permute-done.4.refs_0_, bf16[180,128]{1,0:T(8,128)(2,1)S(1)} %collective-permute-done.5.refs_1_, bf16[180,128]{1,0:T(8,128)(2,1)S(1)} %collective-permute-done.6.refs_2_, bf16[180,128]{1,0:T(8,128)(2,1)S(1)} %collective-permute-done.7.refs_3_, ...), custom_call_target="tpu_custom_call" | custom-call | flops 1000000 | bytes 4000000 | tf_op jit(solution)/shard_map/pallas_call | solution.py:302
  (1 shorter events, 0.0 us)
Async XLA Ops:
  0.0 15.2 %collective-permute-start.8 = (bf16[1,6,12,4,320]{4,3,2,1,0:T(4,128)(2,1)}, bf16[1,6,12,4,320]{4,3,2,1,0:T(4,128)(2,1)S(1)}, u32[]{:S(2)}, u32[]{:S(2)}) collective-permute-start(bf16[1,6,12,4,320]{4,3,2,1,0:T(4,128)(2,1)} %bitcast.8), channel_id=1, source_target_pairs={{1,640},{3,642},{5,644},{7,646},{9,648},{11,650},{13,652},{15,654}... | collective-permute-start | bytes 552968 | tf_op jit(solution)/shard_map/ppermute | solution.py:345
  1.4 15.0 %collective-permute-start = (bf16[180,128]{1,0:T(8,128)(2,1)S(1)}, bf16[180,128]{1,0:T(8,128)(2,1)S(1)}, u32[]{:S(2)}, u32[]{:S(2)}) collective-permute-start(bf16[180,128]{1,0:T(8,128)(2,1)S(1)} %get-tuple-element.42), channel_id=1, source_target_pairs={{0,641},{2,643},{4,645},{6,647},{8,649},{10,651},{12,653},{14,655}... | collective-permute-start | bytes 138248 | tf_op jit(solution)/shard_map/ppermute | solution.py:345
  2.8 18.3 %collective-permute-start.1 = (bf16[180,128]{1,0:T(8,128)(2,1)S(1)}, bf16[180,128]{1,0:T(8,128)(2,1)S(1)}, u32[]{:S(2)}, u32[]{:S(2)}) collective-permute-start(bf16[180,128]{1,0:T(8,128)(2,1)S(1)} %get-tuple-element.43), channel_id=1, source_target_pairs={{0,97},{2,99},{4,101},{6,103},{8,105},{10,107},{12,109},{14,111},{... | collective-permute-start | bytes 138248 | tf_op jit(solution)/shard_map/ppermute | solution.py:345
  4.0 19.0 %collective-permute-start.2 = (bf16[180,128]{1,0:T(8,128)(2,1)S(1)}, bf16[180,128]{1,0:T(8,128)(2,1)S(1)}, u32[]{:S(2)}, u32[]{:S(2)}) collective-permute-start(bf16[180,128]{1,0:T(8,128)(2,1)S(1)} %get-tuple-element.44), channel_id=1, source_target_pairs={{0,671},{2,641},{4,643},{6,645},{8,647},{10,649},{12,651},{14,653}... | collective-permute-start | bytes 138248 | tf_op jit(solution)/shard_map/ppermute | solution.py:345
  5.3 26.2 %collective-permute-start.3 = (bf16[180,128]{1,0:T(8,128)(2,1)S(1)}, bf16[180,128]{1,0:T(8,128)(2,1)S(1)}, u32[]{:S(2)}, u32[]{:S(2)}) collective-permute-start(bf16[180,128]{1,0:T(8,128)(2,1)S(1)} %get-tuple-element.45.refs_11_), channel_id=1, source_target_pairs={{0,127},{2,97},{4,99},{6,101},{8,103},{10,105},{12,107},{14,109},{... | collective-permute-start | bytes 138248 | tf_op jit(solution)/shard_map/ppermute | solution.py:345
  15.2 21.3 %collective-permute-start.9 = (bf16[180,128]{1,0:T(8,128)(2,1)S(1)}, bf16[180,128]{1,0:T(8,128)(2,1)S(1)}, u32[]{:S(2)}, u32[]{:S(2)}) collective-permute-start(bf16[180,128]{1,0:T(8,128)(2,1)S(1)} %get-tuple-element.71), channel_id=1, source_target_pairs={{640,1},{642,3},{644,5},{646,7},{648,9},{650,11},{652,13},{654,15}... | collective-permute-start | bytes 138248 | tf_op jit(solution)/shard_map/ppermute | solution.py:345
  16.5 21.3 %collective-permute-start.10 = (bf16[180,128]{1,0:T(8,128)(2,1)S(1)}, bf16[180,128]{1,0:T(8,128)(2,1)S(1)}, u32[]{:S(2)}, u32[]{:S(2)}) collective-permute-start(bf16[180,128]{1,0:T(8,128)(2,1)S(1)} %get-tuple-element.72), channel_id=1, source_target_pairs={{640,737},{642,739},{644,741},{646,743},{648,745},{650,747},{652,7... | collective-permute-start | bytes 138248 | tf_op jit(solution)/shard_map/ppermute | solution.py:345
  21.1 18.0 %collective-permute-start.11 = (bf16[180,128]{1,0:T(8,128)(2,1)S(1)}, bf16[180,128]{1,0:T(8,128)(2,1)S(1)}, u32[]{:S(2)}, u32[]{:S(2)}) collective-permute-start(bf16[180,128]{1,0:T(8,128)(2,1)S(1)} %get-tuple-element.73), channel_id=1, source_target_pairs={{640,31},{642,1},{644,3},{646,5},{648,7},{650,9},{652,11},{654,13}... | collective-permute-start | bytes 138248 | tf_op jit(solution)/shard_map/ppermute | solution.py:345
  23.1 17.3 %collective-permute-start.12 = (bf16[180,128]{1,0:T(8,128)(2,1)S(1)}, bf16[180,128]{1,0:T(8,128)(2,1)S(1)}, u32[]{:S(2)}, u32[]{:S(2)}) collective-permute-start(bf16[180,128]{1,0:T(8,128)(2,1)S(1)} %get-tuple-element.74), channel_id=1, source_target_pairs={{640,767},{642,737},{644,739},{646,741},{648,743},{650,745},{652,7... | collective-permute-start | bytes 138248 | tf_op jit(solution)/shard_map/ppermute | solution.py:345
  35.0 29.0 %copy-start = (bf16[288,288]{1,0:T(8,128)(2,1)S(1)}, bf16[288,288]{1,0:T(8,128)(2,1)}, u32[]{:S(2)}) copy-start(bf16[288,288]{1,0:T(8,128)(2,1)} %constant.8.clone.refs_8_) | copy-start | bytes 497668
  35.0 12.9 %collective-permute-start.4 = (bf16[180,128]{1,0:T(8,128)(2,1)S(1)}, bf16[180,128]{1,0:T(8,128)(2,1)S(1)}, u32[]{:S(2)}, u32[]{:S(2)}) collective-permute-start(bf16[180,128]{1,0:T(8,128)(2,1)S(1)} %get-tuple-element.56), channel_id=1, source_target_pairs={{641,34},{643,36},{645,38},{647,40},{649,42},{651,44},{653,46},{65... | collective-permute-start | bytes 138248 | tf_op jit(solution)/shard_map/ppermute | solution.py:345
  36.5 15.9 %collective-permute-start.5 = (bf16[180,128]{1,0:T(8,128)(2,1)S(1)}, bf16[180,128]{1,0:T(8,128)(2,1)S(1)}, u32[]{:S(2)}, u32[]{:S(2)}) collective-permute-start(bf16[180,128]{1,0:T(8,128)(2,1)S(1)} %get-tuple-element.57), channel_id=1, source_target_pairs={{641,2},{643,4},{645,6},{647,8},{649,10},{651,12},{653,14},{655,16... | collective-permute-start | bytes 138248 | tf_op jit(solution)/shard_map/ppermute | solution.py:345
  37.8 17.4 %collective-permute-start.6 = (bf16[180,128]{1,0:T(8,128)(2,1)S(1)}, bf16[180,128]{1,0:T(8,128)(2,1)S(1)}, u32[]{:S(2)}, u32[]{:S(2)}) collective-permute-start(bf16[180,128]{1,0:T(8,128)(2,1)S(1)} %get-tuple-element.58), channel_id=1, source_target_pairs={{641,32},{643,34},{645,36},{647,38},{649,40},{651,42},{653,44},{65... | collective-permute-start | bytes 138248 | tf_op jit(solution)/shard_map/ppermute | solution.py:345
  39.1 16.1 %collective-permute-start.7 = (bf16[180,128]{1,0:T(8,128)(2,1)S(1)}, bf16[180,128]{1,0:T(8,128)(2,1)S(1)}, u32[]{:S(2)}, u32[]{:S(2)}) collective-permute-start(bf16[180,128]{1,0:T(8,128)(2,1)S(1)} %get-tuple-element.59), channel_id=1, source_target_pairs={{641,0},{643,2},{645,4},{647,6},{649,8},{651,10},{653,12},{655,14}... | collective-permute-start | bytes 138248 | tf_op jit(solution)/shard_map/ppermute | solution.py:345
  43.9 12.7 %collective-permute-start.13 = (bf16[180,128]{1,0:T(8,128)(2,1)S(1)}, bf16[180,128]{1,0:T(8,128)(2,1)S(1)}, u32[]{:S(2)}, u32[]{:S(2)}) collective-permute-start(bf16[180,128]{1,0:T(8,128)(2,1)S(1)} %get-tuple-element.75), channel_id=1, source_target_pairs={{1,35},{3,37},{5,39},{7,41},{9,43},{11,45},{13,47},{15,49},{17,51}... | collective-permute-start | bytes 138248 | tf_op jit(solution)/shard_map/ppermute | solution.py:345
  47.9 8.6 %collective-permute-start.14 = (bf16[180,128]{1,0:T(8,128)(2,1)S(1)}, bf16[180,128]{1,0:T(8,128)(2,1)S(1)}, u32[]{:S(2)}, u32[]{:S(2)}) collective-permute-start(bf16[180,128]{1,0:T(8,128)(2,1)S(1)} %get-tuple-element.76), channel_id=1, source_target_pairs={{1,3},{3,5},{5,7},{7,9},{9,11},{11,13},{13,15},{15,17},{17,19},{19... | collective-permute-start | bytes 138248 | tf_op jit(solution)/shard_map/ppermute | solution.py:345
  52.3 11.7 %collective-permute-start.15 = (bf16[180,128]{1,0:T(8,128)(2,1)S(1)}, bf16[180,128]{1,0:T(8,128)(2,1)S(1)}, u32[]{:S(2)}, u32[]{:S(2)}) collective-permute-start(bf16[180,128]{1,0:T(8,128)(2,1)S(1)} %get-tuple-element.77), channel_id=1, source_target_pairs={{1,33},{3,35},{5,37},{7,39},{9,41},{11,43},{13,45},{15,47},{17,49}... | collective-permute-start | bytes 138248 | tf_op jit(solution)/shard_map/ppermute | solution.py:345

commit v4 on v3

--- a/solution.py
+++ b/solution.py
@@ -290,7 +290,7 @@
 
     section = lax.axis_index("section")
     pl.when(section == 0)(lambda: place(refs[0:4]))
-    pl.when(section == 1)(lambda: place(refs[4:8]))
+    pl.when(section == 1)(lambda: place([refs[6], refs[4], refs[7], refs[5]]))
 
 
 def call(kernel, operands, places, outs, scratch, flops):
@@ -332,6 +332,10 @@
 
 def straight(lon):
     return lon
+
+
+def eastward(lon):
+    return (lon + 1) % lax.axis_size("lon")
 
 
 def send(block, sections, steps, source_at, target_at):
@@ -416,7 +420,7 @@
         BLOCK_SCRATCH,
         BLOCK_FLOPS,
     )
-    other_shifted = to_shifted(other_first, mirrored, straight)
+    other_shifted = to_shifted(other_first, mirrored, eastward)
     block_two = functools.partial(
         call,
         second_kernel,
@@ -432,13 +436,12 @@
     ]
     other_done = block_two((*other_shifted, *params_two, addend_two))
     across, along, upward = [
-        send(other_done[3 - q], (1, 1), (1 - q // 2, 1 - q % 2), straight, straight)
-        for q in (0, 2, 1)
-    ]
-    other_back = (across, upward, along)
+        send(other_done[3 - q], (1, 1), (1 - q // 2, 1 - q % 2), eastward, straight)
+        for q in (1, 3, 0)
+    ]
     placed = call(
         place_kernel,
-        (*own_back, *other_back, other_done[0], jnp.asarray(place_matrix())),
+        (*own_back, across, along, upward, other_done[1], jnp.asarray(place_matrix())),
         "v" * 9,
         jax.ShapeDtypeStruct(patch.shape, patch.dtype),
         [pltpu.VMEM((2 * WIN, C), jnp.float32)],

time: 65.5 us -> 64.9 us (level)
  the two profiles are of different devices: /device:TPU:401 before, /device:TPU:25 now
where the time goes in v4:
time: 64.9 us; the launch traced here: 64.5 us
  starting transfers between devices  33.7 us (52%)
  waiting for transfers between devices  17.9 us (28%)
  Pallas kernels  12.6 us (19%)
    ppermute x16, starting transfers between devices, send(): return lax.ppermute(block, AXES, route)  33.7 us
    ppermute x16, waiting for transfers between devices, send(): return lax.ppermute(block, AXES, route)  17.9 us
    pallas_call x6, Pallas kernels, call(): pl.pallas_call(kernel, out_shape=outs, in_specs=[pl.BlockSpec(memory_spac...  12.6 us
  transfers between devices with their start and end apart: 16, of which 3 were waited for; matrix products, arithmetic and copies ran while one was open for 0% of the time, Pallas kernels for 18%

profile of v4, /device:TPU:25, one launch (start us, length us, event | category | flops | bytes accessed | tf_op | source)
XLA Modules:
  0.0 64.5 jit_solution(11157869030520144376)
XLA Ops:
  0.0 1.3 %collective-permute-start.8 = (bf16[1,6,12,4,320]{4,3,2,1,0:T(4,128)(2,1)}, bf16[1,6,12,4,320]{4,3,2,1,0:T(4,128)(2,1)S(1)}, u32[]{:S(2)}, u32[]{:S(2)}) collective-permute-start(bf16[1,6,12,4,320]{4,3,2,1,0:T(4,128)(2,1)} %bitcast.8), channel_id=1, source_target_pairs={{1,640},{3,642},{5,644},{7,646},{9,648},{11,650},{13,652},{15,654}... | collective-permute-start | bytes 552968 | tf_op jit(solution)/shard_map/ppermute | solution.py:349
  1.3 7.5 %shard_map.136 = (bf16[180,128]{1,0:T(8,128)(2,1)S(1)}, bf16[180,128]{1,0:T(8,128)(2,1)S(1)}, bf16[180,128]{1,0:T(8,128)(2,1)S(1)}, bf16[180,128]{1,0:T(8,128)(2...) custom-call(bf16[1,6,12,4,320]{4,3,2,1,0:T(4,128)(2,1)} %bitcast.9, ...), custom_call_target="tpu_custom_call" | custom-call | flops 800000000 | bytes 4000000 | tf_op jit(solution)/shard_map/pallas_call | solution.py:302
  8.8 7.0 %collective-permute-start = (bf16[180,128]{1,0:T(8,128)(2,1)S(1)}, bf16[180,128]{1,0:T(8,128)(2,1)S(1)}, u32[]{:S(2)}, u32[]{:S(2)}) collective-permute-start(bf16[180,128]{1,0:T(8,128)(2,1)S(1)} %get-tuple-element.42), channel_id=1, source_target_pairs={{0,641},{2,643},{4,645},{6,647},{8,649},{10,651},{12,653},{14,655}... | collective-permute-start | bytes 138248 | tf_op jit(solution)/shard_map/ppermute | solution.py:349
  15.8 4.0 %collective-permute-start.1 = (bf16[180,128]{1,0:T(8,128)(2,1)S(1)}, bf16[180,128]{1,0:T(8,128)(2,1)S(1)}, u32[]{:S(2)}, u32[]{:S(2)}) collective-permute-start(bf16[180,128]{1,0:T(8,128)(2,1)S(1)} %get-tuple-element.43), channel_id=1, source_target_pairs={{0,97},{2,99},{4,101},{6,103},{8,105},{10,107},{12,109},{14,111},{... | collective-permute-start | bytes 138248 | tf_op jit(solution)/shard_map/ppermute | solution.py:349
  19.8 1.3 %collective-permute-start.2 = (bf16[180,128]{1,0:T(8,128)(2,1)S(1)}, bf16[180,128]{1,0:T(8,128)(2,1)S(1)}, u32[]{:S(2)}, u32[]{:S(2)}) collective-permute-start(bf16[180,128]{1,0:T(8,128)(2,1)S(1)} %get-tuple-element.44), channel_id=1, source_target_pairs={{0,671},{2,641},{4,643},{6,645},{8,647},{10,649},{12,651},{14,653}... | collective-permute-start | bytes 138248 | tf_op jit(solution)/shard_map/ppermute | solution.py:349
  21.1 2.1 %collective-permute-start.3 = (bf16[180,128]{1,0:T(8,128)(2,1)S(1)}, bf16[180,128]{1,0:T(8,128)(2,1)S(1)}, u32[]{:S(2)}, u32[]{:S(2)}) collective-permute-start(bf16[180,128]{1,0:T(8,128)(2,1)S(1)} %get-tuple-element.45.refs_11_), channel_id=1, source_target_pairs={{0,127},{2,97},{4,99},{6,101},{8,103},{10,105},{12,107},{14,109},{... | collective-permute-start | bytes 138248 | tf_op jit(solution)/shard_map/ppermute | solution.py:349
  23.2 0.1 shard_map.137
  23.4 5.9 %collective-permute-done.8.refs_0_ = bf16[1,6,12,4,320]{4,3,2,1,0:T(4,128)(2,1)S(1)} collective-permute-done((bf16[1,6,12,4,320]{4,3,2,1,0:T(4,128)(2,1)}, bf16[1,6,12,4,320]{4,3,2,1,0:T(4,128)(2,1)S(1)}, u32[]{:S(2)}, u32[]{:S(2)}) %collective-permute-start.8) | collective-permute-done | bytes 184352 | tf_op jit(solution)/shard_map/ppermute | solution.py:349
  29.2 3.7 %shard_map.139 = (bf16[180,128]{1,0:T(8,128)(2,1)S(1)}, bf16[180,128]{1,0:T(8,128)(2,1)S(1)}, bf16[180,128]{1,0:T(8,128)(2,1)S(1)}, bf16[180,128]{1,0:T(8,128)(2,1)S(1)}) custom-call(bf16[1,6,12,4,320]{4,3,2,1,0:T(4,128)(2,1)S(1)} %collective-permute-done.8.refs_0_, bf16[288,288]{1,0:T(8,128)(2,1)S(1)} %get-tuple-element.60.refs_1_, ...), custom_call_target="tpu_custom_call" | custom-call | flops 800000000 | bytes 4000000 | tf_op jit(solution)/shard_map/pallas_call | solution.py:302
  32.9 1.3 %collective-permute-start.9 = (bf16[180,128]{1,0:T(8,128)(2,1)S(1)}, bf16[180,128]{1,0:T(8,128)(2,1)S(1)}, u32[]{:S(2)}, u32[]{:S(2)}) collective-permute-start(bf16[180,128]{1,0:T(8,128)(2,1)S(1)} %get-tuple-element.71), channel_id=1, source_target_pairs={{640,33},{642,35},{644,37},{646,39},{648,41},{650,43},{652,45},{65... | collective-permute-start | bytes 138248 | tf_op jit(solution)/shard_map/ppermute | solution.py:349
  34.2 0.0 collective-permute-done.refs_0_
  34.2 1.3 %collective-permute-start.10 = (bf16[180,128]{1,0:T(8,128)(2,1)S(1)}, bf16[180,128]{1,0:T(8,128)(2,1)S(1)}, u32[]{:S(2)}, u32[]{:S(2)}) collective-permute-start(bf16[180,128]{1,0:T(8,128)(2,1)S(1)} %get-tuple-element.72), channel_id=1, source_target_pairs={{640,1},{642,3},{644,5},{646,7},{648,9},{650,11},{652,13},{654,15}... | collective-permute-start | bytes 138248 | tf_op jit(solution)/shard_map/ppermute | solution.py:349
  35.5 0.0 collective-permute-done.1.refs_1_
  35.5 1.3 %collective-permute-start.11 = (bf16[180,128]{1,0:T(8,128)(2,1)S(1)}, bf16[180,128]{1,0:T(8,128)(2,1)S(1)}, u32[]{:S(2)}, u32[]{:S(2)}) collective-permute-start(bf16[180,128]{1,0:T(8,128)(2,1)S(1)} %get-tuple-element.73), channel_id=1, source_target_pairs={{640,63},{642,33},{644,35},{646,37},{648,39},{650,41},{652,43},{65... | collective-permute-start | bytes 138248 | tf_op jit(solution)/shard_map/ppermute | solution.py:349
  36.8 0.0 collective-permute-done.2.refs_2_
  36.8 6.9 %collective-permute-start.12 = (bf16[180,128]{1,0:T(8,128)(2,1)S(1)}, bf16[180,128]{1,0:T(8,128)(2,1)S(1)}, u32[]{:S(2)}, u32[]{:S(2)}) collective-permute-start(bf16[180,128]{1,0:T(8,128)(2,1)S(1)} %get-tuple-element.74), channel_id=1, source_target_pairs={{640,31},{642,1},{644,3},{646,5},{648,7},{650,9},{652,11},{654,13}... | collective-permute-start | bytes 138248 | tf_op jit(solution)/shard_map/ppermute | solution.py:349
  43.7 0.0 collective-permute-done.3.refs_3_
  43.7 0.2 shard_map.138
  43.9 0.0 copy-start
  44.0 1.4 %collective-permute-start.4 = (bf16[180,128]{1,0:T(8,128)(2,1)S(1)}, bf16[180,128]{1,0:T(8,128)(2,1)S(1)}, u32[]{:S(2)}, u32[]{:S(2)}) collective-permute-start(bf16[180,128]{1,0:T(8,128)(2,1)S(1)} %get-tuple-element.56), channel_id=1, source_target_pairs={{641,34},{643,36},{645,38},{647,40},{649,42},{651,44},{653,46},{65... | collective-permute-start | bytes 138248 | tf_op jit(solution)/shard_map/ppermute | solution.py:349
  45.4 0.0 collective-permute-done.9.refs_0_
  45.4 1.3 %collective-permute-start.5 = (bf16[180,128]{1,0:T(8,128)(2,1)S(1)}, bf16[180,128]{1,0:T(8,128)(2,1)S(1)}, u32[]{:S(2)}, u32[]{:S(2)}) collective-permute-start(bf16[180,128]{1,0:T(8,128)(2,1)S(1)} %get-tuple-element.57), channel_id=1, source_target_pairs={{641,2},{643,4},{645,6},{647,8},{649,10},{651,12},{653,14},{655,16... | collective-permute-start | bytes 138248 | tf_op jit(solution)/shard_map/ppermute | solution.py:349
  46.7 0.0 collective-permute-done.10.refs_1_
  46.7 1.3 %collective-permute-start.6 = (bf16[180,128]{1,0:T(8,128)(2,1)S(1)}, bf16[180,128]{1,0:T(8,128)(2,1)S(1)}, u32[]{:S(2)}, u32[]{:S(2)}) collective-permute-start(bf16[180,128]{1,0:T(8,128)(2,1)S(1)} %get-tuple-element.58), channel_id=1, source_target_pairs={{641,32},{643,34},{645,36},{647,38},{649,40},{651,42},{653,44},{65... | collective-permute-start | bytes 138248 | tf_op jit(solution)/shard_map/ppermute | solution.py:349
  48.0 0.0 collective-permute-done.11.refs_2_
  48.0 1.3 %collective-permute-start.7 = (bf16[180,128]{1,0:T(8,128)(2,1)S(1)}, bf16[180,128]{1,0:T(8,128)(2,1)S(1)}, u32[]{:S(2)}, u32[]{:S(2)}) collective-permute-start(bf16[180,128]{1,0:T(8,128)(2,1)S(1)} %get-tuple-element.59), channel_id=1, source_target_pairs={{641,0},{643,2},{645,4},{647,6},{649,8},{651,10},{653,12},{655,14}... | collective-permute-start | bytes 138248 | tf_op jit(solution)/shard_map/ppermute | solution.py:349
  49.3 0.0 collective-permute-done.12.refs_3_
  49.4 0.7 %collective-permute-start.13 = (bf16[180,128]{1,0:T(8,128)(2,1)S(1)}, bf16[180,128]{1,0:T(8,128)(2,1)S(1)}, u32[]{:S(2)}, u32[]{:S(2)}) collective-permute-start(bf16[180,128]{1,0:T(8,128)(2,1)S(1)} %get-tuple-element.75), channel_id=1, source_target_pairs={{33,3},{35,5},{37,7},{39,9},{41,11},{43,13},{45,15},{47,17},{49,19... | collective-permute-start | bytes 138248 | tf_op jit(solution)/shard_map/ppermute | solution.py:349
  50.0 7.9 %collective-permute-done.4.refs_0_ = bf16[180,128]{1,0:T(8,128)(2,1)S(1)} collective-permute-done((bf16[180,128]{1,0:T(8,128)(2,1)S(1)}, bf16[180,128]{1,0:T(8,128)(2,1)S(1)}, u32[]{:S(2)}, u32[]{:S(2)}) %collective-permute-start.4) | collective-permute-done | bytes 46112 | tf_op jit(solution)/shard_map/ppermute | solution.py:349
  57.9 0.7 %collective-permute-start.14 = (bf16[180,128]{1,0:T(8,128)(2,1)S(1)}, bf16[180,128]{1,0:T(8,128)(2,1)S(1)}, u32[]{:S(2)}, u32[]{:S(2)}) collective-permute-start(bf16[180,128]{1,0:T(8,128)(2,1)S(1)} %get-tuple-element.76), channel_id=1, source_target_pairs={{33,1},{35,3},{37,5},{39,7},{41,9},{43,11},{45,13},{47,15},{49,17}... | collective-permute-start | bytes 138248 | tf_op jit(solution)/shard_map/ppermute | solution.py:349
  58.6 0.0 collective-permute-done.5.refs_1_
  58.6 0.7 %collective-permute-start.15 = (bf16[180,128]{1,0:T(8,128)(2,1)S(1)}, bf16[180,128]{1,0:T(8,128)(2,1)S(1)}, u32[]{:S(2)}, u32[]{:S(2)}) collective-permute-start(bf16[180,128]{1,0:T(8,128)(2,1)S(1)} %get-tuple-element.77), channel_id=1, source_target_pairs={{33,35},{35,37},{37,39},{39,41},{41,43},{43,45},{45,47},{47,49},{4... | collective-permute-start | bytes 138248 | tf_op jit(solution)/shard_map/ppermute | solution.py:349
  59.2 4.1 %collective-permute-done.6.refs_2_ = bf16[180,128]{1,0:T(8,128)(2,1)S(1)} collective-permute-done((bf16[180,128]{1,0:T(8,128)(2,1)S(1)}, bf16[180,128]{1,0:T(8,128)(2,1)S(1)}, u32[]{:S(2)}, u32[]{:S(2)}) %collective-permute-start.6) | collective-permute-done | bytes 46112 | tf_op jit(solution)/shard_map/ppermute | solution.py:349
  63.4 0.0 collective-permute-done.7.refs_3_
  63.4 0.0 collective-permute-done.13.refs_4_
  63.4 0.0 collective-permute-done.14.refs_5_
  63.4 0.0 collective-permute-done.15.refs_6_
  63.4 0.0 copy-done
  63.4 1.1 %shard_map.141 = bf16[1,6,12,4,320]{4,3,2,1,0:T(4,128)(2,1)} custom-call(bf16[180,128]{1,0:T(8,128)(2,1)S(1)} %collective-permute-done.4.refs_0_, bf16[180,128]{1,0:T(8,128)(2,1)S(1)} %collective-permute-done.5.refs_1_, bf16[180,128]{1,0:T(8,128)(2,1)S(1)} %collective-permute-done.6.refs_2_, bf16[180,128]{1,0:T(8,128)(2,1)S(1)} %collective-permute-done.7.refs_3_, ...), custom_call_target="tpu_custom_call" | custom-call | flops 1000000 | bytes 4000000 | tf_op jit(solution)/shard_map/pallas_call | solution.py:302
  (1 shorter events, 0.0 us)
Async XLA Ops:
  0.0 29.2 %collective-permute-start.8 = (bf16[1,6,12,4,320]{4,3,2,1,0:T(4,128)(2,1)}, bf16[1,6,12,4,320]{4,3,2,1,0:T(4,128)(2,1)S(1)}, u32[]{:S(2)}, u32[]{:S(2)}) collective-permute-start(bf16[1,6,12,4,320]{4,3,2,1,0:T(4,128)(2,1)} %bitcast.8), channel_id=1, source_target_pairs={{1,640},{3,642},{5,644},{7,646},{9,648},{11,650},{13,652},{15,654}... | collective-permute-start | bytes 552968 | tf_op jit(solution)/shard_map/ppermute | solution.py:349
  8.8 25.4 %collective-permute-start = (bf16[180,128]{1,0:T(8,128)(2,1)S(1)}, bf16[180,128]{1,0:T(8,128)(2,1)S(1)}, u32[]{:S(2)}, u32[]{:S(2)}) collective-permute-start(bf16[180,128]{1,0:T(8,128)(2,1)S(1)} %get-tuple-element.42), channel_id=1, source_target_pairs={{0,641},{2,643},{4,645},{6,647},{8,649},{10,651},{12,653},{14,655}... | collective-permute-start | bytes 138248 | tf_op jit(solution)/shard_map/ppermute | solution.py:349
  15.8 19.7 %collective-permute-start.1 = (bf16[180,128]{1,0:T(8,128)(2,1)S(1)}, bf16[180,128]{1,0:T(8,128)(2,1)S(1)}, u32[]{:S(2)}, u32[]{:S(2)}) collective-permute-start(bf16[180,128]{1,0:T(8,128)(2,1)S(1)} %get-tuple-element.43), channel_id=1, source_target_pairs={{0,97},{2,99},{4,101},{6,103},{8,105},{10,107},{12,109},{14,111},{... | collective-permute-start | bytes 138248 | tf_op jit(solution)/shard_map/ppermute | solution.py:349
  19.8 17.0 %collective-permute-start.2 = (bf16[180,128]{1,0:T(8,128)(2,1)S(1)}, bf16[180,128]{1,0:T(8,128)(2,1)S(1)}, u32[]{:S(2)}, u32[]{:S(2)}) collective-permute-start(bf16[180,128]{1,0:T(8,128)(2,1)S(1)} %get-tuple-element.44), channel_id=1, source_target_pairs={{0,671},{2,641},{4,643},{6,645},{8,647},{10,649},{12,651},{14,653}... | collective-permute-start | bytes 138248 | tf_op jit(solution)/shard_map/ppermute | solution.py:349
  21.1 22.6 %collective-permute-start.3 = (bf16[180,128]{1,0:T(8,128)(2,1)S(1)}, bf16[180,128]{1,0:T(8,128)(2,1)S(1)}, u32[]{:S(2)}, u32[]{:S(2)}) collective-permute-start(bf16[180,128]{1,0:T(8,128)(2,1)S(1)} %get-tuple-element.45.refs_11_), channel_id=1, source_target_pairs={{0,127},{2,97},{4,99},{6,101},{8,103},{10,105},{12,107},{14,109},{... | collective-permute-start | bytes 138248 | tf_op jit(solution)/shard_map/ppermute | solution.py:349
  32.9 12.5 %collective-permute-start.9 = (bf16[180,128]{1,0:T(8,128)(2,1)S(1)}, bf16[180,128]{1,0:T(8,128)(2,1)S(1)}, u32[]{:S(2)}, u32[]{:S(2)}) collective-permute-start(bf16[180,128]{1,0:T(8,128)(2,1)S(1)} %get-tuple-element.71), channel_id=1, source_target_pairs={{640,33},{642,35},{644,37},{646,39},{648,41},{650,43},{652,45},{65... | collective-permute-start | bytes 138248 | tf_op jit(solution)/shard_map/ppermute | solution.py:349
  34.2 12.5 %collective-permute-start.10 = (bf16[180,128]{1,0:T(8,128)(2,1)S(1)}, bf16[180,128]{1,0:T(8,128)(2,1)S(1)}, u32[]{:S(2)}, u32[]{:S(2)}) collective-permute-start(bf16[180,128]{1,0:T(8,128)(2,1)S(1)} %get-tuple-element.72), channel_id=1, source_target_pairs={{640,1},{642,3},{644,5},{646,7},{648,9},{650,11},{652,13},{654,15}... | collective-permute-start | bytes 138248 | tf_op jit(solution)/shard_map/ppermute | solution.py:349
  35.5 12.5 %collective-permute-start.11 = (bf16[180,128]{1,0:T(8,128)(2,1)S(1)}, bf16[180,128]{1,0:T(8,128)(2,1)S(1)}, u32[]{:S(2)}, u32[]{:S(2)}) collective-permute-start(bf16[180,128]{1,0:T(8,128)(2,1)S(1)} %get-tuple-element.73), channel_id=1, source_target_pairs={{640,63},{642,33},{644,35},{646,37},{648,39},{650,41},{652,43},{65... | collective-permute-start | bytes 138248 | tf_op jit(solution)/shard_map/ppermute | solution.py:349
  36.8 12.5 %collective-permute-start.12 = (bf16[180,128]{1,0:T(8,128)(2,1)S(1)}, bf16[180,128]{1,0:T(8,128)(2,1)S(1)}, u32[]{:S(2)}, u32[]{:S(2)}) collective-permute-start(bf16[180,128]{1,0:T(8,128)(2,1)S(1)} %get-tuple-element.74), channel_id=1, source_target_pairs={{640,31},{642,1},{644,3},{646,5},{648,7},{650,9},{652,11},{654,13}... | collective-permute-start | bytes 138248 | tf_op jit(solution)/shard_map/ppermute | solution.py:349
  43.9 19.5 %copy-start = (bf16[288,288]{1,0:T(8,128)(2,1)S(1)}, bf16[288,288]{1,0:T(8,128)(2,1)}, u32[]{:S(2)}) copy-start(bf16[288,288]{1,0:T(8,128)(2,1)} %constant.8.clone.refs_8_) | copy-start | bytes 497668
  44.0 13.9 %collective-permute-start.4 = (bf16[180,128]{1,0:T(8,128)(2,1)S(1)}, bf16[180,128]{1,0:T(8,128)(2,1)S(1)}, u32[]{:S(2)}, u32[]{:S(2)}) collective-permute-start(bf16[180,128]{1,0:T(8,128)(2,1)S(1)} %get-tuple-element.56), channel_id=1, source_target_pairs={{641,34},{643,36},{645,38},{647,40},{649,42},{651,44},{653,46},{65... | collective-permute-start | bytes 138248 | tf_op jit(solution)/shard_map/ppermute | solution.py:349
  45.4 13.2 %collective-permute-start.5 = (bf16[180,128]{1,0:T(8,128)(2,1)S(1)}, bf16[180,128]{1,0:T(8,128)(2,1)S(1)}, u32[]{:S(2)}, u32[]{:S(2)}) collective-permute-start(bf16[180,128]{1,0:T(8,128)(2,1)S(1)} %get-tuple-element.57), channel_id=1, source_target_pairs={{641,2},{643,4},{645,6},{647,8},{649,10},{651,12},{653,14},{655,16... | collective-permute-start | bytes 138248 | tf_op jit(solution)/shard_map/ppermute | solution.py:349
  46.7 16.7 %collective-permute-start.6 = (bf16[180,128]{1,0:T(8,128)(2,1)S(1)}, bf16[180,128]{1,0:T(8,128)(2,1)S(1)}, u32[]{:S(2)}, u32[]{:S(2)}) collective-permute-start(bf16[180,128]{1,0:T(8,128)(2,1)S(1)} %get-tuple-element.58), channel_id=1, source_target_pairs={{641,32},{643,34},{645,36},{647,38},{649,40},{651,42},{653,44},{65... | collective-permute-start | bytes 138248 | tf_op jit(solution)/shard_map/ppermute | solution.py:349
  48.0 15.4 %collective-permute-start.7 = (bf16[180,128]{1,0:T(8,128)(2,1)S(1)}, bf16[180,128]{1,0:T(8,128)(2,1)S(1)}, u32[]{:S(2)}, u32[]{:S(2)}) collective-permute-start(bf16[180,128]{1,0:T(8,128)(2,1)S(1)} %get-tuple-element.59), channel_id=1, source_target_pairs={{641,0},{643,2},{645,4},{647,6},{649,8},{651,10},{653,12},{655,14}... | collective-permute-start | bytes 138248 | tf_op jit(solution)/shard_map/ppermute | solution.py:349
  49.4 14.0 %collective-permute-start.13 = (bf16[180,128]{1,0:T(8,128)(2,1)S(1)}, bf16[180,128]{1,0:T(8,128)(2,1)S(1)}, u32[]{:S(2)}, u32[]{:S(2)}) collective-permute-start(bf16[180,128]{1,0:T(8,128)(2,1)S(1)} %get-tuple-element.75), channel_id=1, source_target_pairs={{33,3},{35,5},{37,7},{39,9},{41,11},{43,13},{45,15},{47,17},{49,19... | collective-permute-start | bytes 138248 | tf_op jit(solution)/shard_map/ppermute | solution.py:349
  57.9 5.5 %collective-permute-start.14 = (bf16[180,128]{1,0:T(8,128)(2,1)S(1)}, bf16[180,128]{1,0:T(8,128)(2,1)S(1)}, u32[]{:S(2)}, u32[]{:S(2)}) collective-permute-start(bf16[180,128]{1,0:T(8,128)(2,1)S(1)} %get-tuple-element.76), channel_id=1, source_target_pairs={{33,1},{35,3},{37,5},{39,7},{41,9},{43,11},{45,13},{47,15},{49,17}... | collective-permute-start | bytes 138248 | tf_op jit(solution)/shard_map/ppermute | solution.py:349
  58.6 4.8 %collective-permute-start.15 = (bf16[180,128]{1,0:T(8,128)(2,1)S(1)}, bf16[180,128]{1,0:T(8,128)(2,1)S(1)}, u32[]{:S(2)}, u32[]{:S(2)}) collective-permute-start(bf16[180,128]{1,0:T(8,128)(2,1)S(1)} %get-tuple-element.77), channel_id=1, source_target_pairs={{33,35},{35,37},{37,39},{39,41},{41,43},{43,45},{45,47},{47,49},{4... | collective-permute-start | bytes 138248 | tf_op jit(solution)/shard_map/ppermute | solution.py:349

commit v5 on v4

--- a/solution.py
+++ b/solution.py
@@ -338,6 +338,10 @@
     return (lon + 1) % lax.axis_size("lon")
 
 
+def mirrored_eastward(lon):
+    return mirrored(eastward(lon))
+
+
 def send(block, sections, steps, source_at, target_at):
     lons, lats = lax.axis_size("lon"), lax.axis_size("lat")
     route = []
@@ -403,7 +407,7 @@
         BLOCK_FLOPS,
     )
     own_first, (addend_one, arranging), params_one = made[:4], made[4:6], made[6:]
-    own_shifted = to_shifted(own_first, straight, mirrored)
+    own_shifted = to_shifted(own_first, straight, mirrored_eastward)
     addend_two, *params_two = call(
         prepare_kernel,
         (table, spread, *params, own_first[0]),
@@ -431,7 +435,7 @@
     )
     own_done = block_two((*own_shifted, *params_two, addend_two))
     own_back = [
-        send(own_done[3 - q], (1, 0), (1 - q // 2, 1 - q % 2), mirrored, straight)
+        send(own_done[3 - q], (1, 0), (1 - q // 2, 1 - q % 2), mirrored_eastward, straight)
         for q in range(4)
     ]
     other_done = block_two((*other_shifted, *params_two, addend_two))

time: 64.9 us -> 61.9 us (0.954)
  the two profiles are of different devices: /device:TPU:25 before, /device:TPU:384 now
where the time goes in v5:
time: 61.9 us; the launch traced here: 61.5 us
  starting transfers between devices  32.1 us (52%)
  waiting for transfers between devices  16.3 us (26%)
  Pallas kernels  12.9 us (21%)
    ppermute x16, starting transfers between devices, send(): return lax.ppermute(block, AXES, route)  32.1 us
    ppermute x16, waiting for transfers between devices, send(): return lax.ppermute(block, AXES, route)  16.3 us
    pallas_call x6, Pallas kernels, call(): pl.pallas_call(kernel, out_shape=outs, in_specs=[pl.BlockSpec(memory_spac...  12.9 us
  transfers between devices with their start and end apart: 16, of which 4 were waited for; matrix products, arithmetic and copies ran while one was open for 0% of the time, Pallas kernels for 19%

profile of v5, /device:TPU:384, one launch (start us, length us, event | category | flops | bytes accessed | tf_op | source)
XLA Modules:
  0.0 61.5 jit_solution(9172504678984832535)
XLA Ops:
  0.0 1.6 %collective-permute-start.8 = (bf16[1,6,12,4,320]{4,3,2,1,0:T(4,128)(2,1)}, bf16[1,6,12,4,320]{4,3,2,1,0:T(4,128)(2,1)S(1)}, u32[]{:S(2)}, u32[]{:S(2)}) collective-permute-start(bf16[1,6,12,4,320]{4,3,2,1,0:T(4,128)(2,1)} %bitcast.8), channel_id=1, source_target_pairs={{1,640},{3,642},{5,644},{7,646},{9,648},{11,650},{13,652},{15,654}... | collective-permute-start | bytes 552968 | tf_op jit(solution)/shard_map/ppermute | solution.py:353
  1.6 0.1 shard_map.136
  1.7 1.3 %collective-permute-start = (bf16[180,128]{1,0:T(8,128)(2,1)S(1)}, bf16[180,128]{1,0:T(8,128)(2,1)S(1)}, u32[]{:S(2)}, u32[]{:S(2)}) collective-permute-start(bf16[180,128]{1,0:T(8,128)(2,1)S(1)} %get-tuple-element.42), channel_id=1, source_target_pairs={{0,673},{2,675},{4,677},{6,679},{8,681},{10,683},{12,685},{14,687}... | collective-permute-start | bytes 138248 | tf_op jit(solution)/shard_map/ppermute | solution.py:353
  3.0 1.3 %collective-permute-start.1 = (bf16[180,128]{1,0:T(8,128)(2,1)S(1)}, bf16[180,128]{1,0:T(8,128)(2,1)S(1)}, u32[]{:S(2)}, u32[]{:S(2)}) collective-permute-start(bf16[180,128]{1,0:T(8,128)(2,1)S(1)} %get-tuple-element.43), channel_id=1, source_target_pairs={{0,641},{2,643},{4,645},{6,647},{8,649},{10,651},{12,653},{14,655}... | collective-permute-start | bytes 138248 | tf_op jit(solution)/shard_map/ppermute | solution.py:353
  4.3 1.3 %collective-permute-start.2 = (bf16[180,128]{1,0:T(8,128)(2,1)S(1)}, bf16[180,128]{1,0:T(8,128)(2,1)S(1)}, u32[]{:S(2)}, u32[]{:S(2)}) collective-permute-start(bf16[180,128]{1,0:T(8,128)(2,1)S(1)} %get-tuple-element.44), channel_id=1, source_target_pairs={{0,703},{2,673},{4,675},{6,677},{8,679},{10,681},{12,683},{14,685}... | collective-permute-start | bytes 138248 | tf_op jit(solution)/shard_map/ppermute | solution.py:353
  5.6 1.3 %collective-permute-start.3 = (bf16[180,128]{1,0:T(8,128)(2,1)S(1)}, bf16[180,128]{1,0:T(8,128)(2,1)S(1)}, u32[]{:S(2)}, u32[]{:S(2)}) collective-permute-start(bf16[180,128]{1,0:T(8,128)(2,1)S(1)} %get-tuple-element.45.refs_11_), channel_id=1, source_target_pairs={{0,671},{2,641},{4,643},{6,645},{8,647},{10,649},{12,651},{14,653}... | collective-permute-start | bytes 138248 | tf_op jit(solution)/shard_map/ppermute | solution.py:353
  6.9 4.7 %shard_map.137 = (f32[2,2880,128]{2,1,0:T(8,128)S(1)}, bf16[1,2,320]{2,1,0:T(2,128)(2,1)S(1)}, bf16[1,2,320]{2,1,0:T(2,128)(2,1)S(1)}, bf16[1,320,960]{2,1,0:T(8...) custom-call(bf16[1,1,10,2,3312]{4,3,2,1,0:T(2,128)(2,1)} %bitcast.7,, ...), custom_call_target="tpu_custom_call" | custom-call | flops 200000000 | bytes 4000000 | tf_op jit(solution)/shard_map/pallas_call | solution.py:302
  11.6 4.4 %collective-permute-done.8.refs_0_ = bf16[1,6,12,4,320]{4,3,2,1,0:T(4,128)(2,1)S(1)} collective-permute-done((bf16[1,6,12,4,320]{4,3,2,1,0:T(4,128)(2,1)}, bf16[1,6,12,4,320]{4,3,2,1,0:T(4,128)(2,1)S(1)}, u32[]{:S(2)}, u32[]{:S(2)}) %collective-permute-start.8) | collective-permute-done | bytes 184352 | tf_op jit(solution)/shard_map/ppermute | solution.py:353
  16.0 1.3 %collective-permute-start.9 = (bf16[180,128]{1,0:T(8,128)(2,1)S(1)}, bf16[180,128]{1,0:T(8,128)(2,1)S(1)}, u32[]{:S(2)}, u32[]{:S(2)}) collective-permute-start(bf16[180,128]{1,0:T(8,128)(2,1)S(1)} %get-tuple-element.71), channel_id=1, source_target_pairs={{640,33},{642,35},{644,37},{646,39},{648,41},{650,43},{652,45},{65... | collective-permute-start | bytes 138248 | tf_op jit(solution)/shard_map/ppermute | solution.py:353
  17.3 0.0 collective-permute-done.refs_0_
  17.3 1.3 %collective-permute-start.10 = (bf16[180,128]{1,0:T(8,128)(2,1)S(1)}, bf16[180,128]{1,0:T(8,128)(2,1)S(1)}, u32[]{:S(2)}, u32[]{:S(2)}) collective-permute-start(bf16[180,128]{1,0:T(8,128)(2,1)S(1)} %get-tuple-element.72), channel_id=1, source_target_pairs={{640,1},{642,3},{644,5},{646,7},{648,9},{650,11},{652,13},{654,15}... | collective-permute-start | bytes 138248 | tf_op jit(solution)/shard_map/ppermute | solution.py:353
  18.6 0.9 %collective-permute-done.1.refs_1_ = bf16[180,128]{1,0:T(8,128)(2,1)S(1)} collective-permute-done((bf16[180,128]{1,0:T(8,128)(2,1)S(1)}, bf16[180,128]{1,0:T(8,128)(2,1)S(1)}, u32[]{:S(2)}, u32[]{:S(2)}) %collective-permute-start.1) | collective-permute-done | bytes 46112 | tf_op jit(solution)/shard_map/ppermute | solution.py:353
  19.5 1.3 %collective-permute-start.11 = (bf16[180,128]{1,0:T(8,128)(2,1)S(1)}, bf16[180,128]{1,0:T(8,128)(2,1)S(1)}, u32[]{:S(2)}, u32[]{:S(2)}) collective-permute-start(bf16[180,128]{1,0:T(8,128)(2,1)S(1)} %get-tuple-element.73), channel_id=1, source_target_pairs={{640,63},{642,33},{644,35},{646,37},{648,39},{650,41},{652,43},{65... | collective-permute-start | bytes 138248 | tf_op jit(solution)/shard_map/ppermute | solution.py:353
  20.8 0.0 collective-permute-done.2.refs_2_
  20.8 1.3 %collective-permute-start.12 = (bf16[180,128]{1,0:T(8,128)(2,1)S(1)}, bf16[180,128]{1,0:T(8,128)(2,1)S(1)}, u32[]{:S(2)}, u32[]{:S(2)}) collective-permute-start(bf16[180,128]{1,0:T(8,128)(2,1)S(1)} %get-tuple-element.74), channel_id=1, source_target_pairs={{640,31},{642,1},{644,3},{646,5},{648,7},{650,9},{652,11},{654,13}... | collective-permute-start | bytes 138248 | tf_op jit(solution)/shard_map/ppermute | solution.py:353
  22.1 6.3 %collective-permute-done.3.refs_3_ = bf16[180,128]{1,0:T(8,128)(2,1)S(1)} collective-permute-done((bf16[180,128]{1,0:T(8,128)(2,1)S(1)}, bf16[180,128]{1,0:T(8,128)(2,1)S(1)}, u32[]{:S(2)}, u32[]{:S(2)}) %collective-permute-start.3) | collective-permute-done | bytes 46112 | tf_op jit(solution)/shard_map/ppermute | solution.py:353
  28.4 3.5 %shard_map.138 = (bf16[180,128]{1,0:T(8,128)(2,1)S(1)}, bf16[180,128]{1,0:T(8,128)(2,1)S(1)}, bf16[180,128]{1,0:T(8,128)(2,1)S(1)}, bf16[180,128]{1,0:T(8,128)(2,1)S(1)}) custom-call(bf16[180,128]{1,0:T(8,128)(2,1)S(1)} %collective-permute-done.refs_0_, bf16[180,128]{1,0:T(8,128)(2,1)S(1)} %collective-permute-done.1.refs_1_, ...), custom_call_target="tpu_custom_call" | custom-call | flops 800000000 | bytes 4000000 | tf_op jit(solution)/shard_map/pallas_call | solution.py:302
  31.9 0.0 copy-start
  31.9 1.4 %collective-permute-start.4 = (bf16[180,128]{1,0:T(8,128)(2,1)S(1)}, bf16[180,128]{1,0:T(8,128)(2,1)S(1)}, u32[]{:S(2)}, u32[]{:S(2)}) collective-permute-start(bf16[180,128]{1,0:T(8,128)(2,1)S(1)} %get-tuple-element.56), channel_id=1, source_target_pairs={{673,34},{675,36},{677,38},{679,40},{681,42},{683,44},{685,46},{68... | collective-permute-start | bytes 138248 | tf_op jit(solution)/shard_map/ppermute | solution.py:353
  33.4 0.0 collective-permute-done.9.refs_0_
  33.4 1.3 %collective-permute-start.5 = (bf16[180,128]{1,0:T(8,128)(2,1)S(1)}, bf16[180,128]{1,0:T(8,128)(2,1)S(1)}, u32[]{:S(2)}, u32[]{:S(2)}) collective-permute-start(bf16[180,128]{1,0:T(8,128)(2,1)S(1)} %get-tuple-element.57), channel_id=1, source_target_pairs={{673,2},{675,4},{677,6},{679,8},{681,10},{683,12},{685,14},{687,16... | collective-permute-start | bytes 138248 | tf_op jit(solution)/shard_map/ppermute | solution.py:353
  34.7 0.0 collective-permute-done.10.refs_1_
  34.7 1.3 %collective-permute-start.6 = (bf16[180,128]{1,0:T(8,128)(2,1)S(1)}, bf16[180,128]{1,0:T(8,128)(2,1)S(1)}, u32[]{:S(2)}, u32[]{:S(2)}) collective-permute-start(bf16[180,128]{1,0:T(8,128)(2,1)S(1)} %get-tuple-element.58), channel_id=1, source_target_pairs={{673,32},{675,34},{677,36},{679,38},{681,40},{683,42},{685,44},{68... | collective-permute-start | bytes 138248 | tf_op jit(solution)/shard_map/ppermute | solution.py:353
  36.0 0.0 collective-permute-done.11.refs_2_
  36.0 1.3 %collective-permute-start.7 = (bf16[180,128]{1,0:T(8,128)(2,1)S(1)}, bf16[180,128]{1,0:T(8,128)(2,1)S(1)}, u32[]{:S(2)}, u32[]{:S(2)}) collective-permute-start(bf16[180,128]{1,0:T(8,128)(2,1)S(1)} %get-tuple-element.59), channel_id=1, source_target_pairs={{673,0},{675,2},{677,4},{679,6},{681,8},{683,10},{685,12},{687,14}... | collective-permute-start | bytes 138248 | tf_op jit(solution)/shard_map/ppermute | solution.py:353
  37.3 0.0 collective-permute-done.12.refs_3_
  37.3 3.5 %shard_map.140 = (bf16[180,128]{1,0:T(8,128)(2,1)S(1)}, bf16[180,128]{1,0:T(8,128)(2,1)S(1)}, bf16[180,128]{1,0:T(8,128)(2,1)S(1)}, bf16[180,128]{1,0:T(8,128)(2,1)S(1)}) custom-call(bf16[180,128]{1,0:T(8,128)(2,1)S(1)} %collective-permute-done.9.refs_0_, bf16[180,128]{1,0:T(8,128)(2,1)S(1)} %collective-permute-done.10.refs_1_, ...), custom_call_target="tpu_custom_call" | custom-call | flops 800000000 | bytes 4000000 | tf_op jit(solution)/shard_map/pallas_call | solution.py:302
  40.8 8.2 %collective-permute-start.13 = (bf16[180,128]{1,0:T(8,128)(2,1)S(1)}, bf16[180,128]{1,0:T(8,128)(2,1)S(1)}, u32[]{:S(2)}, u32[]{:S(2)}) collective-permute-start(bf16[180,128]{1,0:T(8,128)(2,1)S(1)} %get-tuple-element.75), channel_id=1, source_target_pairs={{33,3},{35,5},{37,7},{39,9},{41,11},{43,13},{45,15},{47,17},{49,19... | collective-permute-start | bytes 138248 | tf_op jit(solution)/shard_map/ppermute | solution.py:353
  49.0 0.0 collective-permute-done.4.refs_0_
  49.0 4.8 %collective-permute-start.14 = (bf16[180,128]{1,0:T(8,128)(2,1)S(1)}, bf16[180,128]{1,0:T(8,128)(2,1)S(1)}, u32[]{:S(2)}, u32[]{:S(2)}) collective-permute-start(bf16[180,128]{1,0:T(8,128)(2,1)S(1)} %get-tuple-element.76), channel_id=1, source_target_pairs={{33,1},{35,3},{37,5},{39,7},{41,9},{43,11},{45,13},{47,15},{49,17}... | collective-permute-start | bytes 138248 | tf_op jit(solution)/shard_map/ppermute | solution.py:353
  53.9 0.0 collective-permute-done.5.refs_1_
  53.9 1.9 %collective-permute-start.15 = (bf16[180,128]{1,0:T(8,128)(2,1)S(1)}, bf16[180,128]{1,0:T(8,128)(2,1)S(1)}, u32[]{:S(2)}, u32[]{:S(2)}) collective-permute-start(bf16[180,128]{1,0:T(8,128)(2,1)S(1)} %get-tuple-element.77), channel_id=1, source_target_pairs={{33,35},{35,37},{37,39},{39,41},{41,43},{43,45},{45,47},{47,49},{4... | collective-permute-start | bytes 138248 | tf_op jit(solution)/shard_map/ppermute | solution.py:353
  55.8 0.0 collective-permute-done.6.refs_2_
  55.8 0.0 collective-permute-done.7.refs_3_
  55.8 0.0 collective-permute-done.13.refs_4_
  55.8 0.0 collective-permute-done.14.refs_5_
  55.8 4.6 %collective-permute-done.15.refs_6_ = bf16[180,128]{1,0:T(8,128)(2,1)S(1)} collective-permute-done((bf16[180,128]{1,0:T(8,128)(2,1)S(1)}, bf16[180,128]{1,0:T(8,128)(2,1)S(1)}, u32[]{:S(2)}, u32[]{:S(2)}) %collective-permute-start.15) | collective-permute-done | bytes 46112 | tf_op jit(solution)/shard_map/ppermute | solution.py:353
  60.5 0.0 copy-done
  60.5 1.1 %shard_map.141 = bf16[1,6,12,4,320]{4,3,2,1,0:T(4,128)(2,1)} custom-call(bf16[180,128]{1,0:T(8,128)(2,1)S(1)} %collective-permute-done.4.refs_0_, bf16[180,128]{1,0:T(8,128)(2,1)S(1)} %collective-permute-done.5.refs_1_, bf16[180,128]{1,0:T(8,128)(2,1)S(1)} %collective-permute-done.6.refs_2_, bf16[180,128]{1,0:T(8,128)(2,1)S(1)} %collective-permute-done.7.refs_3_, ...), custom_call_target="tpu_custom_call" | custom-call | flops 1000000 | bytes 4000000 | tf_op jit(solution)/shard_map/pallas_call | solution.py:302
  (1 shorter events, 0.0 us)
Async XLA Ops:
  0.0 16.0 %collective-permute-start.8 = (bf16[1,6,12,4,320]{4,3,2,1,0:T(4,128)(2,1)}, bf16[1,6,12,4,320]{4,3,2,1,0:T(4,128)(2,1)S(1)}, u32[]{:S(2)}, u32[]{:S(2)}) collective-permute-start(bf16[1,6,12,4,320]{4,3,2,1,0:T(4,128)(2,1)} %bitcast.8), channel_id=1, source_target_pairs={{1,640},{3,642},{5,644},{7,646},{9,648},{11,650},{13,652},{15,654}... | collective-permute-start | bytes 552968 | tf_op jit(solution)/shard_map/ppermute | solution.py:353
  1.7 15.6 %collective-permute-start = (bf16[180,128]{1,0:T(8,128)(2,1)S(1)}, bf16[180,128]{1,0:T(8,128)(2,1)S(1)}, u32[]{:S(2)}, u32[]{:S(2)}) collective-permute-start(bf16[180,128]{1,0:T(8,128)(2,1)S(1)} %get-tuple-element.42), channel_id=1, source_target_pairs={{0,673},{2,675},{4,677},{6,679},{8,681},{10,683},{12,685},{14,687}... | collective-permute-start | bytes 138248 | tf_op jit(solution)/shard_map/ppermute | solution.py:353
  3.0 16.5 %collective-permute-start.1 = (bf16[180,128]{1,0:T(8,128)(2,1)S(1)}, bf16[180,128]{1,0:T(8,128)(2,1)S(1)}, u32[]{:S(2)}, u32[]{:S(2)}) collective-permute-start(bf16[180,128]{1,0:T(8,128)(2,1)S(1)} %get-tuple-element.43), channel_id=1, source_target_pairs={{0,641},{2,643},{4,645},{6,647},{8,649},{10,651},{12,653},{14,655}... | collective-permute-start | bytes 138248 | tf_op jit(solution)/shard_map/ppermute | solution.py:353
  4.3 16.5 %collective-permute-start.2 = (bf16[180,128]{1,0:T(8,128)(2,1)S(1)}, bf16[180,128]{1,0:T(8,128)(2,1)S(1)}, u32[]{:S(2)}, u32[]{:S(2)}) collective-permute-start(bf16[180,128]{1,0:T(8,128)(2,1)S(1)} %get-tuple-element.44), channel_id=1, source_target_pairs={{0,703},{2,673},{4,675},{6,677},{8,679},{10,681},{12,683},{14,685}... | collective-permute-start | bytes 138248 | tf_op jit(solution)/shard_map/ppermute | solution.py:353
  5.6 22.8 %collective-permute-start.3 = (bf16[180,128]{1,0:T(8,128)(2,1)S(1)}, bf16[180,128]{1,0:T(8,128)(2,1)S(1)}, u32[]{:S(2)}, u32[]{:S(2)}) collective-permute-start(bf16[180,128]{1,0:T(8,128)(2,1)S(1)} %get-tuple-element.45.refs_11_), channel_id=1, source_target_pairs={{0,671},{2,641},{4,643},{6,645},{8,647},{10,649},{12,651},{14,653}... | collective-permute-start | bytes 138248 | tf_op jit(solution)/shard_map/ppermute | solution.py:353
  16.0 17.3 %collective-permute-start.9 = (bf16[180,128]{1,0:T(8,128)(2,1)S(1)}, bf16[180,128]{1,0:T(8,128)(2,1)S(1)}, u32[]{:S(2)}, u32[]{:S(2)}) collective-permute-start(bf16[180,128]{1,0:T(8,128)(2,1)S(1)} %get-tuple-element.71), channel_id=1, source_target_pairs={{640,33},{642,35},{644,37},{646,39},{648,41},{650,43},{652,45},{65... | collective-permute-start | bytes 138248 | tf_op jit(solution)/shard_map/ppermute | solution.py:353
  17.3 17.3 %collective-permute-start.10 = (bf16[180,128]{1,0:T(8,128)(2,1)S(1)}, bf16[180,128]{1,0:T(8,128)(2,1)S(1)}, u32[]{:S(2)}, u32[]{:S(2)}) collective-permute-start(bf16[180,128]{1,0:T(8,128)(2,1)S(1)} %get-tuple-element.72), channel_id=1, source_target_pairs={{640,1},{642,3},{644,5},{646,7},{648,9},{650,11},{652,13},{654,15}... | collective-permute-start | bytes 138248 | tf_op jit(solution)/shard_map/ppermute | solution.py:353
  19.5 16.4 %collective-permute-start.11 = (bf16[180,128]{1,0:T(8,128)(2,1)S(1)}, bf16[180,128]{1,0:T(8,128)(2,1)S(1)}, u32[]{:S(2)}, u32[]{:S(2)}) collective-permute-start(bf16[180,128]{1,0:T(8,128)(2,1)S(1)} %get-tuple-element.73), channel_id=1, source_target_pairs={{640,63},{642,33},{644,35},{646,37},{648,39},{650,41},{652,43},{65... | collective-permute-start | bytes 138248 | tf_op jit(solution)/shard_map/ppermute | solution.py:353
  20.8 16.5 %collective-permute-start.12 = (bf16[180,128]{1,0:T(8,128)(2,1)S(1)}, bf16[180,128]{1,0:T(8,128)(2,1)S(1)}, u32[]{:S(2)}, u32[]{:S(2)}) collective-permute-start(bf16[180,128]{1,0:T(8,128)(2,1)S(1)} %get-tuple-element.74), channel_id=1, source_target_pairs={{640,31},{642,1},{644,3},{646,5},{648,7},{650,9},{652,11},{654,13}... | collective-permute-start | bytes 138248 | tf_op jit(solution)/shard_map/ppermute | solution.py:353
  31.9 28.5 %copy-start = (bf16[288,288]{1,0:T(8,128)(2,1)S(1)}, bf16[288,288]{1,0:T(8,128)(2,1)}, u32[]{:S(2)}) copy-start(bf16[288,288]{1,0:T(8,128)(2,1)} %constant.8.clone.refs_8_) | copy-start | bytes 497668
  31.9 17.1 %collective-permute-start.4 = (bf16[180,128]{1,0:T(8,128)(2,1)S(1)}, bf16[180,128]{1,0:T(8,128)(2,1)S(1)}, u32[]{:S(2)}, u32[]{:S(2)}) collective-permute-start(bf16[180,128]{1,0:T(8,128)(2,1)S(1)} %get-tuple-element.56), channel_id=1, source_target_pairs={{673,34},{675,36},{677,38},{679,40},{681,42},{683,44},{685,46},{68... | collective-permute-start | bytes 138248 | tf_op jit(solution)/shard_map/ppermute | solution.py:353
  33.4 20.5 %collective-permute-start.5 = (bf16[180,128]{1,0:T(8,128)(2,1)S(1)}, bf16[180,128]{1,0:T(8,128)(2,1)S(1)}, u32[]{:S(2)}, u32[]{:S(2)}) collective-permute-start(bf16[180,128]{1,0:T(8,128)(2,1)S(1)} %get-tuple-element.57), channel_id=1, source_target_pairs={{673,2},{675,4},{677,6},{679,8},{681,10},{683,12},{685,14},{687,16... | collective-permute-start | bytes 138248 | tf_op jit(solution)/shard_map/ppermute | solution.py:353
  34.7 21.1 %collective-permute-start.6 = (bf16[180,128]{1,0:T(8,128)(2,1)S(1)}, bf16[180,128]{1,0:T(8,128)(2,1)S(1)}, u32[]{:S(2)}, u32[]{:S(2)}) collective-permute-start(bf16[180,128]{1,0:T(8,128)(2,1)S(1)} %get-tuple-element.58), channel_id=1, source_target_pairs={{673,32},{675,34},{677,36},{679,38},{681,40},{683,42},{685,44},{68... | collective-permute-start | bytes 138248 | tf_op jit(solution)/shard_map/ppermute | solution.py:353
  36.0 19.8 %collective-permute-start.7 = (bf16[180,128]{1,0:T(8,128)(2,1)S(1)}, bf16[180,128]{1,0:T(8,128)(2,1)S(1)}, u32[]{:S(2)}, u32[]{:S(2)}) collective-permute-start(bf16[180,128]{1,0:T(8,128)(2,1)S(1)} %get-tuple-element.59), channel_id=1, source_target_pairs={{673,0},{675,2},{677,4},{679,6},{681,8},{683,10},{685,12},{687,14}... | collective-permute-start | bytes 138248 | tf_op jit(solution)/shard_map/ppermute | solution.py:353
  40.8 15.0 %collective-permute-start.13 = (bf16[180,128]{1,0:T(8,128)(2,1)S(1)}, bf16[180,128]{1,0:T(8,128)(2,1)S(1)}, u32[]{:S(2)}, u32[]{:S(2)}) collective-permute-start(bf16[180,128]{1,0:T(8,128)(2,1)S(1)} %get-tuple-element.75), channel_id=1, source_target_pairs={{33,3},{35,5},{37,7},{39,9},{41,11},{43,13},{45,15},{47,17},{49,19... | collective-permute-start | bytes 138248 | tf_op jit(solution)/shard_map/ppermute | solution.py:353
  49.0 6.8 %collective-permute-start.14 = (bf16[180,128]{1,0:T(8,128)(2,1)S(1)}, bf16[180,128]{1,0:T(8,128)(2,1)S(1)}, u32[]{:S(2)}, u32[]{:S(2)}) collective-permute-start(bf16[180,128]{1,0:T(8,128)(2,1)S(1)} %get-tuple-element.76), channel_id=1, source_target_pairs={{33,1},{35,3},{37,5},{39,7},{41,9},{43,11},{45,13},{47,15},{49,17}... | collective-permute-start | bytes 138248 | tf_op jit(solution)/shard_map/ppermute | solution.py:353
  53.9 6.6 %collective-permute-start.15 = (bf16[180,128]{1,0:T(8,128)(2,1)S(1)}, bf16[180,128]{1,0:T(8,128)(2,1)S(1)}, u32[]{:S(2)}, u32[]{:S(2)}) collective-permute-start(bf16[180,128]{1,0:T(8,128)(2,1)S(1)} %get-tuple-element.77), channel_id=1, source_target_pairs={{33,35},{35,37},{37,39},{39,41},{41,43},{43,45},{45,47},{47,49},{4... | collective-permute-start | bytes 138248 | tf_op jit(solution)/shard_map/ppermute | solution.py:353

commit v6 on v5

--- a/solution.py
+++ b/solution.py
@@ -61,7 +61,10 @@
 
 def lay_out_bias(table_ref, spread_ref, addend_ref, wide_ref, rows_ref):
     for head in range(HEADS):
-        wide_ref[2 * head : 2 * head + 2, :] = table_ref[0, 0, head].astype(jnp.float32)
+        both = table_ref[0, 0, head].astype(jnp.float32)
+        for window in range(2):
+            at = window * HEADS + head
+            wide_ref[at : at + 1, :] = both[window : window + 1]
     for lev in range(WLEV):
         for lat in range(WLAT):
             parts = []
@@ -136,7 +139,7 @@
             for window in range(2):
                 barred = jnp.logical_or(lat_differs, lev_differs) if window else lat_differs
                 for head in range(HEADS):
-                    at = (2 * head + window) * WIN
+                    at = (window * HEADS + head) * WIN
                     addend_ref[tile, at : at + WIN, :] = jnp.where(
                         barred, jnp.float32(-1e30), addend_ref[tile, at : at + WIN, :]
                     )
@@ -172,23 +175,29 @@
             lane_head = lax.broadcasted_iota(jnp.int32, (WIN, width), 1) // HD
             ones = jnp.ones((WIN, width), jnp.bfloat16)
             values = jnp.concatenate([values, ones], axis=1)
-            gathered = jnp.zeros((WIN, width), jnp.float32)
-            for head in range(heads):
-                own = jnp.where(lane_head == head, queries, jnp.zeros_like(queries))
-                scores = lax.dot_general(
-                    own, keys, (((1,), (1,)), ((), ())), preferred_element_type=jnp.float32
-                ) * HD ** (-0.5)
-                at = (2 * (group * 4 + head) + window) * WIN
-                scores = scores + jnp.concatenate(
-                    [addend_ref[0, at : at + WIN, :], addend_ref[1, at : at + WIN, 0 : WIN - 128]],
-                    axis=1,
-                )
-                raised = jnp.exp(scores - jnp.max(scores, axis=-1, keepdims=True))
-                mixed = jnp.dot(
-                    raised.astype(jnp.bfloat16), values, preferred_element_type=jnp.float32
-                )
-                mixed = mixed[:, :width] / mixed[:, width:]
-                gathered = jnp.where(lane_head == head, mixed, gathered)
+            own = [
+                jnp.where(lane_head == head, queries, jnp.zeros_like(queries))
+                for head in range(heads)
+            ]
+            scores = lax.dot_general(
+                jnp.concatenate(own, axis=0),
+                keys,
+                (((1,), (1,)), ((), ())),
+                preferred_element_type=jnp.float32,
+            ) * HD ** (-0.5)
+            at = (window * HEADS + group * 4) * WIN
+            rows = slice(at, at + heads * WIN)
+            scores = scores + jnp.concatenate(
+                [addend_ref[0, rows, :], addend_ref[1, rows, 0 : WIN - 128]], axis=1
+            )
+            raised = jnp.exp(scores - jnp.max(scores, axis=-1, keepdims=True))
+            mixed = jnp.dot(raised.astype(jnp.bfloat16), values, preferred_element_type=jnp.float32)
+            gathered, sums = mixed[0:WIN, :width], mixed[0:WIN, width:]
+            for head in range(1, heads):
+                part = mixed[head * WIN : (head + 1) * WIN]
+                gathered = jnp.where(lane_head == head, part[:, :width], gathered)
+                sums = jnp.where(lane_head == head, part[:, width:], sums)
+            gathered = gathered / sums
             attended_ref[first : first + WIN, lanes : lanes + width] = gathered.astype(jnp.bfloat16)
     for copy in copies[4:]:
         copy.wait()

time: 61.9 us -> 61.9 us (level)
  transfers between devices with their start and end apart: 16 -> 16, of which waited for: 4 -> 5; matrix products, arithmetic and copies ran while one was open for 0% -> 0% of each run, Pallas kernels for 19% -> 19%
where the time goes in v6:
time: 61.9 us; the launch traced here: 61.5 us
  starting transfers between devices  32.1 us (52%)
  waiting for transfers between devices  16.3 us (26%)
  Pallas kernels  12.9 us (21%)
    ppermute x16, starting transfers between devices, send(): return lax.ppermute(block, AXES, route)  32.1 us
    ppermute x16, waiting for transfers between devices, send(): return lax.ppermute(block, AXES, route)  16.3 us
    pallas_call x6, Pallas kernels, call(): pl.pallas_call(kernel, out_shape=outs, in_specs=[pl.BlockSpec(memory_spac...  12.9 us
  transfers between devices with their start and end apart: 16, of which 5 were waited for; matrix products, arithmetic and copies ran while one was open for 0% of the time, Pallas kernels for 19%

profile of v6, /device:TPU:384, one launch (start us, length us, event | category | flops | bytes accessed | tf_op | source)
XLA Modules:
  0.0 61.5 jit_solution(7737454324223287539)
XLA Ops:
  0.0 1.6 %collective-permute-start.8 = (bf16[1,6,12,4,320]{4,3,2,1,0:T(4,128)(2,1)}, bf16[1,6,12,4,320]{4,3,2,1,0:T(4,128)(2,1)S(1)}, u32[]{:S(2)}, u32[]{:S(2)}) collective-permute-start(bf16[1,6,12,4,320]{4,3,2,1,0:T(4,128)(2,1)} %bitcast.8), channel_id=1, source_target_pairs={{1,640},{3,642},{5,644},{7,646},{9,648},{11,650},{13,652},{15,654}... | collective-permute-start | bytes 552968 | tf_op jit(solution)/shard_map/ppermute | solution.py:362
  1.6 0.1 shard_map.136
  1.7 1.3 %collective-permute-start = (bf16[180,128]{1,0:T(8,128)(2,1)S(1)}, bf16[180,128]{1,0:T(8,128)(2,1)S(1)}, u32[]{:S(2)}, u32[]{:S(2)}) collective-permute-start(bf16[180,128]{1,0:T(8,128)(2,1)S(1)} %get-tuple-element.42), channel_id=1, source_target_pairs={{0,673},{2,675},{4,677},{6,679},{8,681},{10,683},{12,685},{14,687}... | collective-permute-start | bytes 138248 | tf_op jit(solution)/shard_map/ppermute | solution.py:362
  3.0 1.3 %collective-permute-start.1 = (bf16[180,128]{1,0:T(8,128)(2,1)S(1)}, bf16[180,128]{1,0:T(8,128)(2,1)S(1)}, u32[]{:S(2)}, u32[]{:S(2)}) collective-permute-start(bf16[180,128]{1,0:T(8,128)(2,1)S(1)} %get-tuple-element.43), channel_id=1, source_target_pairs={{0,641},{2,643},{4,645},{6,647},{8,649},{10,651},{12,653},{14,655}... | collective-permute-start | bytes 138248 | tf_op jit(solution)/shard_map/ppermute | solution.py:362
  4.3 1.3 %collective-permute-start.2 = (bf16[180,128]{1,0:T(8,128)(2,1)S(1)}, bf16[180,128]{1,0:T(8,128)(2,1)S(1)}, u32[]{:S(2)}, u32[]{:S(2)}) collective-permute-start(bf16[180,128]{1,0:T(8,128)(2,1)S(1)} %get-tuple-element.44), channel_id=1, source_target_pairs={{0,703},{2,673},{4,675},{6,677},{8,679},{10,681},{12,683},{14,685}... | collective-permute-start | bytes 138248 | tf_op jit(solution)/shard_map/ppermute | solution.py:362
  5.6 1.3 %collective-permute-start.3 = (bf16[180,128]{1,0:T(8,128)(2,1)S(1)}, bf16[180,128]{1,0:T(8,128)(2,1)S(1)}, u32[]{:S(2)}, u32[]{:S(2)}) collective-permute-start(bf16[180,128]{1,0:T(8,128)(2,1)S(1)} %get-tuple-element.45.refs_11_), channel_id=1, source_target_pairs={{0,671},{2,641},{4,643},{6,645},{8,647},{10,649},{12,651},{14,653}... | collective-permute-start | bytes 138248 | tf_op jit(solution)/shard_map/ppermute | solution.py:362
  6.9 4.7 %shard_map.137 = (f32[2,2880,128]{2,1,0:T(8,128)S(1)}, bf16[1,2,320]{2,1,0:T(2,128)(2,1)S(1)}, bf16[1,2,320]{2,1,0:T(2,128)(2,1)S(1)}, bf16[1,320,960]{2,1,0:T(8...) custom-call(bf16[1,1,10,2,3312]{4,3,2,1,0:T(2,128)(2,1)} %bitcast.7,, ...), custom_call_target="tpu_custom_call" | custom-call | flops 200000000 | bytes 4000000 | tf_op jit(solution)/shard_map/pallas_call | solution.py:311
  11.6 4.4 %collective-permute-done.8.refs_0_ = bf16[1,6,12,4,320]{4,3,2,1,0:T(4,128)(2,1)S(1)} collective-permute-done((bf16[1,6,12,4,320]{4,3,2,1,0:T(4,128)(2,1)}, bf16[1,6,12,4,320]{4,3,2,1,0:T(4,128)(2,1)S(1)}, u32[]{:S(2)}, u32[]{:S(2)}) %collective-permute-start.8) | collective-permute-done | bytes 184352 | tf_op jit(solution)/shard_map/ppermute | solution.py:362
  16.0 1.3 %collective-permute-start.9 = (bf16[180,128]{1,0:T(8,128)(2,1)S(1)}, bf16[180,128]{1,0:T(8,128)(2,1)S(1)}, u32[]{:S(2)}, u32[]{:S(2)}) collective-permute-start(bf16[180,128]{1,0:T(8,128)(2,1)S(1)} %get-tuple-element.71), channel_id=1, source_target_pairs={{640,33},{642,35},{644,37},{646,39},{648,41},{650,43},{652,45},{65... | collective-permute-start | bytes 138248 | tf_op jit(solution)/shard_map/ppermute | solution.py:362
  17.3 0.1 collective-permute-done.refs_0_
  17.5 1.3 %collective-permute-start.10 = (bf16[180,128]{1,0:T(8,128)(2,1)S(1)}, bf16[180,128]{1,0:T(8,128)(2,1)S(1)}, u32[]{:S(2)}, u32[]{:S(2)}) collective-permute-start(bf16[180,128]{1,0:T(8,128)(2,1)S(1)} %get-tuple-element.72), channel_id=1, source_target_pairs={{640,1},{642,3},{644,5},{646,7},{648,9},{650,11},{652,13},{654,15}... | collective-permute-start | bytes 138248 | tf_op jit(solution)/shard_map/ppermute | solution.py:362
  18.7 0.8 %collective-permute-done.1.refs_1_ = bf16[180,128]{1,0:T(8,128)(2,1)S(1)} collective-permute-done((bf16[180,128]{1,0:T(8,128)(2,1)S(1)}, bf16[180,128]{1,0:T(8,128)(2,1)S(1)}, u32[]{:S(2)}, u32[]{:S(2)}) %collective-permute-start.1) | collective-permute-done | bytes 46112 | tf_op jit(solution)/shard_map/ppermute | solution.py:362
  19.5 1.3 %collective-permute-start.11 = (bf16[180,128]{1,0:T(8,128)(2,1)S(1)}, bf16[180,128]{1,0:T(8,128)(2,1)S(1)}, u32[]{:S(2)}, u32[]{:S(2)}) collective-permute-start(bf16[180,128]{1,0:T(8,128)(2,1)S(1)} %get-tuple-element.73), channel_id=1, source_target_pairs={{640,63},{642,33},{644,35},{646,37},{648,39},{650,41},{652,43},{65... | collective-permute-start | bytes 138248 | tf_op jit(solution)/shard_map/ppermute | solution.py:362
  20.8 0.0 collective-permute-done.2.refs_2_
  20.8 1.3 %collective-permute-start.12 = (bf16[180,128]{1,0:T(8,128)(2,1)S(1)}, bf16[180,128]{1,0:T(8,128)(2,1)S(1)}, u32[]{:S(2)}, u32[]{:S(2)}) collective-permute-start(bf16[180,128]{1,0:T(8,128)(2,1)S(1)} %get-tuple-element.74), channel_id=1, source_target_pairs={{640,31},{642,1},{644,3},{646,5},{648,7},{650,9},{652,11},{654,13}... | collective-permute-start | bytes 138248 | tf_op jit(solution)/shard_map/ppermute | solution.py:362
  22.1 6.3 %collective-permute-done.3.refs_3_ = bf16[180,128]{1,0:T(8,128)(2,1)S(1)} collective-permute-done((bf16[180,128]{1,0:T(8,128)(2,1)S(1)}, bf16[180,128]{1,0:T(8,128)(2,1)S(1)}, u32[]{:S(2)}, u32[]{:S(2)}) %collective-permute-start.3) | collective-permute-done | bytes 46112 | tf_op jit(solution)/shard_map/ppermute | solution.py:362
  28.5 3.5 %shard_map.138 = (bf16[180,128]{1,0:T(8,128)(2,1)S(1)}, bf16[180,128]{1,0:T(8,128)(2,1)S(1)}, bf16[180,128]{1,0:T(8,128)(2,1)S(1)}, bf16[180,128]{1,0:T(8,128)(2,1)S(1)}) custom-call(bf16[180,128]{1,0:T(8,128)(2,1)S(1)} %collective-permute-done.refs_0_, bf16[180,128]{1,0:T(8,128)(2,1)S(1)} %collective-permute-done.1.refs_1_, ...), custom_call_target="tpu_custom_call" | custom-call | flops 800000000 | bytes 4000000 | tf_op jit(solution)/shard_map/pallas_call | solution.py:311
  31.9 0.0 copy-start
  31.9 1.4 %collective-permute-start.4 = (bf16[180,128]{1,0:T(8,128)(2,1)S(1)}, bf16[180,128]{1,0:T(8,128)(2,1)S(1)}, u32[]{:S(2)}, u32[]{:S(2)}) collective-permute-start(bf16[180,128]{1,0:T(8,128)(2,1)S(1)} %get-tuple-element.56), channel_id=1, source_target_pairs={{673,34},{675,36},{677,38},{679,40},{681,42},{683,44},{685,46},{68... | collective-permute-start | bytes 138248 | tf_op jit(solution)/shard_map/ppermute | solution.py:362
  33.4 0.0 collective-permute-done.9.refs_0_
  33.4 1.3 %collective-permute-start.5 = (bf16[180,128]{1,0:T(8,128)(2,1)S(1)}, bf16[180,128]{1,0:T(8,128)(2,1)S(1)}, u32[]{:S(2)}, u32[]{:S(2)}) collective-permute-start(bf16[180,128]{1,0:T(8,128)(2,1)S(1)} %get-tuple-element.57), channel_id=1, source_target_pairs={{673,2},{675,4},{677,6},{679,8},{681,10},{683,12},{685,14},{687,16... | collective-permute-start | bytes 138248 | tf_op jit(solution)/shard_map/ppermute | solution.py:362
  34.7 0.0 collective-permute-done.10.refs_1_
  34.7 1.3 %collective-permute-start.6 = (bf16[180,128]{1,0:T(8,128)(2,1)S(1)}, bf16[180,128]{1,0:T(8,128)(2,1)S(1)}, u32[]{:S(2)}, u32[]{:S(2)}) collective-permute-start(bf16[180,128]{1,0:T(8,128)(2,1)S(1)} %get-tuple-element.58), channel_id=1, source_target_pairs={{673,32},{675,34},{677,36},{679,38},{681,40},{683,42},{685,44},{68... | collective-permute-start | bytes 138248 | tf_op jit(solution)/shard_map/ppermute | solution.py:362
  36.0 0.0 collective-permute-done.11.refs_2_
  36.0 1.3 %collective-permute-start.7 = (bf16[180,128]{1,0:T(8,128)(2,1)S(1)}, bf16[180,128]{1,0:T(8,128)(2,1)S(1)}, u32[]{:S(2)}, u32[]{:S(2)}) collective-permute-start(bf16[180,128]{1,0:T(8,128)(2,1)S(1)} %get-tuple-element.59), channel_id=1, source_target_pairs={{673,0},{675,2},{677,4},{679,6},{681,8},{683,10},{685,12},{687,14}... | collective-permute-start | bytes 138248 | tf_op jit(solution)/shard_map/ppermute | solution.py:362
  37.3 0.0 collective-permute-done.12.refs_3_
  37.3 3.5 %shard_map.140 = (bf16[180,128]{1,0:T(8,128)(2,1)S(1)}, bf16[180,128]{1,0:T(8,128)(2,1)S(1)}, bf16[180,128]{1,0:T(8,128)(2,1)S(1)}, bf16[180,128]{1,0:T(8,128)(2,1)S(1)}) custom-call(bf16[180,128]{1,0:T(8,128)(2,1)S(1)} %collective-permute-done.9.refs_0_, bf16[180,128]{1,0:T(8,128)(2,1)S(1)} %collective-permute-done.10.refs_1_, ...), custom_call_target="tpu_custom_call" | custom-call | flops 800000000 | bytes 4000000 | tf_op jit(solution)/shard_map/pallas_call | solution.py:311
  40.8 8.2 %collective-permute-start.13 = (bf16[180,128]{1,0:T(8,128)(2,1)S(1)}, bf16[180,128]{1,0:T(8,128)(2,1)S(1)}, u32[]{:S(2)}, u32[]{:S(2)}) collective-permute-start(bf16[180,128]{1,0:T(8,128)(2,1)S(1)} %get-tuple-element.75), channel_id=1, source_target_pairs={{33,3},{35,5},{37,7},{39,9},{41,11},{43,13},{45,15},{47,17},{49,19... | collective-permute-start | bytes 138248 | tf_op jit(solution)/shard_map/ppermute | solution.py:362
  49.0 0.0 collective-permute-done.4.refs_0_
  49.0 4.8 %collective-permute-start.14 = (bf16[180,128]{1,0:T(8,128)(2,1)S(1)}, bf16[180,128]{1,0:T(8,128)(2,1)S(1)}, u32[]{:S(2)}, u32[]{:S(2)}) collective-permute-start(bf16[180,128]{1,0:T(8,128)(2,1)S(1)} %get-tuple-element.76), channel_id=1, source_target_pairs={{33,1},{35,3},{37,5},{39,7},{41,9},{43,11},{45,13},{47,15},{49,17}... | collective-permute-start | bytes 138248 | tf_op jit(solution)/shard_map/ppermute | solution.py:362
  53.9 0.0 collective-permute-done.5.refs_1_
  53.9 1.9 %collective-permute-start.15 = (bf16[180,128]{1,0:T(8,128)(2,1)S(1)}, bf16[180,128]{1,0:T(8,128)(2,1)S(1)}, u32[]{:S(2)}, u32[]{:S(2)}) collective-permute-start(bf16[180,128]{1,0:T(8,128)(2,1)S(1)} %get-tuple-element.77), channel_id=1, source_target_pairs={{33,35},{35,37},{37,39},{39,41},{41,43},{43,45},{45,47},{47,49},{4... | collective-permute-start | bytes 138248 | tf_op jit(solution)/shard_map/ppermute | solution.py:362
  55.8 0.0 collective-permute-done.6.refs_2_
  55.8 0.0 collective-permute-done.7.refs_3_
  55.8 0.0 collective-permute-done.13.refs_4_
  55.8 0.0 collective-permute-done.14.refs_5_
  55.8 4.6 %collective-permute-done.15.refs_6_ = bf16[180,128]{1,0:T(8,128)(2,1)S(1)} collective-permute-done((bf16[180,128]{1,0:T(8,128)(2,1)S(1)}, bf16[180,128]{1,0:T(8,128)(2,1)S(1)}, u32[]{:S(2)}, u32[]{:S(2)}) %collective-permute-start.15) | collective-permute-done | bytes 46112 | tf_op jit(solution)/shard_map/ppermute | solution.py:362
  60.5 0.0 copy-done
  60.5 1.1 %shard_map.141 = bf16[1,6,12,4,320]{4,3,2,1,0:T(4,128)(2,1)} custom-call(bf16[180,128]{1,0:T(8,128)(2,1)S(1)} %collective-permute-done.4.refs_0_, bf16[180,128]{1,0:T(8,128)(2,1)S(1)} %collective-permute-done.5.refs_1_, bf16[180,128]{1,0:T(8,128)(2,1)S(1)} %collective-permute-done.6.refs_2_, bf16[180,128]{1,0:T(8,128)(2,1)S(1)} %collective-permute-done.7.refs_3_, ...), custom_call_target="tpu_custom_call" | custom-call | flops 1000000 | bytes 4000000 | tf_op jit(solution)/shard_map/pallas_call | solution.py:311
  (1 shorter events, 0.0 us)
Async XLA Ops:
  0.0 16.0 %collective-permute-start.8 = (bf16[1,6,12,4,320]{4,3,2,1,0:T(4,128)(2,1)}, bf16[1,6,12,4,320]{4,3,2,1,0:T(4,128)(2,1)S(1)}, u32[]{:S(2)}, u32[]{:S(2)}) collective-permute-start(bf16[1,6,12,4,320]{4,3,2,1,0:T(4,128)(2,1)} %bitcast.8), channel_id=1, source_target_pairs={{1,640},{3,642},{5,644},{7,646},{9,648},{11,650},{13,652},{15,654}... | collective-permute-start | bytes 552968 | tf_op jit(solution)/shard_map/ppermute | solution.py:362
  1.7 15.7 %collective-permute-start = (bf16[180,128]{1,0:T(8,128)(2,1)S(1)}, bf16[180,128]{1,0:T(8,128)(2,1)S(1)}, u32[]{:S(2)}, u32[]{:S(2)}) collective-permute-start(bf16[180,128]{1,0:T(8,128)(2,1)S(1)} %get-tuple-element.42), channel_id=1, source_target_pairs={{0,673},{2,675},{4,677},{6,679},{8,681},{10,683},{12,685},{14,687}... | collective-permute-start | bytes 138248 | tf_op jit(solution)/shard_map/ppermute | solution.py:362
  3.0 16.5 %collective-permute-start.1 = (bf16[180,128]{1,0:T(8,128)(2,1)S(1)}, bf16[180,128]{1,0:T(8,128)(2,1)S(1)}, u32[]{:S(2)}, u32[]{:S(2)}) collective-permute-start(bf16[180,128]{1,0:T(8,128)(2,1)S(1)} %get-tuple-element.43), channel_id=1, source_target_pairs={{0,641},{2,643},{4,645},{6,647},{8,649},{10,651},{12,653},{14,655}... | collective-permute-start | bytes 138248 | tf_op jit(solution)/shard_map/ppermute | solution.py:362
  4.3 16.5 %collective-permute-start.2 = (bf16[180,128]{1,0:T(8,128)(2,1)S(1)}, bf16[180,128]{1,0:T(8,128)(2,1)S(1)}, u32[]{:S(2)}, u32[]{:S(2)}) collective-permute-start(bf16[180,128]{1,0:T(8,128)(2,1)S(1)} %get-tuple-element.44), channel_id=1, source_target_pairs={{0,703},{2,673},{4,675},{6,677},{8,679},{10,681},{12,683},{14,685}... | collective-permute-start | bytes 138248 | tf_op jit(solution)/shard_map/ppermute | solution.py:362
  5.6 22.8 %collective-permute-start.3 = (bf16[180,128]{1,0:T(8,128)(2,1)S(1)}, bf16[180,128]{1,0:T(8,128)(2,1)S(1)}, u32[]{:S(2)}, u32[]{:S(2)}) collective-permute-start(bf16[180,128]{1,0:T(8,128)(2,1)S(1)} %get-tuple-element.45.refs_11_), channel_id=1, source_target_pairs={{0,671},{2,641},{4,643},{6,645},{8,647},{10,649},{12,651},{14,653}... | collective-permute-start | bytes 138248 | tf_op jit(solution)/shard_map/ppermute | solution.py:362
  16.0 17.3 %collective-permute-start.9 = (bf16[180,128]{1,0:T(8,128)(2,1)S(1)}, bf16[180,128]{1,0:T(8,128)(2,1)S(1)}, u32[]{:S(2)}, u32[]{:S(2)}) collective-permute-start(bf16[180,128]{1,0:T(8,128)(2,1)S(1)} %get-tuple-element.71), channel_id=1, source_target_pairs={{640,33},{642,35},{644,37},{646,39},{648,41},{650,43},{652,45},{65... | collective-permute-start | bytes 138248 | tf_op jit(solution)/shard_map/ppermute | solution.py:362
  17.5 17.2 %collective-permute-start.10 = (bf16[180,128]{1,0:T(8,128)(2,1)S(1)}, bf16[180,128]{1,0:T(8,128)(2,1)S(1)}, u32[]{:S(2)}, u32[]{:S(2)}) collective-permute-start(bf16[180,128]{1,0:T(8,128)(2,1)S(1)} %get-tuple-element.72), channel_id=1, source_target_pairs={{640,1},{642,3},{644,5},{646,7},{648,9},{650,11},{652,13},{654,15}... | collective-permute-start | bytes 138248 | tf_op jit(solution)/shard_map/ppermute | solution.py:362
  19.5 16.5 %collective-permute-start.11 = (bf16[180,128]{1,0:T(8,128)(2,1)S(1)}, bf16[180,128]{1,0:T(8,128)(2,1)S(1)}, u32[]{:S(2)}, u32[]{:S(2)}) collective-permute-start(bf16[180,128]{1,0:T(8,128)(2,1)S(1)} %get-tuple-element.73), channel_id=1, source_target_pairs={{640,63},{642,33},{644,35},{646,37},{648,39},{650,41},{652,43},{65... | collective-permute-start | bytes 138248 | tf_op jit(solution)/shard_map/ppermute | solution.py:362
  20.8 16.5 %collective-permute-start.12 = (bf16[180,128]{1,0:T(8,128)(2,1)S(1)}, bf16[180,128]{1,0:T(8,128)(2,1)S(1)}, u32[]{:S(2)}, u32[]{:S(2)}) collective-permute-start(bf16[180,128]{1,0:T(8,128)(2,1)S(1)} %get-tuple-element.74), channel_id=1, source_target_pairs={{640,31},{642,1},{644,3},{646,5},{648,7},{650,9},{652,11},{654,13}... | collective-permute-start | bytes 138248 | tf_op jit(solution)/shard_map/ppermute | solution.py:362
  31.9 28.5 %copy-start = (bf16[288,288]{1,0:T(8,128)(2,1)S(1)}, bf16[288,288]{1,0:T(8,128)(2,1)}, u32[]{:S(2)}) copy-start(bf16[288,288]{1,0:T(8,128)(2,1)} %constant.8.clone.refs_8_) | copy-start | bytes 497668
  31.9 17.1 %collective-permute-start.4 = (bf16[180,128]{1,0:T(8,128)(2,1)S(1)}, bf16[180,128]{1,0:T(8,128)(2,1)S(1)}, u32[]{:S(2)}, u32[]{:S(2)}) collective-permute-start(bf16[180,128]{1,0:T(8,128)(2,1)S(1)} %get-tuple-element.56), channel_id=1, source_target_pairs={{673,34},{675,36},{677,38},{679,40},{681,42},{683,44},{685,46},{68... | collective-permute-start | bytes 138248 | tf_op jit(solution)/shard_map/ppermute | solution.py:362
  33.4 20.5 %collective-permute-start.5 = (bf16[180,128]{1,0:T(8,128)(2,1)S(1)}, bf16[180,128]{1,0:T(8,128)(2,1)S(1)}, u32[]{:S(2)}, u32[]{:S(2)}) collective-permute-start(bf16[180,128]{1,0:T(8,128)(2,1)S(1)} %get-tuple-element.57), channel_id=1, source_target_pairs={{673,2},{675,4},{677,6},{679,8},{681,10},{683,12},{685,14},{687,16... | collective-permute-start | bytes 138248 | tf_op jit(solution)/shard_map/ppermute | solution.py:362
  34.7 21.1 %collective-permute-start.6 = (bf16[180,128]{1,0:T(8,128)(2,1)S(1)}, bf16[180,128]{1,0:T(8,128)(2,1)S(1)}, u32[]{:S(2)}, u32[]{:S(2)}) collective-permute-start(bf16[180,128]{1,0:T(8,128)(2,1)S(1)} %get-tuple-element.58), channel_id=1, source_target_pairs={{673,32},{675,34},{677,36},{679,38},{681,40},{683,42},{685,44},{68... | collective-permute-start | bytes 138248 | tf_op jit(solution)/shard_map/ppermute | solution.py:362
  36.0 19.8 %collective-permute-start.7 = (bf16[180,128]{1,0:T(8,128)(2,1)S(1)}, bf16[180,128]{1,0:T(8,128)(2,1)S(1)}, u32[]{:S(2)}, u32[]{:S(2)}) collective-permute-start(bf16[180,128]{1,0:T(8,128)(2,1)S(1)} %get-tuple-element.59), channel_id=1, source_target_pairs={{673,0},{675,2},{677,4},{679,6},{681,8},{683,10},{685,12},{687,14}... | collective-permute-start | bytes 138248 | tf_op jit(solution)/shard_map/ppermute | solution.py:362
  40.8 15.0 %collective-permute-start.13 = (bf16[180,128]{1,0:T(8,128)(2,1)S(1)}, bf16[180,128]{1,0:T(8,128)(2,1)S(1)}, u32[]{:S(2)}, u32[]{:S(2)}) collective-permute-start(bf16[180,128]{1,0:T(8,128)(2,1)S(1)} %get-tuple-element.75), channel_id=1, source_target_pairs={{33,3},{35,5},{37,7},{39,9},{41,11},{43,13},{45,15},{47,17},{49,19... | collective-permute-start | bytes 138248 | tf_op jit(solution)/shard_map/ppermute | solution.py:362
  49.0 6.8 %collective-permute-start.14 = (bf16[180,128]{1,0:T(8,128)(2,1)S(1)}, bf16[180,128]{1,0:T(8,128)(2,1)S(1)}, u32[]{:S(2)}, u32[]{:S(2)}) collective-permute-start(bf16[180,128]{1,0:T(8,128)(2,1)S(1)} %get-tuple-element.76), channel_id=1, source_target_pairs={{33,1},{35,3},{37,5},{39,7},{41,9},{43,11},{45,13},{47,15},{49,17}... | collective-permute-start | bytes 138248 | tf_op jit(solution)/shard_map/ppermute | solution.py:362
  53.9 6.6 %collective-permute-start.15 = (bf16[180,128]{1,0:T(8,128)(2,1)S(1)}, bf16[180,128]{1,0:T(8,128)(2,1)S(1)}, u32[]{:S(2)}, u32[]{:S(2)}) collective-permute-start(bf16[180,128]{1,0:T(8,128)(2,1)S(1)} %get-tuple-element.77), channel_id=1, source_target_pairs={{33,35},{35,37},{37,39},{39,41},{41,43},{43,45},{45,47},{47,49},{4... | collective-permute-start | bytes 138248 | tf_op jit(solution)/shard_map/ppermute | solution.py:362
